TPU v7x, 32 devices: a whole 2x2x4 slice. The times are simulated.
32 devices in a mesh: slab: 2 (over x), col: 16 (over z, y, core).
Axes of the slice: x: 2, y: 2, z: 4, core: 2. Of those that a mesh axis runs over, the one named last changes fastest.
Arguments:
- tiles: bfloat16 [192, 12, 128, 128], P(('slab', 'col')), parts along dimension 0, may hold values from -6 to 6
- tile_cols: int32 [192, 12], P(('slab', 'col')), parts along dimension 0, may hold values from 0 to 23, as said below
- tile_count: int32 [192], P(('slab', 'col')), parts along dimension 0, may hold values from 8 to 12
- candidates: int32 [192, 12], P(('slab', 'col')), parts along dimension 0, may hold values from 0 to 95, as said below
- degree: int32 [192, 128], P(('slab', 'col')), parts along dimension 0, may hold values from 8 to 64
Outputs:
- snn_weights: bfloat16 [192, 12, 128, 128], P(('slab', 'col')), parts along dimension 0
There are 2 independent parts, one for each index of `slab`. A program takes and returns all parts, laid end to end along the dimension named above; each array names one. Nothing has to cross between parts.
Inputs may be any that keep to these rules, and one draw needn't show every extreme that they name: `tile_cols`: the 12 column blocks of a block row are distinct. The 12 candidates of a block row are distinct; the candidates of the 6 block rows of one device, taken together, name exactly one block row of each aligned range of 6 block rows.
All inputs are finite; a program needn't handle non-finite values.
Results may differ from a plain program's by a relative error of at most 0.001.
Values may be sent and summed in bfloat16 or wider, within the bound.
No kernel may reach another device: no remote copies, remote signals or barrier semaphores. Data moves between devices by JAX's collectives and lax.ppermute only.
A program may use at most 128 MiB of HBM per device.

v0:
```python
import jax
import jax.numpy as jnp
from jax import lax
from jax.sharding import PartitionSpec as P


def pick_small(selector, table):
    extra = table.ndim - 1
    shaped = selector.reshape(selector.shape + (1,) * extra)
    return jnp.sum(jnp.where(shaped, table[None], 0), axis=1).astype(jnp.int32)


def local(tiles, tile_cols, tile_count, candidates, degree):
    local_rows = tiles.shape[0]
    peer_count = lax.axis_size("col")
    slot_total = tile_cols.shape[1]
    side = tiles.shape[2]
    owners = candidates // local_rows
    device_ids = jnp.arange(peer_count, dtype=jnp.int32)
    row_ids = jnp.arange(local_rows, dtype=jnp.int32)
    matches = owners[:, :, None] == device_ids[None, None, :]
    wanted = jnp.max(jnp.where(matches, (candidates % local_rows)[:, :, None], 0), axis=(0, 1))
    asked_rows = lax.all_to_all(
        wanted.reshape(peer_count, 1), "col", split_axis=0, concat_axis=0, tiled=True
    ).reshape(peer_count)
    ask_select = asked_rows[:, None] == row_ids[None, :]
    ask_onehot = ask_select.astype(jnp.bfloat16)
    send_tiles = jnp.dot(
        ask_onehot, tiles.reshape(local_rows, -1), preferred_element_type=jnp.float32
    )
    send_tiles = send_tiles.astype(jnp.bfloat16).reshape((peer_count,) + tiles.shape[1:])
    send_cols = pick_small(ask_select, tile_cols)
    send_total = pick_small(ask_select, tile_count)
    send_degree = pick_small(ask_select, degree)
    fetched_tiles, fetched_cols, fetched_total, fetched_degree = (
        lax.all_to_all(send_tiles, "col", split_axis=0, concat_axis=0, tiled=True),
        lax.all_to_all(send_cols, "col", split_axis=0, concat_axis=0, tiled=True),
        lax.all_to_all(send_total, "col", split_axis=0, concat_axis=0, tiled=True),
        lax.all_to_all(send_degree, "col", split_axis=0, concat_axis=0, tiled=True),
    )
    fetched_flat = fetched_tiles.reshape(peer_count, -1)
    slot_ids = jnp.arange(slot_total, dtype=jnp.int32)

    def row_output(inputs):
        row_tiles, row_cols, row_total, row_owners, row_degree = inputs
        owner_select = row_owners[:, None] == device_ids[None, :]
        owner_onehot = owner_select.astype(jnp.bfloat16)
        other_tiles = jnp.dot(owner_onehot, fetched_flat, preferred_element_type=jnp.float32)
        other_tiles = other_tiles.astype(jnp.bfloat16).reshape(
            row_owners.shape[0], slot_total, side, side
        )
        other_cols = pick_small(owner_select, fetched_cols)
        other_total = pick_small(owner_select, fetched_total)
        other_degree = pick_small(owner_select, fetched_degree)
        live_row = slot_ids < row_total
        live_other = slot_ids[None, :] < other_total[:, None]
        matches = (
            (row_cols[None, :, None] == other_cols[:, None, :])
            & live_row[None, :, None]
            & live_other[:, None, :]
        )
        match_mask = matches.astype(jnp.bfloat16)
        row_matched = jnp.einsum(
            "qrs,rxk->qsxk", match_mask, row_tiles, preferred_element_type=jnp.float32
        )
        row_matched = row_matched.astype(jnp.bfloat16)
        shared = jnp.einsum(
            "qsxk,qsyk->qxy", row_matched, other_tiles, preferred_element_type=jnp.float32
        )
        product = (
            row_degree.astype(jnp.float32)[None, :, None]
            * other_degree.astype(jnp.float32)[:, None, :]
        )
        return (shared / jnp.sqrt(product)).astype(jnp.bfloat16)

    return lax.map(row_output, (tiles, tile_cols, tile_count, owners, degree))


def solution(mesh):
    in_specs = (
        P(("slab", "col"), None, None, None),
        P(("slab", "col"), None),
        P(("slab", "col")),
        P(("slab", "col"), None),
        P(("slab", "col"), None),
    )
    out_specs = P(("slab", "col"), None, None, None)
    return jax.shard_map(local, mesh=mesh, in_specs=in_specs, out_specs=out_specs, check_vma=False)
```

profile of v0, /device:TPU:0, one launch (start us, length us, event | category | flops | bytes accessed | tf_op | source)
XLA Modules:
  0.0 282.4 jit_solution(1544737795490558427)
XLA Ops:
  0.0 0.7 add_select_fusion
  1.5 7.4 %all-to-all-start = ((s32[16,1,1]{2,1,0:T(1,128)}), s32[16,1,1]{2,1,0:T(1,128)S(1)}, u32[]{:S(2)}, u32[]{:S(2)}) async-start(s32[16,1,1]{2,1,0:T(1,128)} %copy.13), calls=%async_computation | async-start | bytes 16384 | tf_op jit(solution)/shard_map/all_to_all | solution.py:23
  8.9 6.3 %all-to-all-done = s32[16,1,1]{2,1,0:T(1,128)S(1)} async-done(((s32[16,1,1]{2,1,0:T(1,128)}), s32[16,1,1]{2,1,0:T(1,128)S(1)}, u32[]{:S(2)}, u32[]{:S(2)}) %all-to-all-start) | async-done | bytes 96 | tf_op jit(solution)/shard_map/all_to_all | solution.py:23
  15.6 0.7 select_reduce_fusion.6
  17.0 3.5 %all-to-all-start.2 = ((s32[16,1,1]{2,1,0:T(1,128)}), s32[16,1,1]{2,1,0:T(1,128)S(1)}, u32[]{:S(2)}, u32[]{:S(2)}) async-start(s32[16,1,1]{2,1,0:T(1,128)} %copy.15), calls=%async_computation.2 | async-start | bytes 16384 | tf_op jit(solution)/shard_map/all_to_all | solution.py:38
  20.5 1.4 select_reduce_fusion.4
  21.9 5.0 %all-to-all-done.2 = s32[16,1,1]{2,1,0:T(1,128)S(1)} async-done(((s32[16,1,1]{2,1,0:T(1,128)}), s32[16,1,1]{2,1,0:T(1,128)S(1)}, u32[]{:S(2)}, u32[]{:S(2)}) %all-to-all-start.2) | async-done | bytes 96 | tf_op jit(solution)/shard_map/all_to_all | solution.py:38
  26.9 3.5 %all-to-all-start.1 = ((s32[16,1,12]{2,1,0:T(1,128)}), s32[16,1,12]{2,1,0:T(1,128)S(1)}, u32[]{:S(2)}, u32[]{:S(2)}) async-start(s32[16,1,12]{2,1,0:T(1,128)} %bitcast.2), calls=%async_computation.1 | async-start | bytes 16384 | tf_op jit(solution)/shard_map/all_to_all | solution.py:37
  30.4 9.0 %fusion.36 = bf16[2,8,1536,128]{3,1,2,0:T(8,128)(2,1)S(1)} fusion(bf16[1,6,1536,128]{3,2,1,0:T(8,128)(2,1)} %bitcast.92, s32[16]{0:T(128)S(1)} %reduce), kind=kOutput, calls=%fused_computation.39 | convolution fusion | flops 40894560 | bytes 8650816 | tf_op jit(solution)/shard_map/dot_general | solution.py:28
  39.3 3.8 %copy.23 = bf16[2,8,1536,128]{3,2,1,0:T(8,128)(2,1)} copy(bf16[2,8,1536,128]{3,1,2,0:T(8,128)(2,1)S(1)} %fusion.36) | data formatting | bytes 12582912
  43.2 6.1 %all-to-all-start.3 = ((bf16[16,12,128,128]{3,2,1,0:T(8,128)(2,1)}), bf16[16,12,128,128]{3,2,1,0:T(8,128)(2,1)}, u32[]{:S(2)}, u32[]{:S(2)}) async-start(bf16[16,12,128,128]{3,2,1,0:T(8,128)(2,1)} %bitcast.91), calls=%async_computation.3 | async-start | bytes 12582912 | tf_op jit(solution)/shard_map/all_to_all | solution.py:36
  50.0 113.5 %all-to-all-done.3 = bf16[16,12,128,128]{3,2,1,0:T(8,128)(2,1)} async-done(((bf16[16,12,128,128]{3,2,1,0:T(8,128)(2,1)}), bf16[16,12,128,128]{3,2,1,0:T(8,128)(2,1)}, u32[]{:S(2)}, u32[]{:S(2)}) %all-to-all-start.3) | async-done | bytes 6291488 | tf_op jit(solution)/shard_map/all_to_all | solution.py:36
  163.5 28.1 %all-to-all-start.4 = ((s32[16,1,128]{2,1,0:T(1,128)}), s32[16,1,128]{2,1,0:T(1,128)S(1)}, u32[]{:S(2)}, u32[]{:S(2)}) async-start(s32[16,1,128]{2,1,0:T(1,128)} %bitcast.6), calls=%async_computation.4 | async-start | bytes 16384 | tf_op jit(solution)/shard_map/all_to_all | solution.py:39
  192.0 8.6 %copy.46 = bf16[2,8,1536,128]{3,1,2,0:T(8,128)(2,1)} copy(bf16[2,8,1536,128]{3,2,1,0:T(8,128)(2,1)} %bitcast.33) | data formatting | bytes 12582912
  200.6 81.8 %while.12 = (s32[]{:T(128)}, bf16[6,12,128,128]{3,2,1,0:T(8,128)(2,1)}, s32[6,12]{1,0:T(8,128)}, s32[6,12]{1,0:T(8,128)S(1)}, s32[16,12]{1,0:T(8,128)S(1)}, /*in...) while((s32[]{:T(128)}, ...), condition=%wide.region_8.9_spmd.clone.clone, body=%wide.region_4.8_spmd.clone.clone.sunk | while | flops 741468800 | bytes 48796596 | solution.py:76
  200.6 0.7 fusion.54
  201.2 4.6 %convolution_convert_fusion.5 = bf16[12,196608]{1,0:T(8,128)(2,1)S(1)} fusion(bf16[16,196608]{1,0:T(8,128)(2,1)} %get-tuple-element.282, s32[12]{0:T(128)S(1)} %get-tuple-element.248), kind=kOutput, calls=%fused_computation.2.clone.1 | convolution fusion | flops 77856960 | bytes 11010096 | tf_op jit(solution)/shard_map/while/body/eval_jaxpr/dot_general | solution.py:48
  205.9 1.2 copy.52
  207.4 1.0 constant_dynamic-slice_fusion.5
  210.0 1.8 convolution_convert_fusion.6
  212.0 2.2 fusion.56
  214.2 0.7 fusion.54
  214.9 4.6 %convolution_convert_fusion.5 = bf16[12,196608]{1,0:T(8,128)(2,1)S(1)} fusion(bf16[16,196608]{1,0:T(8,128)(2,1)} %get-tuple-element.282, s32[12]{0:T(128)S(1)} %get-tuple-element.248), kind=kOutput, calls=%fused_computation.2.clone.1 | convolution fusion | flops 77856960 | bytes 11010096 | tf_op jit(solution)/shard_map/while/body/eval_jaxpr/dot_general | solution.py:48
  219.5 1.2 copy.52
  221.0 1.0 constant_dynamic-slice_fusion.5
  223.6 1.8 convolution_convert_fusion.6
  225.6 2.2 fusion.56
  227.8 0.7 fusion.54
  228.5 4.6 %convolution_convert_fusion.5 = bf16[12,196608]{1,0:T(8,128)(2,1)S(1)} fusion(bf16[16,196608]{1,0:T(8,128)(2,1)} %get-tuple-element.282, s32[12]{0:T(128)S(1)} %get-tuple-element.248), kind=kOutput, calls=%fused_computation.2.clone.1 | convolution fusion | flops 77856960 | bytes 11010096 | tf_op jit(solution)/shard_map/while/body/eval_jaxpr/dot_general | solution.py:48
  233.1 1.2 copy.52
  234.6 1.0 constant_dynamic-slice_fusion.5
  237.3 1.8 convolution_convert_fusion.6
  239.3 2.2 fusion.56
  242.1 4.6 %convolution_convert_fusion.5 = bf16[12,196608]{1,0:T(8,128)(2,1)S(1)} fusion(bf16[16,196608]{1,0:T(8,128)(2,1)} %get-tuple-element.282, s32[12]{0:T(128)S(1)} %get-tuple-element.248), kind=kOutput, calls=%fused_computation.2.clone.1 | convolution fusion | flops 77856960 | bytes 11010096 | tf_op jit(solution)/shard_map/while/body/eval_jaxpr/dot_general | solution.py:48
  246.8 1.2 copy.52
  248.3 1.0 constant_dynamic-slice_fusion.5
  250.9 1.8 convolution_convert_fusion.6
  252.9 2.2 fusion.56
  255.8 4.6 %convolution_convert_fusion.5 = bf16[12,196608]{1,0:T(8,128)(2,1)S(1)} fusion(bf16[16,196608]{1,0:T(8,128)(2,1)} %get-tuple-element.282, s32[12]{0:T(128)S(1)} %get-tuple-element.248), kind=kOutput, calls=%fused_computation.2.clone.1 | convolution fusion | flops 77856960 | bytes 11010096 | tf_op jit(solution)/shard_map/while/body/eval_jaxpr/dot_general | solution.py:48
  260.4 1.2 copy.52
  261.9 1.0 constant_dynamic-slice_fusion.5
  264.5 1.8 convolution_convert_fusion.6
  266.5 2.2 fusion.56
  269.4 4.6 %convolution_convert_fusion.5 = bf16[12,196608]{1,0:T(8,128)(2,1)S(1)} fusion(bf16[16,196608]{1,0:T(8,128)(2,1)} %get-tuple-element.282, s32[12]{0:T(128)S(1)} %get-tuple-element.248), kind=kOutput, calls=%fused_computation.2.clone.1 | convolution fusion | flops 77856960 | bytes 11010096 | tf_op jit(solution)/shard_map/while/body/eval_jaxpr/dot_general | solution.py:48
  274.0 1.2 copy.52
  275.5 1.0 constant_dynamic-slice_fusion.5
  278.2 1.8 convolution_convert_fusion.6
  280.2 2.2 fusion.56
  (77 shorter events, 17.3 us)
Async XLA Ops:
  1.5 13.7 %all-to-all-start = ((s32[16,1,1]{2,1,0:T(1,128)}), s32[16,1,1]{2,1,0:T(1,128)S(1)}, u32[]{:S(2)}, u32[]{:S(2)}) async-start(s32[16,1,1]{2,1,0:T(1,128)} %copy.13), calls=%async_computation | async-start | bytes 16384 | tf_op jit(solution)/shard_map/all_to_all | solution.py:23
  17.0 9.9 %all-to-all-start.2 = ((s32[16,1,1]{2,1,0:T(1,128)}), s32[16,1,1]{2,1,0:T(1,128)S(1)}, u32[]{:S(2)}, u32[]{:S(2)}) async-start(s32[16,1,1]{2,1,0:T(1,128)} %copy.15), calls=%async_computation.2 | async-start | bytes 16384 | tf_op jit(solution)/shard_map/all_to_all | solution.py:38
  26.9 16.3 %all-to-all-start.1 = ((s32[16,1,12]{2,1,0:T(1,128)}), s32[16,1,12]{2,1,0:T(1,128)S(1)}, u32[]{:S(2)}, u32[]{:S(2)}) async-start(s32[16,1,12]{2,1,0:T(1,128)} %bitcast.2), calls=%async_computation.1 | async-start | bytes 16384 | tf_op jit(solution)/shard_map/all_to_all | solution.py:37
  43.2 6.2 %copy-start = (s32[6,128]{1,0:T(8,128)S(1)}, s32[6,128]{1,0:T(8,128)}, u32[]{:S(2)}) copy-start(s32[6,128]{1,0:T(8,128)} %param.11) | copy-start | bytes 9220
  43.2 120.3 %all-to-all-start.3 = ((bf16[16,12,128,128]{3,2,1,0:T(8,128)(2,1)}), bf16[16,12,128,128]{3,2,1,0:T(8,128)(2,1)}, u32[]{:S(2)}, u32[]{:S(2)}) async-start(bf16[16,12,128,128]{3,2,1,0:T(8,128)(2,1)} %bitcast.91), calls=%async_computation.3 | async-start | bytes 12582912 | tf_op jit(solution)/shard_map/all_to_all | solution.py:36
  163.5 37.0 %all-to-all-start.4 = ((s32[16,1,128]{2,1,0:T(1,128)}), s32[16,1,128]{2,1,0:T(1,128)S(1)}, u32[]{:S(2)}, u32[]{:S(2)}) async-start(s32[16,1,128]{2,1,0:T(1,128)} %bitcast.6), calls=%async_computation.4 | async-start | bytes 16384 | tf_op jit(solution)/shard_map/all_to_all | solution.py:39
  192.0 8.6 %copy-start.1 = (s32[6]{0:T(128)S(1)}, s32[6]{0:T(128)}, u32[]{:S(2)}) copy-start(s32[6]{0:T(128)} %param.9) | copy-start | bytes 76
where the time goes:
time: 284 us; the launch traced here: 282 us
  waiting for transfers between devices  125 us (44%)
  matrix products  60.8 us (21%)
  starting transfers between devices  48.6 us (17%)
  local copies, waits for them, and re-layouts  36.5 us (13%)
  other arithmetic  11.2 us (4%)
    all_to_all x1, waiting for transfers between devices, local(): lax.all_to_all(send_tiles, 'col', split_axis=0, concat_axis=0, tiled=True)  114 us
    all_to_all x1, starting transfers between devices, local(): lax.all_to_all(send_degree, 'col', split_axis=0, concat_axis=0, tiled=True)  28.1 us
    dot_general x6, matrix products, row_output(): jnp.dot(owner_onehot, fetched_flat, preferred_element_type=jnp.float32)  27.7 us
    dot_general x6, matrix products, row_output(): jnp.einsum('qsxk,qsyk->qxy', row_matched, other_tiles, preferred_element_...  13.1 us
    unnamed x6, local copies, waits for them, and re-layouts  12.4 us
    dot_general x6, matrix products, row_output(): jnp.einsum('qrs,rxk->qsxk', match_mask, row_tiles, preferred_element_type...  11 us
    dynamic_slice x12, local copies, waits for them, and re-layouts, local(): return lax.map(row_output, (tiles, tile_cols, tile_count, owners, degree))  9.72 us
    dot_general x1, matrix products, local(): jnp.dot(ask_onehot, tiles.reshape(local_rows, -1), preferred_element_type...  8.95 us
  transfers between devices with their start and end apart: 5, of which 3 were waited for; matrix products, arithmetic and copies ran while one was open for 8% of the time, Pallas kernels for 0%

commit v1 on v0

v1 whole, which is shorter than its diff:
```python
import functools

import jax
import jax.numpy as jnp
from jax import lax
from jax.experimental import pallas as pl
from jax.experimental.pallas import tpu as pltpu
from jax.sharding import PartitionSpec as P

VMEM_LIMIT = 48 * 1024 * 1024


def pick_rows_kernel(rows_ref, tiles_ref, out_ref, sems):
    for k in range(out_ref.shape[0]):
        pltpu.make_async_copy(tiles_ref.at[rows_ref[k]], out_ref.at[k], sems.at[k]).start()
    for k in range(out_ref.shape[0]):
        pltpu.make_async_copy(tiles_ref.at[0], out_ref.at[k], sems.at[k]).wait()


def pick_rows(rows, tiles):
    total = rows.shape[0]
    return pl.pallas_call(
        pick_rows_kernel,
        out_shape=jax.ShapeDtypeStruct((total,) + tiles.shape[1:], tiles.dtype),
        in_specs=[pl.BlockSpec(memory_space=pltpu.SMEM), pl.BlockSpec(memory_space=pl.ANY)],
        out_specs=pl.BlockSpec(memory_space=pl.ANY),
        scratch_shapes=[pltpu.SemaphoreType.DMA((total,))],
        name="pick_rows",
    )(rows, tiles)


def blocks_kernel(owner_ref, slot_ref, tiles_ref, fetched_ref, scale_row_ref, scale_other_ref, out_ref):
    local_rows, slots, side, _ = tiles_ref.shape
    cands = out_ref.shape[1]

    def one_row(i, carry):
        left = jnp.concatenate([tiles_ref[i, r] for r in range(slots)], axis=1)
        scale_x = jnp.broadcast_to(scale_row_ref[i], (side, side)).T

        def one_block(q, inner):
            owner = owner_ref[i * cands + q]
            picked = []
            for r in range(slots):
                s = slot_ref[(i * cands + q) * slots + r]
                tile = fetched_ref[owner, jnp.maximum(s, 0)]
                picked.append(jnp.where(s >= 0, tile, jnp.zeros_like(tile)))
            right = jnp.concatenate(picked, axis=1)
            shared = lax.dot_general(left, right, (((1,), (1,)), ((), ())), preferred_element_type=jnp.float32)
            out_ref[i, q] = (shared * (scale_x * scale_other_ref[owner])).astype(out_ref.dtype)
            return inner

        return lax.fori_loop(0, cands, one_block, carry, unroll=2)

    lax.fori_loop(0, local_rows, one_row, 0)


def blocks(owners, slot_of, tiles, fetched, scale_row, scale_other):
    local_rows, slots, side, _ = tiles.shape
    cands = owners.shape[1]
    smem = pl.BlockSpec(memory_space=pltpu.SMEM)
    vmem = pl.BlockSpec(memory_space=pltpu.VMEM)
    return pl.pallas_call(
        blocks_kernel,
        out_shape=jax.ShapeDtypeStruct((local_rows, cands, side, side), jnp.bfloat16),
        in_specs=[smem, smem, vmem, vmem, vmem, vmem],
        out_specs=vmem,
        compiler_params=pltpu.CompilerParams(vmem_limit_bytes=VMEM_LIMIT),
        name="blocks",
    )(owners.reshape(-1), slot_of.reshape(-1), tiles, fetched, scale_row[:, None, :], scale_other[:, None, :])


def local(tiles, tile_cols, tile_count, candidates, degree):
    local_rows, slots, side, _ = tiles.shape
    peers = lax.axis_size("col")
    me = lax.axis_index("col")
    owners = candidates // local_rows
    peer_ids = jnp.arange(peers, dtype=jnp.int32)
    row_ids = jnp.arange(local_rows, dtype=jnp.int32)

    matches = owners[:, :, None] == peer_ids
    wanted = jnp.max(jnp.where(matches, (candidates % local_rows)[:, :, None], 0), axis=(0, 1))

    note = jnp.concatenate([wanted, tile_count, tile_cols.reshape(-1), degree.reshape(-1)])
    note = jnp.pad(note, (0, -note.shape[0] % 128))
    notes = lax.all_to_all(
        jnp.broadcast_to(note, (peers, note.shape[0])), "col", split_axis=0, concat_axis=0, tiled=True
    )
    asked = lax.dynamic_index_in_dim(notes, me, axis=1, keepdims=False)
    at = peers
    counts_all = notes[:, at : at + local_rows]
    at += local_rows
    cols_all = notes[:, at : at + local_rows * slots].reshape(peers, local_rows, slots)
    at += local_rows * slots
    degree_all = notes[:, at : at + local_rows * side].reshape(peers, local_rows, side)

    send = pick_rows(asked, tiles)
    fetched = lax.all_to_all(send, "col", split_axis=0, concat_axis=0, tiled=True)

    mine = wanted[:, None] == row_ids
    count_got = jnp.sum(jnp.where(mine, counts_all, 0), axis=1)
    cols_got = jnp.sum(jnp.where(mine[:, :, None], cols_all, 0), axis=1)
    degree_got = jnp.sum(jnp.where(mine[:, :, None], degree_all, 0), axis=1)
    slot_ids = jnp.arange(slots, dtype=jnp.int32)
    cols_got = jnp.where(slot_ids < count_got[:, None], cols_got, -1)
    cols_other = jnp.sum(jnp.where(matches[..., None], cols_got, 0), axis=2)
    cols_mine = jnp.where(slot_ids < tile_count[:, None], tile_cols, -2)
    meets = cols_mine[:, None, :, None] == cols_other[:, :, None, :]
    slot_of = jnp.sum(jnp.where(meets, slot_ids + 1, 0), axis=3) - 1

    scale_row = lax.rsqrt(degree.astype(jnp.float32))
    scale_other = lax.rsqrt(degree_got.astype(jnp.float32))
    return blocks(owners, slot_of, tiles, fetched, scale_row, scale_other)


def solution(mesh):
    in_specs = (
        P(("slab", "col"), None, None, None),
        P(("slab", "col"), None),
        P(("slab", "col")),
        P(("slab", "col"), None),
        P(("slab", "col"), None),
    )
    out_specs = P(("slab", "col"), None, None, None)
    return jax.shard_map(local, mesh=mesh, in_specs=in_specs, out_specs=out_specs, check_vma=False)
```

time: 284 us -> 371 us (1.31)
  the two profiles are of different devices: /device:TPU:0 before, /device:TPU:13 now
where the time goes in v1:
time: 371 us
  Pallas kernels  211 us (57%)
  waiting for transfers between devices  139 us (37%)
  starting transfers between devices  13.8 us (4%)
  other arithmetic  3.89 us (1%)
    pallas_call x1, Pallas kernels, pick_rows(): pl.pallas_call(pick_rows_kernel, out_shape=jax.ShapeDtypeStruct((total,)...  192 us
    all_to_all x1, waiting for transfers between devices, local(): lax.all_to_all(send, 'col', split_axis=0, concat_axis=0, tiled=True)  135 us
    pallas_call x1, Pallas kernels, blocks(): pl.pallas_call(blocks_kernel, out_shape=jax.ShapeDtypeStruct((local_rows,...  19 us
  transfers between devices with their start and end apart: 2, of which 2 were waited for; matrix products, arithmetic and copies ran while one was open for 1% of the time, Pallas kernels for 0%

profile of v1, /device:TPU:13, one launch (start us, length us, event | category | flops | bytes accessed | tf_op | source)
XLA Modules:
  0.0 370.9 jit_solution(2746208672023791795)
XLA Ops:
  0.0 0.8 reshape.67
  0.8 0.7 add_select_fusion
  1.5 0.1 select_reduce_fusion.4
  1.6 0.8 pad_add_fusion
  2.3 0.7 broadcast_in_dim.97
  3.0 6.6 %all-to-all-start = ((s32[16,1,896]{2,1,0:T(1,128)}), s32[16,1,896]{2,1,0:T(1,128)S(1)}, u32[]{:S(2)}, u32[]{:S(2)}) async-start(s32[16,1,896]{2,1,0:T(1,128)} %broadcast_in_dim.97), calls=%async_computation | async-start | bytes 114688 | tf_op jit(solution)/shard_map/all_to_all | solution.py:85
  9.6 4.2 %all-to-all-done = s32[16,1,896]{2,1,0:T(1,128)S(1)} async-done(((s32[16,1,896]{2,1,0:T(1,128)}), s32[16,1,896]{2,1,0:T(1,128)S(1)}, u32[]{:S(2)}, u32[]{:S(2)}) %all-to-all-start) | async-done | bytes 57376 | tf_op jit(solution)/shard_map/all_to_all | solution.py:85
  13.8 1.0 dynamic-slice_reduce_fusion.rows_ref
  14.7 192.5 %pick_rows.1 = bf16[16,12,128,128]{3,2,1,0:T(8,128)(2,1)} custom-call(s32[16]{0:T(128)} %dynamic-slice_reduce_fusion.rows_ref, bf16[6,12,128,128]{3,2,1,0:T(8,128)(2,1)} %tiles_ref.3), custom_call_target="tpu_custom_call" | custom-call | tf_op jit(solution)/shard_map/pick_rows/pallas_call | solution.py:22
  207.3 0.0 copy-start.1
  207.3 0.0 copy-start.2
  207.3 0.0 copy-start.3
  207.3 0.0 copy-start
  207.3 7.2 %all-to-all-start.1 = ((bf16[16,12,128,128]{3,2,1,0:T(8,128)(2,1)}), bf16[16,12,128,128]{3,2,1,0:T(8,128)(2,1)}, u32[]{:S(2)}, u32[]{:S(2)}) async-start(bf16[16,12,128,128]{3,2,1,0:T(8,128)(2,1)} %pick_rows.1), calls=%async_computation.1 | async-start | bytes 12582912 | tf_op jit(solution)/shard_map/all_to_all | solution.py:97
  214.5 0.1 reshape.66.owner_ref
  214.6 0.0 copy-done.1
  214.6 0.1 iota_compare_fusion.1
  214.7 0.0 copy-done.2
  214.7 0.0 copy-done.3
  214.7 0.1 fusion.3
  214.8 0.1 iota_compare_fusion
  214.9 0.1 slice.13
  215.0 0.1 slice.14
  215.1 0.1 reshape.69
  215.1 0.2 fusion
  215.3 0.1 select_reduce_fusion.3
  215.4 0.1 fusion.1
  215.5 0.3 select_reduce_fusion.1
  215.8 1.4 select_reduce_fusion
  217.2 0.1 sub.14.slot_ref
  217.3 0.1 select_reduce_fusion.2
  217.4 134.6 %all-to-all-done.1.fetched_ref = bf16[16,12,128,128]{3,2,1,0:T(8,128)(2,1)} async-done(((bf16[16,12,128,128]{3,2,1,0:T(8,128)(2,1)}), bf16[16,12,128,128]{3,2,1,0:T(8,128)(2,1)}, u32[]{:S(2)}, u32[]{:S(2)}) %all-to-all-start.1) | async-done | bytes 6291488 | tf_op jit(solution)/shard_map/all_to_all | solution.py:97
  352.0 0.0 copy-done
  352.0 19.0 %blocks.1 = bf16[6,12,128,128]{3,2,1,0:T(8,128)(2,1)} custom-call(s32[72]{0:T(128)S(1)} %reshape.66.owner_ref, s32[864]{0:T(1024)S(1)} %sub.14.slot_ref, bf16[6,12,128,128]{3,2,1,0:T(8,128)(2,1)S(1)} %copy-done, bf16[16,12,128,128]{3,2,1,0:T(8,128)(2,1)} %all-to-all-done.1.fetched_ref, f32[6,1,128]{2,1,0:T(1,128)S(1)} %broadcast_in_dim.106.scale_row_ref, ...), custom_call_target="tpu_custom_call" | custom-call | tf_op jit(solution)/shard_map/blocks/pallas_call | solution.py:62
  (8 shorter events, 0.0 us)
Async XLA Ops:
  3.0 10.8 %all-to-all-start = ((s32[16,1,896]{2,1,0:T(1,128)}), s32[16,1,896]{2,1,0:T(1,128)S(1)}, u32[]{:S(2)}, u32[]{:S(2)}) async-start(s32[16,1,896]{2,1,0:T(1,128)} %broadcast_in_dim.97), calls=%async_computation | async-start | bytes 114688 | tf_op jit(solution)/shard_map/all_to_all | solution.py:85
  207.3 7.4 %copy-start.1 = (s32[6,128]{1,0:T(8,128)S(1)}, s32[6,128]{1,0:T(8,128)}, u32[]{:S(2)}) copy-start(s32[6,128]{1,0:T(8,128)} %param.9) | copy-start | bytes 9220
  207.3 7.5 %copy-start.2 = (s32[6,12]{1,0:T(8,128)S(1)}, s32[6,12]{1,0:T(8,128)}, u32[]{:S(2)}) copy-start(s32[6,12]{1,0:T(8,128)} %param.6) | copy-start | bytes 868
  207.3 7.5 %copy-start.3 = (s32[6]{0:T(128)S(1)}, s32[6]{0:T(128)}, u32[]{:S(2)}) copy-start(s32[6]{0:T(128)} %param.7) | copy-start | bytes 76
  207.3 144.7 %copy-start = (bf16[6,12,128,128]{3,2,1,0:T(8,128)(2,1)S(1)}, bf16[6,12,128,128]{3,2,1,0:T(8,128)(2,1)}, u32[]{:S(2)}) copy-start(bf16[6,12,128,128]{3,2,1,0:T(8,128)(2,1)} %tiles_ref.3) | copy-start | bytes 7077892
  207.3 144.7 %all-to-all-start.1 = ((bf16[16,12,128,128]{3,2,1,0:T(8,128)(2,1)}), bf16[16,12,128,128]{3,2,1,0:T(8,128)(2,1)}, u32[]{:S(2)}, u32[]{:S(2)}) async-start(bf16[16,12,128,128]{3,2,1,0:T(8,128)(2,1)} %pick_rows.1), calls=%async_computation.1 | async-start | bytes 12582912 | tf_op jit(solution)/shard_map/all_to_all | solution.py:97

commit v2 on v1

--- a/solution.py
+++ b/solution.py
@@ -22,9 +22,10 @@
     return pl.pallas_call(
         pick_rows_kernel,
         out_shape=jax.ShapeDtypeStruct((total,) + tiles.shape[1:], tiles.dtype),
-        in_specs=[pl.BlockSpec(memory_space=pltpu.SMEM), pl.BlockSpec(memory_space=pl.ANY)],
+        in_specs=[pl.BlockSpec(memory_space=pltpu.SMEM), pl.BlockSpec(memory_space=pltpu.VMEM)],
         out_specs=pl.BlockSpec(memory_space=pl.ANY),
         scratch_shapes=[pltpu.SemaphoreType.DMA((total,))],
+        compiler_params=pltpu.CompilerParams(vmem_limit_bytes=VMEM_LIMIT),
         name="pick_rows",
     )(rows, tiles)
 

time: 371 us -> 183 us (0.49)
  Pallas kernels: 211 us -> 22.3 us
    pallas_call x1, Pallas kernels: 192 us -> 3.34 us  [pick_rows(): pl.pallas_call(pick_rows_kernel, out_shape=jax.ShapeDtypeStruct((total,)...]
where the time goes in v2:
time: 183 us
  waiting for transfers between devices  139 us (76%)
  Pallas kernels  22.3 us (12%)
  starting transfers between devices  13.8 us (8%)
  local copies, waits for them, and re-layouts  3.98 us (2%)
  other arithmetic  3.89 us (2%)
    all_to_all x1, waiting for transfers between devices, local(): lax.all_to_all(send, 'col', split_axis=0, concat_axis=0, tiled=True)  135 us
    pallas_call x1, Pallas kernels, blocks(): pl.pallas_call(blocks_kernel, out_shape=jax.ShapeDtypeStruct((local_rows,...  18.9 us
    all_to_all x1, starting transfers between devices, local(): lax.all_to_all(send, 'col', split_axis=0, concat_axis=0, tiled=True)  7.24 us
    all_to_all x1, starting transfers between devices, local(): lax.all_to_all(jnp.broadcast_to(note, (peers, note.shape[0])), 'col', spl...  6.55 us
    all_to_all x1, waiting for transfers between devices, local(): lax.all_to_all(jnp.broadcast_to(note, (peers, note.shape[0])), 'col', spl...  4.22 us
  transfers between devices with their start and end apart: 2, of which 2 were waited for; matrix products, arithmetic and copies ran while one was open for 1% of the time, Pallas kernels for 0%

profile of v2, /device:TPU:13, one launch (start us, length us, event | category | flops | bytes accessed | tf_op | source)
XLA Modules:
  0.0 182.9 jit_solution(4440443533263378462)
XLA Ops:
  0.0 0.8 reshape.67
  0.8 0.7 add_select_fusion
  1.5 0.1 select_reduce_fusion.4
  1.6 0.8 pad_add_fusion
  2.3 0.7 broadcast_in_dim.97
  3.0 6.6 %all-to-all-start = ((s32[16,1,896]{2,1,0:T(1,128)}), s32[16,1,896]{2,1,0:T(1,128)S(1)}, u32[]{:S(2)}, u32[]{:S(2)}) async-start(s32[16,1,896]{2,1,0:T(1,128)} %broadcast_in_dim.97), calls=%async_computation | async-start | bytes 114688 | tf_op jit(solution)/shard_map/all_to_all | solution.py:86
  9.6 4.2 %all-to-all-done = s32[16,1,896]{2,1,0:T(1,128)S(1)} async-done(((s32[16,1,896]{2,1,0:T(1,128)}), s32[16,1,896]{2,1,0:T(1,128)S(1)}, u32[]{:S(2)}, u32[]{:S(2)}) %all-to-all-start) | async-done | bytes 57376 | tf_op jit(solution)/shard_map/all_to_all | solution.py:86
  13.8 0.4 dynamic-slice_reduce_fusion.rows_ref
  14.2 0.0 copy-start
  14.2 1.7 copy-done
  15.9 3.3 %pick_rows.1 = bf16[16,12,128,128]{3,2,1,0:T(8,128)(2,1)} custom-call(s32[16]{0:T(128)S(1)} %dynamic-slice_reduce_fusion.rows_ref, bf16[6,12,128,128]{3,2,1,0:T(8,128)(2,1)S(1)} %copy-done), custom_call_target="tpu_custom_call" | custom-call | tf_op jit(solution)/shard_map/pick_rows/pallas_call | solution.py:22
  19.3 0.0 copy-start.2
  19.3 0.0 copy-start.3
  19.3 0.0 copy-start.4
  19.3 0.0 copy-start.1
  19.3 7.2 %all-to-all-start.1 = ((bf16[16,12,128,128]{3,2,1,0:T(8,128)(2,1)}), bf16[16,12,128,128]{3,2,1,0:T(8,128)(2,1)}, u32[]{:S(2)}, u32[]{:S(2)}) async-start(bf16[16,12,128,128]{3,2,1,0:T(8,128)(2,1)} %pick_rows.1), calls=%async_computation.1 | async-start | bytes 12582912 | tf_op jit(solution)/shard_map/all_to_all | solution.py:98
  26.5 0.1 reshape.66.owner_ref
  26.6 0.0 copy-done.2
  26.7 0.1 iota_compare_fusion.1
  26.7 0.0 copy-done.3
  26.7 0.0 copy-done.4
  26.7 0.1 fusion.3
  26.8 0.1 iota_compare_fusion
  26.9 0.1 slice.13
  27.0 0.1 slice.14
  27.1 0.1 reshape.69
  27.2 0.2 fusion
  27.3 0.1 select_reduce_fusion.3
  27.4 0.1 fusion.1
  27.5 0.3 select_reduce_fusion.1
  27.8 1.4 select_reduce_fusion
  29.2 0.1 sub.14.slot_ref
  29.3 0.1 select_reduce_fusion.2
  29.4 134.6 %all-to-all-done.1.fetched_ref = bf16[16,12,128,128]{3,2,1,0:T(8,128)(2,1)} async-done(((bf16[16,12,128,128]{3,2,1,0:T(8,128)(2,1)}), bf16[16,12,128,128]{3,2,1,0:T(8,128)(2,1)}, u32[]{:S(2)}, u32[]{:S(2)}) %all-to-all-start.1) | async-done | bytes 6291488 | tf_op jit(solution)/shard_map/all_to_all | solution.py:98
  164.0 0.0 copy-done.1
  164.0 18.9 %blocks.1 = bf16[6,12,128,128]{3,2,1,0:T(8,128)(2,1)} custom-call(s32[72]{0:T(128)S(1)} %reshape.66.owner_ref, s32[864]{0:T(1024)S(1)} %sub.14.slot_ref, bf16[6,12,128,128]{3,2,1,0:T(8,128)(2,1)S(1)} %copy-done.1, bf16[16,12,128,128]{3,2,1,0:T(8,128)(2,1)} %all-to-all-done.1.fetched_ref, f32[6,1,128]{2,1,0:T(1,128)S(1)} %broadcast_in_dim.106.scale_row_ref, ...), custom_call_target="tpu_custom_call" | custom-call | tf_op jit(solution)/shard_map/blocks/pallas_call | solution.py:63
  (8 shorter events, 0.1 us)
Async XLA Ops:
  3.0 10.8 %all-to-all-start = ((s32[16,1,896]{2,1,0:T(1,128)}), s32[16,1,896]{2,1,0:T(1,128)S(1)}, u32[]{:S(2)}, u32[]{:S(2)}) async-start(s32[16,1,896]{2,1,0:T(1,128)} %broadcast_in_dim.97), calls=%async_computation | async-start | bytes 114688 | tf_op jit(solution)/shard_map/all_to_all | solution.py:86
  14.2 1.7 copy-start
  19.3 7.4 %copy-start.2 = (s32[6,128]{1,0:T(8,128)S(1)}, s32[6,128]{1,0:T(8,128)}, u32[]{:S(2)}) copy-start(s32[6,128]{1,0:T(8,128)} %param.9) | copy-start | bytes 9220
  19.3 7.5 %copy-start.3 = (s32[6,12]{1,0:T(8,128)S(1)}, s32[6,12]{1,0:T(8,128)}, u32[]{:S(2)}) copy-start(s32[6,12]{1,0:T(8,128)} %param.6) | copy-start | bytes 868
  19.3 7.5 %copy-start.4 = (s32[6]{0:T(128)S(1)}, s32[6]{0:T(128)}, u32[]{:S(2)}) copy-start(s32[6]{0:T(128)} %param.7) | copy-start | bytes 76
  19.3 144.7 %copy-start.1 = (bf16[6,12,128,128]{3,2,1,0:T(8,128)(2,1)S(1)}, bf16[6,12,128,128]{3,2,1,0:T(8,128)(2,1)}, u32[]{:S(2)}) copy-start(bf16[6,12,128,128]{3,2,1,0:T(8,128)(2,1)} %tiles_ref.3) | copy-start | bytes 7077892
  19.3 144.7 %all-to-all-start.1 = ((bf16[16,12,128,128]{3,2,1,0:T(8,128)(2,1)}), bf16[16,12,128,128]{3,2,1,0:T(8,128)(2,1)}, u32[]{:S(2)}, u32[]{:S(2)}) async-start(bf16[16,12,128,128]{3,2,1,0:T(8,128)(2,1)} %pick_rows.1), calls=%async_computation.1 | async-start | bytes 12582912 | tf_op jit(solution)/shard_map/all_to_all | solution.py:98

commit v3 on v1

v3 whole, which is shorter than its diff:
```python
import functools

import jax
import jax.numpy as jnp
from jax import lax
from jax.experimental import pallas as pl
from jax.experimental.pallas import tpu as pltpu
from jax.sharding import PartitionSpec as P

VMEM_LIMIT = 48 * 1024 * 1024
SMEM = pl.BlockSpec(memory_space=pltpu.SMEM)
VMEM = pl.BlockSpec(memory_space=pltpu.VMEM)
HBM = pl.BlockSpec(memory_space=pl.ANY)
PARAMS = pltpu.CompilerParams(vmem_limit_bytes=VMEM_LIMIT)


def pick_rows_kernel(sizes, rows_ref, tiles_ref, *refs):
    outs, sems = refs[:-1], refs[-1]
    places = [(ref, k) for ref, size in zip(outs, sizes) for k in range(size)]
    for at, (ref, k) in enumerate(places):
        pltpu.make_async_copy(tiles_ref.at[rows_ref[at]], ref.at[k], sems.at[at]).start()
    for at, (ref, k) in enumerate(places):
        pltpu.make_async_copy(tiles_ref.at[0], ref.at[k], sems.at[at]).wait()


def pick_rows(rows, tiles, sizes):
    return pl.pallas_call(
        functools.partial(pick_rows_kernel, sizes),
        out_shape=[jax.ShapeDtypeStruct((size,) + tiles.shape[1:], tiles.dtype) for size in sizes],
        in_specs=[SMEM, VMEM],
        out_specs=[HBM] * len(sizes),
        scratch_shapes=[pltpu.SemaphoreType.DMA((sum(sizes),))],
        compiler_params=PARAMS,
        name="pick_rows",
    )(rows, tiles)


def fetch_rows(total, source_ref, row_ref, sources, target_ref, sems):
    for k in range(total):
        for at, ref in enumerate(sources):

            last = at == len(sources) - 1

            @pl.when(source_ref[k] >= at if last else source_ref[k] == at)
            def _():
                pltpu.make_async_copy(ref.at[row_ref[k]], target_ref.at[k], sems.at[k]).start()

    for k in range(total):
        pltpu.make_async_copy(sources[0].at[0], target_ref.at[k], sems.at[k]).wait()


def collect_kernel(total, source_ref, row_ref, *refs):
    *sources, out_ref, sems = refs
    fetch_rows(total, source_ref, row_ref, sources, out_ref, sems)


def collect(places, *sources):
    total = len(places)
    source_ids = jnp.stack([jnp.asarray(s, jnp.int32) for s, _ in places])
    row_ids = jnp.stack([jnp.asarray(row, jnp.int32) for _, row in places])
    return pl.pallas_call(
        functools.partial(collect_kernel, total),
        out_shape=jax.ShapeDtypeStruct((total,) + sources[0].shape[1:], sources[0].dtype),
        in_specs=[SMEM, SMEM] + [HBM] * len(sources),
        out_specs=VMEM,
        scratch_shapes=[pltpu.SemaphoreType.DMA((total,))],
        compiler_params=PARAMS,
        name="collect",
    )(source_ids, row_ids, *sources)


def blocks_kernel(total, prior, place_ref, slot_ref, source_ref, row_ref, tiles_ref, scale_row_ref, scale_got_ref, *refs):
    *sources, out_ref, fetched_ref, sems = refs
    if prior:
        prior_ref, *sources = sources
    local_rows, slots, side, _ = tiles_ref.shape
    cands = out_ref.shape[1]
    fetch_rows(total, source_ref, row_ref, sources, fetched_ref, sems)

    def one_row(i, carry):
        left = jnp.concatenate([tiles_ref[i, r] for r in range(slots)], axis=1)
        scale_x = jnp.broadcast_to(scale_row_ref[i], (side, side)).T

        def one_block(q, inner):
            place = place_ref[i * cands + q]

            @pl.when(place >= 0)
            def _():
                picked = []
                for r in range(slots):
                    s = slot_ref[(i * cands + q) * slots + r]
                    tile = fetched_ref[place, jnp.maximum(s, 0)]
                    picked.append(jnp.where(s >= 0, tile, jnp.zeros_like(tile)))
                right = jnp.concatenate(picked, axis=1)
                shared = lax.dot_general(left, right, (((1,), (1,)), ((), ())), preferred_element_type=jnp.float32)
                out_ref[i, q] = (shared * (scale_x * scale_got_ref[place])).astype(out_ref.dtype)

            if prior:

                @pl.when(place < 0)
                def _():
                    out_ref[i, q] = prior_ref[i, q]

            return inner

        return lax.fori_loop(0, cands, one_block, carry, unroll=2)

    lax.fori_loop(0, local_rows, one_row, 0)


def blocks(place, slot_of, places, tiles, scale_row, scale_got, sources, prior=None):
    local_rows, slots, side, _ = tiles.shape
    total = len(places)
    source_ids = jnp.stack([jnp.asarray(s, jnp.int32) for s, _ in places])
    row_ids = jnp.stack([jnp.asarray(row, jnp.int32) for _, row in places])
    extra = [] if prior is None else [prior]
    return pl.pallas_call(
        functools.partial(blocks_kernel, total, prior is not None),
        out_shape=jax.ShapeDtypeStruct((local_rows, place.shape[1], side, side), jnp.bfloat16),
        in_specs=[SMEM] * 4 + [VMEM] * (3 + len(extra)) + [HBM] * len(sources),
        out_specs=VMEM,
        scratch_shapes=[
            pltpu.VMEM((total,) + tiles.shape[1:], tiles.dtype),
            pltpu.SemaphoreType.DMA((total,)),
        ],
        compiler_params=PARAMS,
        name="blocks",
    )(
        place.reshape(-1), slot_of.reshape(-1), source_ids, row_ids, tiles, scale_row[:, None, :], scale_got[:, None, :],
        *extra, *sources,
    )


def exchange_direct(wanted_by, me, tiles):
    asked = lax.dynamic_index_in_dim(wanted_by, me, axis=1, keepdims=False)
    (send,) = pick_rows(asked, tiles, (asked.shape[0],))
    return lax.all_to_all(send, "col", split_axis=0, concat_axis=0, tiled=True)


def moves(target):
    return [(4 * z + p, 4 * target[z] + p) for z in range(4) for p in range(4) if target[z] is not None]


BESIDE = moves([1, 0, 3, 2])
MIDDLE = moves([None, 2, 1, None])
ACROSS = moves([2, None, None, 1])
OUTWARD = moves([None, 0, 3, None])
Y_MATE = [(i, i ^ 2) for i in range(16)]
CORE_MATE = [(i, i ^ 1) for i in range(16)]


def relay(wanted_by, me, tiles, make_blocks):
    plane, mate = me // 4, me % 4
    inner = (plane == 1) | (plane == 2)

    def want(to_plane, m, from_plane):
        return wanted_by[4 * to_plane + (mate ^ m), 4 * from_plane + mate]

    outer = jnp.where(inner, plane ^ 2, plane)
    row_ids = jnp.arange(tiles.shape[0], dtype=jnp.int32)
    key = row_ids + 4
    for at, m in ((3, 1), (2, 0), (1, 3), (0, 2)):
        key = jnp.where(row_ids == want(outer ^ 3, m, outer), at, key)
    rank = jnp.sum((key[None, :] < key[:, None]).astype(jnp.int32), axis=1)
    order = jnp.sum(jnp.where(rank[None, :] == row_ids[:, None], row_ids[None, :], 0), axis=1)

    def rank_of(row):
        return jnp.sum(jnp.where(row_ids == row, rank, 0))

    middle = lax.ppermute(tiles, "col", MIDDLE)
    rows = [want(plane ^ 1, m, plane) for m in range(4)] + [want(plane, m, plane) for m in (2, 3, 0, 1)]
    beside_send, y1_send, own = pick_rows(jnp.stack(rows), tiles, (4, 2, 2))
    beside = lax.ppermute(beside_send, "col", BESIDE)
    y1 = lax.ppermute(y1_send, "col", Y_MATE)
    far_send = pick_rows(order, tiles, (2, 2, 2))
    far = [lax.ppermute(part, "col", ACROSS) for part in far_send]

    out_send = collect([(0, want(plane ^ 1, m, plane ^ 3)) for m in range(4)], middle)
    out_near = lax.ppermute(out_send, "col", OUTWARD)
    y2 = lax.ppermute(collect([(0, 2), (0, 3)], beside), "col", Y_MATE)

    def far_place(row):
        at = rank_of(row)
        return at // 2, at % 2

    g1_send = collect([far_place(want(plane ^ 1, m, plane ^ 2)) for m in (2, 3)], *far[:1])
    g1 = lax.ppermute(g1_send, "col", OUTWARD)
    g2_send = collect([far_place(want(plane ^ 1, m, plane ^ 2)) for m in (0, 1)], *far[:2])
    g2 = lax.ppermute(g2_send, "col", OUTWARD)

    core_a = lax.ppermute(collect([(0, 1), (1, 1), (2, 1), (3, 1)], own, y1, beside, y2), "col", CORE_MATE)
    done = make_blocks(
        (0, 1), [(0, 0), (4, 0), (1, 0), (4, 1), (2, 0), (4, 2), (3, 0), (4, 3)], (own, y1, beside, y2, core_a), None
    )

    def third(m):
        return jnp.where(inner, 0, 1), jnp.where(inner, want(plane, m, plane ^ 3), m)

    y3 = lax.ppermute(collect([third(2), third(3)], middle, out_near), "col", Y_MATE)
    core_b = lax.ppermute(collect([third(1), (2, 1)], middle, out_near, y3), "col", CORE_MATE)
    done = make_blocks((2,), [third(0), (3, 0), (2, 0), (3, 1)], (middle, out_near, y3, core_b), done)

    def fourth(m):
        at = rank_of(want(plane, m, plane ^ 2))
        return jnp.where(inner, at // 2, 3), jnp.where(inner, at % 2, m % 2)

    y4 = lax.ppermute(collect([fourth(2), fourth(3)], *far, g1), "col", Y_MATE)
    core_c = lax.ppermute(collect([fourth(1), (4, 1)], *far, g2, y4), "col", CORE_MATE)
    return make_blocks((3,), [fourth(0), (5, 0), (4, 0), (5, 1)], (*far, g2, y4, core_c), done)


def local(tiles, tile_cols, tile_count, candidates, degree):
    local_rows, slots, side, _ = tiles.shape
    peers = lax.axis_size("col")
    me = lax.axis_index("col")
    owners = candidates // local_rows
    peer_ids = jnp.arange(peers, dtype=jnp.int32)
    row_ids = jnp.arange(local_rows, dtype=jnp.int32)

    matches = owners[:, :, None] == peer_ids
    wanted = jnp.max(jnp.where(matches, (candidates % local_rows)[:, :, None], 0), axis=(0, 1))

    note = jnp.concatenate([wanted, tile_count, tile_cols.reshape(-1), degree.reshape(-1)])
    note = jnp.pad(note, (0, -note.shape[0] % 128))
    notes = lax.all_to_all(
        jnp.broadcast_to(note, (peers, note.shape[0])), "col", split_axis=0, concat_axis=0, tiled=True
    )
    wanted_by = notes[:, :peers]
    at = peers
    counts_all = notes[:, at : at + local_rows]
    at += local_rows
    cols_all = notes[:, at : at + local_rows * slots].reshape(peers, local_rows, slots)
    at += local_rows * slots
    degree_all = notes[:, at : at + local_rows * side].reshape(peers, local_rows, side)

    mine = wanted[:, None] == row_ids
    count_got = jnp.sum(jnp.where(mine, counts_all, 0), axis=1)
    cols_got = jnp.sum(jnp.where(mine[:, :, None], cols_all, 0), axis=1)
    degree_got = jnp.sum(jnp.where(mine[:, :, None], degree_all, 0), axis=1)
    slot_ids = jnp.arange(slots, dtype=jnp.int32)
    cols_got = jnp.where(slot_ids < count_got[:, None], cols_got, -1)
    cols_other = jnp.sum(jnp.where(matches[..., None], cols_got, 0), axis=2)
    cols_mine = jnp.where(slot_ids < tile_count[:, None], tile_cols, -2)
    meets = cols_mine[:, None, :, None] == cols_other[:, :, None, :]
    slot_of = jnp.sum(jnp.where(meets, slot_ids + 1, 0), axis=3) - 1

    scale_row = lax.rsqrt(degree.astype(jnp.float32))
    scale_other = lax.rsqrt(degree_got.astype(jnp.float32))

    if peers != 16:
        fetched = exchange_direct(wanted_by, me, tiles)
        places = [(0, k) for k in range(peers)]
        return blocks(owners, slot_of, places, tiles, scale_row, scale_other, [fetched])

    plane, mate = me // 4, me % 4
    inner = (plane == 1) | (plane == 2)
    group_planes = [plane, plane ^ 1, jnp.where(inner, plane ^ 3, plane ^ 2), jnp.where(inner, plane ^ 2, plane ^ 3)]

    def make_blocks(groups, places, sources, prior):
        place = jnp.full_like(owners, -1)
        for at, group in enumerate(groups):
            place = jnp.where(owners // 4 == group_planes[group], 4 * at + (mate ^ (owners % 4)), place)
        owner_of = jnp.concatenate([4 * group_planes[g] + (mate ^ jnp.arange(4, dtype=jnp.int32)) for g in groups])
        scale_got = jnp.sum(jnp.where((owner_of[:, None] == peer_ids)[:, :, None], scale_other, 0.0), axis=1)
        return blocks(place, slot_of, places, tiles, scale_row, scale_got, sources, prior)

    return relay(wanted_by, me, tiles, make_blocks)


def solution(mesh):
    in_specs = (
        P(("slab", "col"), None, None, None),
        P(("slab", "col"), None),
        P(("slab", "col")),
        P(("slab", "col"), None),
        P(("slab", "col"), None),
    )
    out_specs = P(("slab", "col"), None, None, None)
    return jax.shard_map(local, mesh=mesh, in_specs=in_specs, out_specs=out_specs, check_vma=False)
```

time: 371 us -> 242 us (0.65)
  the two profiles are of different devices: /device:TPU:13 before, /device:TPU:0 now
where the time goes in v3:
time: 242 us; the launch traced here: 240 us
  waiting for transfers between devices  92.8 us (38%)
  Pallas kernels  63.6 us (26%)
  starting transfers between devices  29.5 us (12%)
  between operations  23.4 us (10%)
  other arithmetic  16.9 us (7%)
  local copies, waits for them, and re-layouts  13.6 us (6%)
    all_to_all x1, waiting for transfers between devices, local(): lax.all_to_all(jnp.broadcast_to(note, (peers, note.shape[0])), 'col', spl...  46 us
    pallas_call x3, Pallas kernels, blocks(): pl.pallas_call(functools.partial(blocks_kernel, total, prior is not None)...  39.6 us
    ppermute x3, waiting for transfers between devices, relay(): far = [lax.ppermute(part, 'col', ACROSS) for part in far_send]  27.8 us
    pallas_call x9, Pallas kernels, collect(): pl.pallas_call(functools.partial(collect_kernel, total), out_shape=jax.Sh...  20.5 us
    ppermute x1, waiting for transfers between devices, relay(): lax.ppermute(collect([third(2), third(3)], middle, out_near), 'col', Y_MATE)  13.3 us
    ppermute x3, starting transfers between devices, relay(): far = [lax.ppermute(part, 'col', ACROSS) for part in far_send]  11.9 us
    all_to_all x1, starting transfers between devices, local(): lax.all_to_all(jnp.broadcast_to(note, (peers, note.shape[0])), 'col', spl...  7.39 us
    reduce_sum x1, other arithmetic, rank_of(): return jnp.sum(jnp.where(row_ids == row, rank, 0))  5.88 us
  transfers between devices with their start and end apart: 16, of which 8 were waited for; matrix products, arithmetic and copies ran while one was open for 10% of the time, Pallas kernels for 21%

profile of v3, /device:TPU:0, one launch (start us, length us, event | category | flops | bytes accessed | tf_op | source)
XLA Modules:
  0.0 239.8 jit_solution(2848812766862988607)
XLA Ops:
  0.0 2.1 collective-permute-start.4
  2.1 0.8 reshape.163
  2.8 0.7 select_select_fusion
  3.7 0.8 pad_add_fusion
  4.4 0.7 broadcast_in_dim.194
  5.1 7.4 %all-to-all-start = ((s32[16,1,896]{2,1,0:T(1,128)}), s32[16,1,896]{2,1,0:T(1,128)S(1)}, u32[]{:S(2)}, u32[]{:S(2)}) async-start(s32[16,1,896]{2,1,0:T(1,128)} %broadcast_in_dim.194), calls=%async_computation | async-start | bytes 114688 | tf_op jit(solution)/shard_map/all_to_all | solution.py:225
  12.8 0.7 convert_rsqrt_fusion.1
  13.5 46.0 %all-to-all-done = s32[16,1,896]{2,1,0:T(1,128)S(1)} async-done(((s32[16,1,896]{2,1,0:T(1,128)}), s32[16,1,896]{2,1,0:T(1,128)S(1)}, u32[]{:S(2)}, u32[]{:S(2)}) %all-to-all-start) | async-done | bytes 57376 | tf_op jit(solution)/shard_map/all_to_all | solution.py:225
  59.5 0.8 fusion.19
  60.3 5.0 %stack.128.rows_ref = s32[8]{0:T(128)S(1)} concatenate(s32[1]{0:T(128)} %bitcast.14, s32[1]{0:T(128)} %bitcast.15, s32[1]{0:T(128)} %bitcast.16, s32[1]{0:T(128)} %bitcast.17, s32[1]{0:T(128)} %bitcast.18, s32[1]{0:T(128)} %bitcast.19, s32[1]{0:T(128)} %bitcast.20, s32[1]{0:T(128)} %bitcast.21), dimensions={0} | concatenate | bytes 64 | tf_op jit(solution)/shard_map/stack | solution.py:172
  65.3 1.7 copy-done
  66.9 1.8 pick_rows.2
  68.7 0.9 copy-done.3
  69.6 0.9 copy-done.9
  71.5 2.5 %compare_select_fusion.12 = s32[6]{0:T(128)S(1)} fusion(s32[]{:T(128)} %bitcast.5, s32[]{:T(128)} %bitcast.4, s32[]{:T(128)} %bitcast.3, s32[]{:T(128)} %bitcast.2), kind=kLoop, calls=%fused_computation.54 | loop fusion | flops 54 | bytes 40 | tf_op jit(solution)/shard_map/jit(_where)/select_n | solution.py:163
  74.3 1.8 pick_rows.3
  76.2 0.9 copy-done.10
  77.0 4.4 %collective-permute-start.8 = (bf16[2,12,128,128]{3,2,1,0:T(8,128)(2,1)}, bf16[2,12,128,128]{3,2,1,0:T(8,128)(2,1)S(1)}, u32[]{:S(2)}, u32[]{:S(2)}) collective-permute-start(bf16[2,12,128,128]{3,2,1,0:T(8,128)(2,1)} %get-tuple-element.14), channel_id=1, source_target_pairs={{0,8},{1,9},{2,10},{3,11},{12,4},{13,5},{14,6},{15,7},{16,24},{17,... | collective-permute-start | bytes 2359304 | tf_op jit(solution)/shard_map/ppermute | solution.py:176
  81.4 1.3 collective-permute-start.9
  82.8 2.6 %pad_add_fusion.10.row_ref = s32[4]{0:T(128)S(1)} fusion(s32[1]{0:T(128)} %bitcast.25, s32[1]{0:T(128)} %bitcast.24, s32[1]{0:T(128)} %bitcast.23, s32[1]{0:T(128)} %bitcast.22), kind=kLoop, calls=%fused_computation.73 | loop fusion | flops 12 | bytes 32 | tf_op jit(solution)/shard_map/stack | solution.py:60
  85.4 3.1 %collect.11 = bf16[4,12,128,128]{3,2,1,0:T(8,128)(2,1)} custom-call(s32[4]{0:T(128)S(1)} %broadcast_11_source_ref.2.source_ref, s32[4]{0:T(128)S(1)} %pad_add_fusion.10.row_ref, bf16[6,12,128,128]{3,2,1,0:T(8,128)(2,1)} %collective-permute-done.4.refs_0_.refs_1_), custom_call_target="tpu_custom_call" | custom-call | tf_op jit(solution)/shard_map/collect/pallas_call | solution.py:61
  88.5 1.3 collective-permute-start.5
  90.0 5.9 %fusion.14 = (s32[]{:T(128)}, s32[]{:T(128)}, s32[]{:T(128)}, s32[]{:T(128)}, s32[]{:T(128)}, /*index=5*/s32[]{:T(128)}, s32[]{:T(128)}, s32[]{:T(128)}) fusion(s32[6]{0:T(128)S(1)} %convert_reduce_fusion, s32[]{:T(128)} %bitcast.50, s32[]{:T(128)} %bitcast.46, s32[]{:T(128)} %bitcast.44, s32[]{:T(128)} %bitcast.40, s32[]{:T(128)} %bitcast.38, s32[]{:T(128)} %bitcast.34, ...), kind=kLoop, calls=%fused_computation.69 | loop fusion | flops 136 | bytes 88 | tf_op jit(solution)/shard_map/reduce_sum | solution.py:168
  100.8 0.7 collective-permute-start
  101.5 21.5 %collective-permute-done.8.refs_0_.refs_1_ = bf16[2,12,128,128]{3,2,1,0:T(8,128)(2,1)S(1)} collective-permute-done((bf16[2,12,128,128]{3,2,1,0:T(8,128)(2,1)}, bf16[2,12,128,128]{3,2,1,0:T(8,128)(2,1)S(1)}, u32[]{:S(2)}, u32[]{:S(2)}) %collective-permute-start.8) | collective-permute-done | bytes 786464 | tf_op jit(solution)/shard_map/ppermute | solution.py:176
  123.1 6.1 %collective-permute-start.10 = (bf16[2,12,128,128]{3,2,1,0:T(8,128)(2,1)}, bf16[2,12,128,128]{3,2,1,0:T(8,128)(2,1)}, u32[]{:S(2)}, u32[]{:S(2)}) collective-permute-start(bf16[2,12,128,128]{3,2,1,0:T(8,128)(2,1)} %copy-done.10), channel_id=1, source_target_pairs={{0,8},{1,9},{2,10},{3,11},{12,4},{13,5},{14,6},{15,7},{16,24},{17,... | collective-permute-start | bytes 2359304 | tf_op jit(solution)/shard_map/ppermute | solution.py:176
  129.2 1.8 collect.15
  131.1 1.3 collective-permute-start.12
  132.4 2.6 %collect.9 = bf16[2,12,128,128]{3,2,1,0:T(8,128)(2,1)} custom-call(s32[2]{0:T(128)S(1)} %broadcast_10_source_ref.2.source_ref, s32[2]{0:T(128)S(1)} %copy-done.8, bf16[4,12,128,128]{3,2,1,0:T(8,128)(2,1)} %collective-permute-done.1.refs_0_.refs_2_), custom_call_target="tpu_custom_call" | custom-call | tf_op jit(solution)/shard_map/collect/pallas_call | solution.py:61
  135.0 5.0 %collective-permute-done.9.refs_1_.refs_2_ = bf16[2,12,128,128]{3,2,1,0:T(8,128)(2,1)S(1)} collective-permute-done((bf16[2,12,128,128]{3,2,1,0:T(8,128)(2,1)}, bf16[2,12,128,128]{3,2,1,0:T(8,128)(2,1)S(1)}, u32[]{:S(2)}, u32[]{:S(2)}) %collective-permute-start.9) | collective-permute-done | bytes 786464 | tf_op jit(solution)/shard_map/ppermute | solution.py:176
  152.7 1.9 collect.14
  154.6 1.3 collective-permute-done.10.refs_2_.refs_3_
  156.0 1.3 collective-permute-start.11
  157.8 2.6 %collect.16 = bf16[2,12,128,128]{3,2,1,0:T(8,128)(2,1)} custom-call(s32[2]{0:T(128)S(1)} %get-tuple-element.75.source_ref, s32[2]{0:T(128)S(1)} %get-tuple-element.76.row_ref, bf16[2,12,128,128]{3,2,1,0:T(8,128)(2,1)S(1)} %collective-permute-done.8.refs_0_.refs_1_, bf16[2,12,128,128]{3,2,1,0:T(8,128)(2,1)S(1)} %collective-permute-done.9.refs_1_.refs_2_, ...), custom_call_target="tpu_custom_call" | custom-call | tf_op jit(solution)/shard_map/collect/pallas_call | solution.py:61
  160.4 0.7 collective-permute-start.13
  161.1 3.2 %collect.10 = bf16[4,12,128,128]{3,2,1,0:T(8,128)(2,1)} custom-call(s32[4]{0:T(128)S(1)} %iota.91.source_ref, s32[4]{0:T(128)S(1)} %broadcast_9_row_ref.2.row_ref, bf16[2,12,128,128]{3,2,1,0:T(8,128)(2,1)S(1)} %copy-done.4, bf16[2,12,128,128]{3,2,1,0:T(8,128)(2,1)} %collective-permute-done.refs_1_, ...), custom_call_target="tpu_custom_call" | custom-call | tf_op jit(solution)/shard_map/collect/pallas_call | solution.py:61
  164.4 1.8 collect.12
  166.2 1.5 collective-permute-start.6
  173.2 1.4 select_reduce_fusion
  176.2 1.0 collective-permute-done.11.refs_3_.refs_4_
  177.3 4.0 %collective-permute-done.13.refs_4_.refs_5_ = bf16[2,12,128,128]{3,2,1,0:T(8,128)(2,1)} collective-permute-done((bf16[2,12,128,128]{3,2,1,0:T(8,128)(2,1)}, bf16[2,12,128,128]{3,2,1,0:T(8,128)(2,1)}, u32[]{:S(2)}, u32[]{:S(2)}) %collective-permute-start.13) | collective-permute-done | bytes 786464 | tf_op jit(solution)/shard_map/ppermute | solution.py:207
  181.3 1.7 collect.17
  183.1 13.3 %collective-permute-done.6.refs_2_.refs_3_ = bf16[2,12,128,128]{3,2,1,0:T(8,128)(2,1)} collective-permute-done((bf16[2,12,128,128]{3,2,1,0:T(8,128)(2,1)}, bf16[2,12,128,128]{3,2,1,0:T(8,128)(2,1)}, u32[]{:S(2)}, u32[]{:S(2)}) %collective-permute-start.6) | collective-permute-done | bytes 786464 | tf_op jit(solution)/shard_map/ppermute | solution.py:199
  196.4 1.8 collect.13
  198.8 16.7 %blocks.3.refs_0_ = bf16[6,12,128,128]{3,2,1,0:T(8,128)(2,1)} custom-call(s32[72]{0:T(128)S(1)} %reshape.168.place_ref, s32[864]{0:T(1024)S(1)} %sub.55.slot_ref, s32[8]{0:T(128)S(1)} %copy-done.6, s32[8]{0:T(128)S(1)} %copy-done.7, bf16[6,12,128,128]{3,2,1,0:T(8,128)(2,1)} %tiles_ref.9, f32[6,1,128]{2,1,0:T(1,128)S(1)} %broadcast_in_dim.207.scale_row_ref, ...), custom_call_target="tpu_custom_call" | custom-call | tf_op jit(solution)/shard_map/blocks/pallas_call | solution.py:117
  215.5 10.5 %blocks.4.refs_0_ = bf16[6,12,128,128]{3,2,1,0:T(8,128)(2,1)S(1)} custom-call(s32[72]{0:T(128)S(1)} %reshape.167.place_ref, s32[864]{0:T(1024)S(1)} %sub.55.slot_ref, s32[4]{0:T(128)S(1)} %get-tuple-element.70.source_ref, s32[4]{0:T(128)S(1)} %get-tuple-element.60.row_ref, bf16[6,12,128,128]{3,2,1,0:T(8,128)(2,1)} %tiles_ref.9, ...), custom_call_target="tpu_custom_call" | custom-call | tf_op jit(solution)/shard_map/blocks/pallas_call | solution.py:117
  226.0 1.4 copy-done.2
  227.4 12.3 %blocks.5 = bf16[6,12,128,128]{3,2,1,0:T(8,128)(2,1)} custom-call(s32[72]{0:T(128)S(1)} %reshape.162.place_ref, s32[864]{0:T(1024)S(1)} %sub.55.slot_ref, s32[4]{0:T(128)S(1)} %pad_add_fusion.7.source_ref, s32[4]{0:T(128)S(1)} %get-tuple-element.61.row_ref, bf16[6,12,128,128]{3,2,1,0:T(8,128)(2,1)} %tiles_ref.9, ...), custom_call_target="tpu_custom_call" | custom-call | tf_op jit(solution)/shard_map/blocks/pallas_call | solution.py:117
  (81 shorter events, 5.1 us)
Async XLA Ops:
  0.0 85.3 %collective-permute-start.4 = (bf16[6,12,128,128]{3,2,1,0:T(8,128)(2,1)}, bf16[6,12,128,128]{3,2,1,0:T(8,128)(2,1)}, u32[]{:S(2)}, u32[]{:S(2)}) collective-permute-start(bf16[6,12,128,128]{3,2,1,0:T(8,128)(2,1)} %tiles_ref.9), channel_id=1, source_target_pairs={{4,8},{5,9},{6,10},{7,11},{8,4},{9,5},{10,6},{11,7},{20,24},{21,25... | collective-permute-start | bytes 7077896 | tf_op jit(solution)/shard_map/ppermute | solution.py:170
  5.1 54.4 %all-to-all-start = ((s32[16,1,896]{2,1,0:T(1,128)}), s32[16,1,896]{2,1,0:T(1,128)S(1)}, u32[]{:S(2)}, u32[]{:S(2)}) async-start(s32[16,1,896]{2,1,0:T(1,128)} %broadcast_in_dim.194), calls=%async_computation | async-start | bytes 114688 | tf_op jit(solution)/shard_map/all_to_all | solution.py:225
  65.3 1.7 copy-start
  66.9 7.4 %copy-start.1 = (bf16[6,12,128,128]{3,2,1,0:T(8,128)(2,1)S(1)}, bf16[6,12,128,128]{3,2,1,0:T(8,128)(2,1)}, u32[]{:S(2)}) copy-start(bf16[6,12,128,128]{3,2,1,0:T(8,128)(2,1)} %tiles_ref.9) | copy-start | bytes 7077892
  68.7 0.9 copy-start.3
  69.6 0.9 copy-start.9
  70.5 60.6 %collective-permute-start.1 = (bf16[4,12,128,128]{3,2,1,0:T(8,128)(2,1)}, bf16[4,12,128,128]{3,2,1,0:T(8,128)(2,1)}, u32[]{:S(2)}, u32[]{:S(2)}) collective-permute-start(bf16[4,12,128,128]{3,2,1,0:T(8,128)(2,1)} %get-tuple-element.13), channel_id=1, source_target_pairs={{0,4},{1,5},{2,6},{3,7},{4,0},{5,1},{6,2},{7,3},{8,12},{9,13},{10,... | collective-permute-start | bytes 4718600 | tf_op jit(solution)/shard_map/ppermute | solution.py:173
  76.2 0.9 copy-start.10
  77.0 46.0 %collective-permute-start.8 = (bf16[2,12,128,128]{3,2,1,0:T(8,128)(2,1)}, bf16[2,12,128,128]{3,2,1,0:T(8,128)(2,1)S(1)}, u32[]{:S(2)}, u32[]{:S(2)}) collective-permute-start(bf16[2,12,128,128]{3,2,1,0:T(8,128)(2,1)} %get-tuple-element.14), channel_id=1, source_target_pairs={{0,8},{1,9},{2,10},{3,11},{12,4},{13,5},{14,6},{15,7},{16,24},{17,... | collective-permute-start | bytes 2359304 | tf_op jit(solution)/shard_map/ppermute | solution.py:176
  81.4 58.5 %collective-permute-start.9 = (bf16[2,12,128,128]{3,2,1,0:T(8,128)(2,1)}, bf16[2,12,128,128]{3,2,1,0:T(8,128)(2,1)S(1)}, u32[]{:S(2)}, u32[]{:S(2)}) collective-permute-start(bf16[2,12,128,128]{3,2,1,0:T(8,128)(2,1)} %get-tuple-element.15), channel_id=1, source_target_pairs={{0,8},{1,9},{2,10},{3,11},{12,4},{13,5},{14,6},{15,7},{16,24},{17,... | collective-permute-start | bytes 2359304 | tf_op jit(solution)/shard_map/ppermute | solution.py:176
  85.3 4.4 %copy-start.11 = (s32[6,12]{1,0:T(8,128)S(1)}, s32[6,12]{1,0:T(8,128)}, u32[]{:S(2)}) copy-start(s32[6,12]{1,0:T(8,128)} %param.6) | copy-start | bytes 868
  85.4 4.4 %copy-start.12 = (s32[6]{0:T(128)S(1)}, s32[6]{0:T(128)}, u32[]{:S(2)}) copy-start(s32[6]{0:T(128)} %param.7) | copy-start | bytes 76
  88.5 43.9 %copy-start.8 = (s32[2]{0:T(128)S(1)}, s32[2]{0:T(128)}, u32[]{:S(2)}) copy-start(s32[2]{0:T(128)} %constant.208.clone.1.row_ref) | copy-start | bytes 28
  88.5 75.9 %collective-permute-start.5 = (bf16[4,12,128,128]{3,2,1,0:T(8,128)(2,1)}, bf16[4,12,128,128]{3,2,1,0:T(8,128)(2,1)S(1)}, u32[]{:S(2)}, u32[]{:S(2)}) collective-permute-start(bf16[4,12,128,128]{3,2,1,0:T(8,128)(2,1)} %collect.11), channel_id=1, source_target_pairs={{4,0},{5,1},{6,2},{7,3},{8,12},{9,13},{10,14},{11,15},{20,16},{21,... | collective-permute-start | bytes 4718600 | tf_op jit(solution)/shard_map/ppermute | solution.py:179
  100.8 60.3 %collective-permute-start = (bf16[2,12,128,128]{3,2,1,0:T(8,128)(2,1)}, bf16[2,12,128,128]{3,2,1,0:T(8,128)(2,1)}, u32[]{:S(2)}, u32[]{:S(2)}) collective-permute-start(bf16[2,12,128,128]{3,2,1,0:T(8,128)(2,1)} %copy-done.9), channel_id=1, source_target_pairs={{0,2},{1,3},{2,0},{3,1},{4,6},{5,7},{6,4},{7,5},{8,10},{9,11},{10,... | collective-permute-start | bytes 2359304 | tf_op jit(solution)/shard_map/ppermute | solution.py:174
  123.1 32.9 %collective-permute-start.10 = (bf16[2,12,128,128]{3,2,1,0:T(8,128)(2,1)}, bf16[2,12,128,128]{3,2,1,0:T(8,128)(2,1)}, u32[]{:S(2)}, u32[]{:S(2)}) collective-permute-start(bf16[2,12,128,128]{3,2,1,0:T(8,128)(2,1)} %copy-done.10), channel_id=1, source_target_pairs={{0,8},{1,9},{2,10},{3,11},{12,4},{13,5},{14,6},{15,7},{16,24},{17,... | collective-permute-start | bytes 2359304 | tf_op jit(solution)/shard_map/ppermute | solution.py:176
  131.1 26.7 %collective-permute-start.12 = (bf16[2,12,128,128]{3,2,1,0:T(8,128)(2,1)}, bf16[2,12,128,128]{3,2,1,0:T(8,128)(2,1)}, u32[]{:S(2)}, u32[]{:S(2)}) collective-permute-start(bf16[2,12,128,128]{3,2,1,0:T(8,128)(2,1)} %collect.15), channel_id=1, source_target_pairs={{4,0},{5,1},{6,2},{7,3},{8,12},{9,13},{10,14},{11,15},{20,16},{21,... | collective-permute-start | bytes 2359304 | tf_op jit(solution)/shard_map/ppermute | solution.py:187
  139.9 21.1 %collective-permute-start.2 = (bf16[2,12,128,128]{3,2,1,0:T(8,128)(2,1)}, bf16[2,12,128,128]{3,2,1,0:T(8,128)(2,1)}, u32[]{:S(2)}, u32[]{:S(2)}) collective-permute-start(bf16[2,12,128,128]{3,2,1,0:T(8,128)(2,1)} %collect.9), channel_id=1, source_target_pairs={{0,2},{1,3},{2,0},{3,1},{4,6},{5,7},{6,4},{7,5},{8,10},{9,11},{10,... | collective-permute-start | bytes 2359304 | tf_op jit(solution)/shard_map/ppermute | solution.py:180
  156.0 21.3 %collective-permute-start.11 = (bf16[2,12,128,128]{3,2,1,0:T(8,128)(2,1)}, bf16[2,12,128,128]{3,2,1,0:T(8,128)(2,1)}, u32[]{:S(2)}, u32[]{:S(2)}) collective-permute-start(bf16[2,12,128,128]{3,2,1,0:T(8,128)(2,1)} %collect.14), channel_id=1, source_target_pairs={{4,0},{5,1},{6,2},{7,3},{8,12},{9,13},{10,14},{11,15},{20,16},{21,... | collective-permute-start | bytes 2359304 | tf_op jit(solution)/shard_map/ppermute | solution.py:189
  157.8 3.3 %copy-start.4 = (bf16[2,12,128,128]{3,2,1,0:T(8,128)(2,1)S(1)}, bf16[2,12,128,128]{3,2,1,0:T(8,128)(2,1)}, u32[]{:S(2)}) copy-start(bf16[2,12,128,128]{3,2,1,0:T(8,128)(2,1)} %copy-done.3) | copy-start | bytes 2359300
  160.4 20.9 %collective-permute-start.13 = (bf16[2,12,128,128]{3,2,1,0:T(8,128)(2,1)}, bf16[2,12,128,128]{3,2,1,0:T(8,128)(2,1)}, u32[]{:S(2)}, u32[]{:S(2)}) collective-permute-start(bf16[2,12,128,128]{3,2,1,0:T(8,128)(2,1)} %collect.16), channel_id=1, source_target_pairs={{0,2},{1,3},{2,0},{3,1},{4,6},{5,7},{6,4},{7,5},{8,10},{9,11},{10,... | collective-permute-start | bytes 2359304 | tf_op jit(solution)/shard_map/ppermute | solution.py:207
  164.3 34.4 %collective-permute-start.3 = (bf16[4,12,128,128]{3,2,1,0:T(8,128)(2,1)}, bf16[4,12,128,128]{3,2,1,0:T(8,128)(2,1)}, u32[]{:S(2)}, u32[]{:S(2)}) collective-permute-start(bf16[4,12,128,128]{3,2,1,0:T(8,128)(2,1)} %collect.10), channel_id=1, source_target_pairs={{0,1},{1,0},{2,3},{3,2},{4,5},{5,4},{6,7},{7,6},{8,9},{9,8},{10,11... | collective-permute-start | bytes 4718600 | tf_op jit(solution)/shard_map/ppermute | solution.py:191
  166.2 30.1 %collective-permute-start.6 = (bf16[2,12,128,128]{3,2,1,0:T(8,128)(2,1)}, bf16[2,12,128,128]{3,2,1,0:T(8,128)(2,1)}, u32[]{:S(2)}, u32[]{:S(2)}) collective-permute-start(bf16[2,12,128,128]{3,2,1,0:T(8,128)(2,1)} %collect.12), channel_id=1, source_target_pairs={{0,2},{1,3},{2,0},{3,1},{4,6},{5,7},{6,4},{7,5},{8,10},{9,11},{10,... | collective-permute-start | bytes 2359304 | tf_op jit(solution)/shard_map/ppermute | solution.py:199
  183.0 44.4 %collective-permute-start.14 = (bf16[2,12,128,128]{3,2,1,0:T(8,128)(2,1)S(1)}, bf16[2,12,128,128]{3,2,1,0:T(8,128)(2,1)S(1)}, u32[]{:S(2)}, u32[]{:S(2)}) collective-permute-start(bf16[2,12,128,128]{3,2,1,0:T(8,128)(2,1)S(1)} %collect.17), channel_id=1, source_target_pairs={{0,1},{1,0},{2,3},{3,2},{4,5},{5,4},{6,7},{7,6},{8,9},{9,8},{10,11... | collective-permute-start | bytes 2359304 | tf_op jit(solution)/shard_map/ppermute | solution.py:208
  196.4 2.4 copy-start.5
  196.4 2.4 copy-start.6
  196.4 2.4 copy-start.7
  198.1 17.3 %collective-permute-start.7 = (bf16[2,12,128,128]{3,2,1,0:T(8,128)(2,1)S(1)}, bf16[2,12,128,128]{3,2,1,0:T(8,128)(2,1)S(1)}, u32[]{:S(2)}, u32[]{:S(2)}) collective-permute-start(bf16[2,12,128,128]{3,2,1,0:T(8,128)(2,1)S(1)} %collect.13), channel_id=1, source_target_pairs={{0,1},{1,0},{2,3},{3,2},{4,5},{5,4},{6,7},{7,6},{8,9},{9,8},{10,11... | collective-permute-start | bytes 2359304 | tf_op jit(solution)/shard_map/ppermute | solution.py:200
  226.0 1.4 copy-start.2

commit v4 on v1

v4 whole, which is shorter than its diff:
```python
import functools

import jax
import jax.numpy as jnp
from jax import lax
from jax.experimental import pallas as pl
from jax.experimental.pallas import tpu as pltpu
from jax.sharding import PartitionSpec as P

VMEM_LIMIT = 48 * 1024 * 1024
SMEM = pl.BlockSpec(memory_space=pltpu.SMEM)
VMEM = pl.BlockSpec(memory_space=pltpu.VMEM)
HBM = pl.BlockSpec(memory_space=pl.ANY)
PARAMS = pltpu.CompilerParams(vmem_limit_bytes=VMEM_LIMIT)


def pick_rows_kernel(sizes, rows_ref, tiles_ref, *refs):
    outs, sems = refs[:-1], refs[-1]
    places = [(ref, k) for ref, size in zip(outs, sizes) for k in range(size)]
    for at, (ref, k) in enumerate(places):
        pltpu.make_async_copy(tiles_ref.at[rows_ref[at]], ref.at[k], sems.at[at]).start()
    for at, (ref, k) in enumerate(places):
        pltpu.make_async_copy(tiles_ref.at[0], ref.at[k], sems.at[at]).wait()


def pick_rows(rows, tiles, sizes):
    return pl.pallas_call(
        functools.partial(pick_rows_kernel, sizes),
        out_shape=[jax.ShapeDtypeStruct((size,) + tiles.shape[1:], tiles.dtype) for size in sizes],
        in_specs=[SMEM, VMEM],
        out_specs=[HBM] * len(sizes),
        scratch_shapes=[pltpu.SemaphoreType.DMA((sum(sizes),))],
        compiler_params=PARAMS,
        name="pick_rows",
    )(rows, tiles)


def fetch_rows(total, source_ref, row_ref, sources, target_ref, sems):
    for k in range(total):
        for at, ref in enumerate(sources):

            last = at == len(sources) - 1

            @pl.when(source_ref[k] >= at if last else source_ref[k] == at)
            def _():
                pltpu.make_async_copy(ref.at[row_ref[k]], target_ref.at[k], sems.at[k]).start()

    for k in range(total):
        pltpu.make_async_copy(sources[0].at[0], target_ref.at[k], sems.at[k]).wait()


def collect_kernel(total, source_ref, row_ref, *refs):
    sources, outs, sems = refs[: -1 - total], refs[-1 - total : -1], refs[-1]
    for at, ref in enumerate(sources):

        @pl.when(source_ref[0] == at)
        def _():
            for k in range(total):
                pltpu.make_async_copy(ref.at[row_ref[k]], outs[k].at[0], sems.at[k]).start()

    for k in range(total):
        pltpu.make_async_copy(sources[0].at[0], outs[k].at[0], sems.at[k]).wait()


def collect_each(source, rows, *sources):
    total = rows.shape[0]
    return pl.pallas_call(
        functools.partial(collect_kernel, total),
        out_shape=[jax.ShapeDtypeStruct((1,) + sources[0].shape[1:], sources[0].dtype)] * total,
        in_specs=[SMEM, SMEM] + [HBM] * len(sources),
        out_specs=[VMEM] * total,
        scratch_shapes=[pltpu.SemaphoreType.DMA((total,))],
        compiler_params=PARAMS,
        name="collect",
    )(source[None], rows, *sources)


def blocks_kernel(total, owner_ref, slot_ref, source_ref, row_ref, tiles_ref, scale_row_ref, scale_got_ref, *refs):
    *sources, out_ref, fetched_ref, sems = refs
    local_rows, slots, side, _ = tiles_ref.shape
    cands = out_ref.shape[1]
    together = 2 if cands % 2 == 0 else 1
    fetch_rows(total, source_ref, row_ref, sources, fetched_ref, sems)

    def one_row(i, carry):
        left = jnp.concatenate([tiles_ref[i, r] for r in range(slots)], axis=1)
        scale_x = jnp.broadcast_to(scale_row_ref[i], (side, side)).T

        def some_blocks(step, inner):
            right = []
            for k in range(together):
                block = i * cands + step * together + k
                owner = owner_ref[block]
                picked = []
                for r in range(slots):
                    s = slot_ref[block * slots + r]
                    tile = fetched_ref[owner, jnp.maximum(s, 0)]
                    picked.append(jnp.where(s >= 0, tile, jnp.zeros_like(tile)))
                right.append(jnp.concatenate(picked, axis=1))
            right = jnp.concatenate(right, axis=0)
            shared = lax.dot_general(left, right, (((1,), (1,)), ((), ())), preferred_element_type=jnp.float32)
            for k in range(together):
                q = step * together + k
                scale = scale_x * scale_got_ref[owner_ref[i * cands + q]]
                out_ref[i, q] = (shared[:, k * side : (k + 1) * side] * scale).astype(out_ref.dtype)
            return inner

        return lax.fori_loop(0, cands // together, some_blocks, carry)

    lax.fori_loop(0, local_rows, one_row, 0)


def blocks(owners, slot_of, source_ids, row_ids, tiles, scale_row, scale_got, sources):
    local_rows, slots, side, _ = tiles.shape
    total = source_ids.shape[0]
    return pl.pallas_call(
        functools.partial(blocks_kernel, total),
        out_shape=jax.ShapeDtypeStruct((local_rows, owners.shape[1], side, side), jnp.bfloat16),
        in_specs=[SMEM] * 4 + [VMEM] * 3 + [HBM] * len(sources),
        out_specs=VMEM,
        scratch_shapes=[
            pltpu.VMEM((total,) + tiles.shape[1:], tiles.dtype),
            pltpu.SemaphoreType.DMA((total,)),
        ],
        compiler_params=PARAMS,
        name="blocks",
    )(
        owners.reshape(-1), slot_of.reshape(-1), source_ids, row_ids, tiles, scale_row[:, None, :], scale_got[:, None, :],
        *sources,
    )


def exchange_direct(wanted_by, me, tiles):
    asked = lax.dynamic_index_in_dim(wanted_by, me, axis=1, keepdims=False)
    (send,) = pick_rows(asked, tiles, (asked.shape[0],))
    return lax.all_to_all(send, "col", split_axis=0, concat_axis=0, tiled=True)


def moves(targets, flip=0):
    return [(4 * z + p, 4 * t + (p ^ flip)) for z, t in enumerate(targets) if t is not None for p in range(4)]


HALVES = [list(range(8)), list(range(8, 16))]


def relay(wanted_by, me, tiles, middle):
    plane, mate = me // 4, me % 4
    inner = (plane == 1) | (plane == 2)
    flips = jnp.arange(4, dtype=jnp.int32)
    peer_ids = jnp.arange(16, dtype=jnp.int32)

    def lookup(readers, owner):
        of_owner = jnp.sum(jnp.where(peer_ids == owner, wanted_by, 0), axis=1)
        return jnp.sum(jnp.where(readers[:, None] == peer_ids, of_owner, 0), axis=1)

    half = me // 8 * 8 + jnp.arange(8, dtype=jnp.int32)
    beyond = 4 * (plane ^ 3) + (mate ^ flips)
    half_send, first_send = pick_rows(lookup(jnp.concatenate([half, beyond[:1]]), me), tiles, (8, 1))
    near = lax.all_to_all(half_send, "col", split_axis=0, concat_axis=0, axis_index_groups=HALVES, tiled=True)
    beyond_got = [lax.ppermute(first_send, "col", moves([3, None, None, 0]))]

    readers = jnp.concatenate(
        [jnp.where(inner, 4 * plane, 4 * (plane ^ 3)) + (mate ^ flips[1:]),
         jnp.where(inner, 4 * (plane ^ 1), 4 * (plane ^ 2)) + (mate ^ flips)]
    )
    rows = lookup(readers, jnp.where(inner, 4 * (plane ^ 3) + mate, me))
    sends = collect_each(jnp.where(inner, 1, 0), rows, tiles, middle)
    beyond_got += [lax.ppermute(sends[m - 1], "col", moves([3, 1, 2, 0], m)) for m in (1, 2, 3)]
    across_got = [lax.ppermute(sends[m + 3], "col", moves([2, 0, 3, 1], m)) for m in range(4)]

    mine_in_middle = lookup(me[None], 4 * (plane ^ 3) + mate)[0]
    owner_plane, flip = peer_ids // 4, mate ^ (peer_ids % 4)
    is_near, is_beyond = owner_plane // 2 == plane // 2, owner_plane == plane ^ 3
    is_middle = is_beyond & inner & (flip == 0)
    source_ids = jnp.where(is_near, 0, jnp.where(is_middle, 1, jnp.where(is_beyond, 2, 6) + flip))
    row_ids = jnp.where(is_near, peer_ids % 8, jnp.where(is_middle, mine_in_middle, 0))
    return source_ids, row_ids, [near, middle, *beyond_got, *across_got]


def local(tiles, tile_cols, tile_count, candidates, degree):
    local_rows, slots, side, _ = tiles.shape
    peers = lax.axis_size("col")
    me = lax.axis_index("col")
    owners = candidates // local_rows
    peer_ids = jnp.arange(peers, dtype=jnp.int32)
    row_ids = jnp.arange(local_rows, dtype=jnp.int32)

    matches = owners[:, :, None] == peer_ids
    wanted = jnp.max(jnp.where(matches, (candidates % local_rows)[:, :, None], 0), axis=(0, 1))

    note = jnp.concatenate([wanted, tile_count, tile_cols.reshape(-1), degree.reshape(-1)])
    note = jnp.pad(note, (0, -note.shape[0] % 128))
    note = jnp.broadcast_to(note, (peers, note.shape[0]))
    relayed = peers == 16
    if relayed:
        tiles_behind, note = lax.optimization_barrier((tiles, note))
    notes = lax.all_to_all(note, "col", split_axis=0, concat_axis=0, tiled=True)
    if relayed:
        middle = lax.ppermute(tiles_behind, "col", moves([None, 2, 1, None]))
    wanted_by = notes[:, :peers]
    at = peers
    counts_all = notes[:, at : at + local_rows]
    at += local_rows
    cols_all = notes[:, at : at + local_rows * slots].reshape(peers, local_rows, slots)
    at += local_rows * slots
    degree_all = notes[:, at : at + local_rows * side].reshape(peers, local_rows, side)

    mine = wanted[:, None] == row_ids
    count_got = jnp.sum(jnp.where(mine, counts_all, 0), axis=1)
    cols_got = jnp.sum(jnp.where(mine[:, :, None], cols_all, 0), axis=1)
    degree_got = jnp.sum(jnp.where(mine[:, :, None], degree_all, 0), axis=1)
    slot_ids = jnp.arange(slots, dtype=jnp.int32)
    cols_got = jnp.where(slot_ids < count_got[:, None], cols_got, -1)
    cols_other = jnp.sum(jnp.where(matches[..., None], cols_got, 0), axis=2)
    cols_mine = jnp.where(slot_ids < tile_count[:, None], tile_cols, -2)
    meets = cols_mine[:, None, :, None] == cols_other[:, :, None, :]
    slot_of = jnp.sum(jnp.where(meets, slot_ids + 1, 0), axis=3) - 1

    scale_row = lax.rsqrt(degree.astype(jnp.float32))
    scale_other = lax.rsqrt(degree_got.astype(jnp.float32))

    if relayed:
        source_ids, row_ids, sources = relay(wanted_by, me, tiles, middle)
    else:
        sources = [exchange_direct(wanted_by, me, tiles)]
        source_ids, row_ids = jnp.zeros_like(peer_ids), peer_ids
    return blocks(owners, slot_of, source_ids, row_ids, tiles, scale_row, scale_other, sources)


def solution(mesh):
    in_specs = (
        P(("slab", "col"), None, None, None),
        P(("slab", "col"), None),
        P(("slab", "col")),
        P(("slab", "col"), None),
        P(("slab", "col"), None),
    )
    out_specs = P(("slab", "col"), None, None, None)
    return jax.shard_map(local, mesh=mesh, in_specs=in_specs, out_specs=out_specs, check_vma=False)
```

time: 371 us -> 187 us (0.50)
  the two profiles are of different devices: /device:TPU:13 before, /device:TPU:0 now
where the time goes in v4:
time: 187 us; the launch traced here: 186 us
  starting transfers between devices  110 us (59%)
  waiting for transfers between devices  30.2 us (16%)
  Pallas kernels  26.3 us (14%)
  local copies, waits for them, and re-layouts  10.5 us (6%)
  other arithmetic  9.01 us (5%)
    ppermute x4, starting transfers between devices, relay(): lax.ppermute(sends[m + 3], 'col', moves([2, 0, 3, 1], m))  85.7 us
    ppermute x4, waiting for transfers between devices, relay(): lax.ppermute(sends[m + 3], 'col', moves([2, 0, 3, 1], m))  23.6 us
    pallas_call x1, Pallas kernels, blocks(): pl.pallas_call(functools.partial(blocks_kernel, total), out_shape=jax.Sha...  20.2 us
    all_to_all x1, starting transfers between devices, local(): notes = lax.all_to_all(note, 'col', split_axis=0, concat_axis=0, tiled=True)  7.39 us
    all_to_all x1, waiting for transfers between devices, local(): notes = lax.all_to_all(note, 'col', split_axis=0, concat_axis=0, tiled=True)  6.6 us
    ppermute x3, starting transfers between devices, relay(): lax.ppermute(sends[m - 1], 'col', moves([3, 1, 2, 0], m))  6.48 us
    unnamed x27, local copies, waits for them, and re-layouts  5.25 us
    all_to_all x1, starting transfers between devices, relay(): lax.all_to_all(half_send, 'col', split_axis=0, concat_axis=0, axis_index_...  4.58 us
  transfers between devices with their start and end apart: 11, of which 4 were waited for; matrix products, arithmetic and copies ran while one was open for 6% of the time, Pallas kernels for 2%

profile of v4, /device:TPU:0, one launch (start us, length us, event | category | flops | bytes accessed | tf_op | source)
XLA Modules:
  0.0 186.2 jit_solution(11800508635705388168)
XLA Ops:
  0.0 0.7 add_select_fusion
  0.7 0.8 reshape.75
  1.5 0.1 select_reduce_fusion.4
  1.6 0.8 pad_add_fusion
  2.4 0.7 all_to_all.11
  3.0 7.4 %all-to-all-start = ((s32[16,1,896]{2,1,0:T(1,128)}), s32[16,1,896]{2,1,0:T(1,128)S(1)}, u32[]{:S(2)}, u32[]{:S(2)}) async-start(s32[16,1,896]{2,1,0:T(1,128)} %all_to_all.11), calls=%async_computation | async-start | bytes 114688 | tf_op jit(solution)/shard_map/all_to_all | solution.py:197
  10.5 0.1 pad_add_fusion.1
  10.6 6.6 %all-to-all-done = s32[16,1,896]{2,1,0:T(1,128)S(1)} async-done(((s32[16,1,896]{2,1,0:T(1,128)}), s32[16,1,896]{2,1,0:T(1,128)S(1)}, u32[]{:S(2)}, u32[]{:S(2)}) %all-to-all-start) | async-done | bytes 57376 | tf_op jit(solution)/shard_map/all_to_all | solution.py:197
  17.3 0.7 select_reduce_fusion.5
  17.9 0.2 select_reduce_fusion.6.rows_ref
  18.1 1.7 copy-done
  19.8 2.9 %pick_rows.1 = (bf16[8,12,128,128]{3,2,1,0:T(8,128)(2,1)S(1)}, bf16[1,12,128,128]{3,2,1,0:T(8,128)(2,1)}) custom-call(s32[9]{0:T(128)S(1)} %select_reduce_fusion.6.rows_ref, bf16[6,12,128,128]{3,2,1,0:T(8,128)(2,1)S(1)} %copy-done), custom_call_target="tpu_custom_call" | custom-call | tf_op jit(solution)/shard_map/pick_rows/pallas_call | solution.py:27
  22.7 1.7 copy-done.2
  24.4 4.6 %all-to-all-start.1 = ((bf16[8,12,128,128]{3,2,1,0:T(8,128)(2,1)}), bf16[8,12,128,128]{3,2,1,0:T(8,128)(2,1)}, u32[]{:S(2)}, u32[]{:S(2)}) async-start(bf16[8,12,128,128]{3,2,1,0:T(8,128)(2,1)} %copy-done.2), calls=%async_computation.1 | async-start | bytes 6291456 | tf_op jit(solution)/shard_map/all_to_all | solution.py:159
  29.0 2.1 %collective-permute-start = (bf16[6,12,128,128]{3,2,1,0:T(8,128)(2,1)S(1)}, bf16[6,12,128,128]{3,2,1,0:T(8,128)(2,1)}, u32[]{:S(2)}, u32[]{:S(2)}) collective-permute-start(bf16[6,12,128,128]{3,2,1,0:T(8,128)(2,1)S(1)} %copy-done.1), channel_id=1, source_target_pairs={{4,8},{5,9},{6,10},{7,11},{8,4},{9,5},{10,6},{11,7},{20,24},{21,25... | collective-permute-start | bytes 7077896 | tf_op jit(solution)/shard_map/ppermute | solution.py:199
  31.1 0.7 reshape.74.owner_ref
  31.8 0.5 iota_add_fusion.1
  32.3 0.1 xor_add_fusion
  32.4 0.1 pad_add_fusion.2
  32.6 0.1 iota_compare_fusion
  32.8 0.1 reshape.77
  32.8 3.5 %collective-permute-start.1 = (bf16[1,12,128,128]{3,2,1,0:T(8,128)(2,1)}, bf16[1,12,128,128]{3,2,1,0:T(8,128)(2,1)S(1)}, u32[]{:S(2)}, u32[]{:S(2)}) collective-permute-start(bf16[1,12,128,128]{3,2,1,0:T(8,128)(2,1)} %get-tuple-element.19), channel_id=1, source_target_pairs={{0,12},{1,13},{2,14},{3,15},{12,0},{13,1},{14,2},{15,3},{16,28},{1... | collective-permute-start | bytes 1179656 | tf_op jit(solution)/shard_map/ppermute | solution.py:160
  36.3 0.2 select_reduce_fusion.9.row_ref
  36.5 0.2 fusion
  36.7 0.1 select_reduce_fusion.3
  36.9 0.3 select_reduce_fusion.1
  37.2 3.3 %collect.1 = (bf16[1,12,128,128]{3,2,1,0:T(8,128)(2,1)S(1)}, bf16[1,12,128,128]{3,2,1,0:T(8,128)(2,1)S(1)}, bf16[1,12,128,128]{3,2,1,0:T(8,128)(2,1)}, bf16[1,12...) custom-call(s32[1]{0:T(128)} %bitcast.2.source_ref, ...), custom_call_target="tpu_custom_call" | custom-call | tf_op jit(solution)/shard_map/collect/pallas_call | solution.py:67
  40.5 2.0 %collective-permute-start.2 = (bf16[1,12,128,128]{3,2,1,0:T(8,128)(2,1)S(1)}, bf16[1,12,128,128]{3,2,1,0:T(8,128)(2,1)S(1)}, u32[]{:S(2)}, u32[]{:S(2)}) collective-permute-start(bf16[1,12,128,128]{3,2,1,0:T(8,128)(2,1)S(1)} %get-tuple-element.20), channel_id=1, source_target_pairs={{0,13},{1,12},{2,15},{3,14},{4,5},{5,4},{6,7},{7,6},{8,9},{9,8},{1... | collective-permute-start | bytes 1179656 | tf_op jit(solution)/shard_map/ppermute | solution.py:168
  42.4 2.3 %collective-permute-start.3 = (bf16[1,12,128,128]{3,2,1,0:T(8,128)(2,1)S(1)}, bf16[1,12,128,128]{3,2,1,0:T(8,128)(2,1)S(1)}, u32[]{:S(2)}, u32[]{:S(2)}) collective-permute-start(bf16[1,12,128,128]{3,2,1,0:T(8,128)(2,1)S(1)} %get-tuple-element.21), channel_id=1, source_target_pairs={{0,14},{1,15},{2,12},{3,13},{4,6},{5,7},{6,4},{7,5},{8,10},{9,11},... | collective-permute-start | bytes 1179656 | tf_op jit(solution)/shard_map/ppermute | solution.py:168
  44.7 0.7 fusion.7
  45.4 1.4 select_reduce_fusion
  46.8 0.6 broadcast_add_fusion
  47.4 2.2 %collective-permute-start.4 = (bf16[1,12,128,128]{3,2,1,0:T(8,128)(2,1)}, bf16[1,12,128,128]{3,2,1,0:T(8,128)(2,1)}, u32[]{:S(2)}, u32[]{:S(2)}) collective-permute-start(bf16[1,12,128,128]{3,2,1,0:T(8,128)(2,1)} %get-tuple-element.22), channel_id=1, source_target_pairs={{0,15},{1,14},{2,13},{3,12},{4,7},{5,6},{6,5},{7,4},{8,11},{9,10},... | collective-permute-start | bytes 1179656 | tf_op jit(solution)/shard_map/ppermute | solution.py:168
  49.6 78.3 %collective-permute-start.5 = (bf16[1,12,128,128]{3,2,1,0:T(8,128)(2,1)}, bf16[1,12,128,128]{3,2,1,0:T(8,128)(2,1)}, u32[]{:S(2)}, u32[]{:S(2)}) collective-permute-start(bf16[1,12,128,128]{3,2,1,0:T(8,128)(2,1)} %get-tuple-element.23), channel_id=1, source_target_pairs={{0,8},{1,9},{2,10},{3,11},{4,0},{5,1},{6,2},{7,3},{8,12},{9,13},{1... | collective-permute-start | bytes 1179656 | tf_op jit(solution)/shard_map/ppermute | solution.py:169
  127.9 3.9 %collective-permute-start.7 = (bf16[1,12,128,128]{3,2,1,0:T(8,128)(2,1)}, bf16[1,12,128,128]{3,2,1,0:T(8,128)(2,1)}, u32[]{:S(2)}, u32[]{:S(2)}) collective-permute-start(bf16[1,12,128,128]{3,2,1,0:T(8,128)(2,1)} %get-tuple-element.25), channel_id=1, source_target_pairs={{0,10},{1,11},{2,8},{3,9},{4,2},{5,3},{6,0},{7,1},{8,14},{9,15},{1... | collective-permute-start | bytes 1179656 | tf_op jit(solution)/shard_map/ppermute | solution.py:169
  131.8 3.6 %collective-permute-start.8 = (bf16[1,12,128,128]{3,2,1,0:T(8,128)(2,1)}, bf16[1,12,128,128]{3,2,1,0:T(8,128)(2,1)}, u32[]{:S(2)}, u32[]{:S(2)}) collective-permute-start(bf16[1,12,128,128]{3,2,1,0:T(8,128)(2,1)} %get-tuple-element.26), channel_id=1, source_target_pairs={{0,11},{1,10},{2,9},{3,8},{4,3},{5,2},{6,1},{7,0},{8,15},{9,14},{1... | collective-permute-start | bytes 1179656 | tf_op jit(solution)/shard_map/ppermute | solution.py:169
  135.3 1.2 compare_select_fusion.5
  136.5 0.7 slice.27
  137.2 0.9 sub.33.slot_ref
  138.1 1.4 reshape.78
  139.5 0.9 select_reduce_fusion.2
  140.5 5.7 %collective-permute-done.6.refs_7_ = bf16[1,12,128,128]{3,2,1,0:T(8,128)(2,1)} collective-permute-done((bf16[1,12,128,128]{3,2,1,0:T(8,128)(2,1)}, bf16[1,12,128,128]{3,2,1,0:T(8,128)(2,1)}, u32[]{:S(2)}, u32[]{:S(2)}) %collective-permute-start.6) | collective-permute-done | bytes 393248 | tf_op jit(solution)/shard_map/ppermute | solution.py:169
  146.3 9.9 %collective-permute-done.7.refs_8_ = bf16[1,12,128,128]{3,2,1,0:T(8,128)(2,1)} collective-permute-done((bf16[1,12,128,128]{3,2,1,0:T(8,128)(2,1)}, bf16[1,12,128,128]{3,2,1,0:T(8,128)(2,1)}, u32[]{:S(2)}, u32[]{:S(2)}) %collective-permute-start.7) | collective-permute-done | bytes 393248 | tf_op jit(solution)/shard_map/ppermute | solution.py:169
  156.2 7.9 %collective-permute-done.8.refs_9_ = bf16[1,12,128,128]{3,2,1,0:T(8,128)(2,1)} collective-permute-done((bf16[1,12,128,128]{3,2,1,0:T(8,128)(2,1)}, bf16[1,12,128,128]{3,2,1,0:T(8,128)(2,1)}, u32[]{:S(2)}, u32[]{:S(2)}) %collective-permute-start.8) | collective-permute-done | bytes 393248 | tf_op jit(solution)/shard_map/ppermute | solution.py:169
  164.1 0.7 copy-done.3
  164.8 0.6 copy-done.4
  165.4 0.6 copy-done.5
  166.0 20.2 %blocks.1 = bf16[6,12,128,128]{3,2,1,0:T(8,128)(2,1)} custom-call(s32[72]{0:T(128)S(1)} %copy-done.3, s32[864]{0:T(1024)S(1)} %sub.33.slot_ref, s32[16]{0:T(128)S(1)} %copy-done.5, s32[16]{0:T(128)S(1)} %copy-done.4, bf16[6,12,128,128]{3,2,1,0:T(8,128)(2,1)S(1)} %copy-done.1, f32[6,1,128]{2,1,0:T(1,128)S(1)} %broadcast_in_dim.169.scale_row_ref, ...), custom_call_target="tpu_custom_call" | custom-call | tf_op jit(solution)/shard_map/blocks/pallas_call | solution.py:116
  (46 shorter events, 0.4 us)
Async XLA Ops:
  3.0 14.2 %all-to-all-start = ((s32[16,1,896]{2,1,0:T(1,128)}), s32[16,1,896]{2,1,0:T(1,128)S(1)}, u32[]{:S(2)}, u32[]{:S(2)}) async-start(s32[16,1,896]{2,1,0:T(1,128)} %all_to_all.11), calls=%async_computation | async-start | bytes 114688 | tf_op jit(solution)/shard_map/all_to_all | solution.py:197
  17.3 19.3 %copy-start.6 = (s32[16,1,896]{2,0,1:T(8,128)}, s32[16,1,896]{2,0,1:T(8,128)S(1)}, u32[]{:S(2)}) copy-start(s32[16,1,896]{2,0,1:T(8,128)S(1)} %copy.8) | copy-start | bytes 172036
  18.1 1.7 copy-start
  22.7 1.7 copy-start.2
  24.4 4.6 %copy-start.1 = (bf16[6,12,128,128]{3,2,1,0:T(8,128)(2,1)S(1)}, bf16[6,12,128,128]{3,2,1,0:T(8,128)(2,1)}, u32[]{:S(2)}) copy-start(bf16[6,12,128,128]{3,2,1,0:T(8,128)(2,1)} %tiles_ref.3) | copy-start | bytes 7077892
  24.4 7.4 %copy-start.8 = (s32[6,128]{1,0:T(8,128)S(1)}, s32[6,128]{1,0:T(8,128)}, u32[]{:S(2)}) copy-start(s32[6,128]{1,0:T(8,128)} %param.9) | copy-start | bytes 9220
  24.4 8.2 %copy-start.9 = (s32[6,12]{1,0:T(8,128)S(1)}, s32[6,12]{1,0:T(8,128)}, u32[]{:S(2)}) copy-start(s32[6,12]{1,0:T(8,128)} %param.6) | copy-start | bytes 868
  24.4 8.2 %copy-start.10 = (s32[6]{0:T(128)S(1)}, s32[6]{0:T(128)}, u32[]{:S(2)}) copy-start(s32[6]{0:T(128)} %param.7) | copy-start | bytes 76
  24.4 139.7 %all-to-all-start.1 = ((bf16[8,12,128,128]{3,2,1,0:T(8,128)(2,1)}), bf16[8,12,128,128]{3,2,1,0:T(8,128)(2,1)}, u32[]{:S(2)}, u32[]{:S(2)}) async-start(bf16[8,12,128,128]{3,2,1,0:T(8,128)(2,1)} %copy-done.2), calls=%async_computation.1 | async-start | bytes 6291456 | tf_op jit(solution)/shard_map/all_to_all | solution.py:159
  29.0 8.2 %collective-permute-start = (bf16[6,12,128,128]{3,2,1,0:T(8,128)(2,1)S(1)}, bf16[6,12,128,128]{3,2,1,0:T(8,128)(2,1)}, u32[]{:S(2)}, u32[]{:S(2)}) collective-permute-start(bf16[6,12,128,128]{3,2,1,0:T(8,128)(2,1)S(1)} %copy-done.1), channel_id=1, source_target_pairs={{4,8},{5,9},{6,10},{7,11},{8,4},{9,5},{10,6},{11,7},{20,24},{21,25... | collective-permute-start | bytes 7077896 | tf_op jit(solution)/shard_map/ppermute | solution.py:199
  32.8 95.0 %collective-permute-start.1 = (bf16[1,12,128,128]{3,2,1,0:T(8,128)(2,1)}, bf16[1,12,128,128]{3,2,1,0:T(8,128)(2,1)S(1)}, u32[]{:S(2)}, u32[]{:S(2)}) collective-permute-start(bf16[1,12,128,128]{3,2,1,0:T(8,128)(2,1)} %get-tuple-element.19), channel_id=1, source_target_pairs={{0,12},{1,13},{2,14},{3,15},{12,0},{13,1},{14,2},{15,3},{16,28},{1... | collective-permute-start | bytes 1179656 | tf_op jit(solution)/shard_map/ppermute | solution.py:160
  37.2 7.6 %copy-start.12 = (s32[16]{0:T(128)S(1)}, s32[16]{0:T(128)}, u32[]{:S(2)}) copy-start(s32[16]{0:T(128)} %get-tuple-element.29) | copy-start | bytes 196
  37.2 8.2 %copy-start.11 = (s32[12]{0:T(128)S(1)}, s32[12]{0:T(128)}, u32[]{:S(2)}) copy-start(s32[12]{0:T(128)} %iota_add_fusion.1) | copy-start | bytes 148
  37.2 99.3 %copy-start.7 = (s32[16,1,896]{2,0,1:T(8,128)S(1)}, s32[16,1,896]{2,0,1:T(8,128)}, u32[]{:S(2)}) copy-start(s32[16,1,896]{2,0,1:T(8,128)} %copy-done.6) | copy-start | bytes 172036
  40.5 87.4 %collective-permute-start.2 = (bf16[1,12,128,128]{3,2,1,0:T(8,128)(2,1)S(1)}, bf16[1,12,128,128]{3,2,1,0:T(8,128)(2,1)S(1)}, u32[]{:S(2)}, u32[]{:S(2)}) collective-permute-start(bf16[1,12,128,128]{3,2,1,0:T(8,128)(2,1)S(1)} %get-tuple-element.20), channel_id=1, source_target_pairs={{0,13},{1,12},{2,15},{3,14},{4,5},{5,4},{6,7},{7,6},{8,9},{9,8},{1... | collective-permute-start | bytes 1179656 | tf_op jit(solution)/shard_map/ppermute | solution.py:168
  42.4 89.3 %collective-permute-start.3 = (bf16[1,12,128,128]{3,2,1,0:T(8,128)(2,1)S(1)}, bf16[1,12,128,128]{3,2,1,0:T(8,128)(2,1)S(1)}, u32[]{:S(2)}, u32[]{:S(2)}) collective-permute-start(bf16[1,12,128,128]{3,2,1,0:T(8,128)(2,1)S(1)} %get-tuple-element.21), channel_id=1, source_target_pairs={{0,14},{1,15},{2,12},{3,13},{4,6},{5,7},{6,4},{7,5},{8,10},{9,11},... | collective-permute-start | bytes 1179656 | tf_op jit(solution)/shard_map/ppermute | solution.py:168
  47.4 93.1 %collective-permute-start.4 = (bf16[1,12,128,128]{3,2,1,0:T(8,128)(2,1)}, bf16[1,12,128,128]{3,2,1,0:T(8,128)(2,1)}, u32[]{:S(2)}, u32[]{:S(2)}) collective-permute-start(bf16[1,12,128,128]{3,2,1,0:T(8,128)(2,1)} %get-tuple-element.22), channel_id=1, source_target_pairs={{0,15},{1,14},{2,13},{3,12},{4,7},{5,6},{6,5},{7,4},{8,11},{9,10},... | collective-permute-start | bytes 1179656 | tf_op jit(solution)/shard_map/ppermute | solution.py:168
  49.6 90.9 %collective-permute-start.5 = (bf16[1,12,128,128]{3,2,1,0:T(8,128)(2,1)}, bf16[1,12,128,128]{3,2,1,0:T(8,128)(2,1)}, u32[]{:S(2)}, u32[]{:S(2)}) collective-permute-start(bf16[1,12,128,128]{3,2,1,0:T(8,128)(2,1)} %get-tuple-element.23), channel_id=1, source_target_pairs={{0,8},{1,9},{2,10},{3,11},{4,0},{5,1},{6,2},{7,3},{8,12},{9,13},{1... | collective-permute-start | bytes 1179656 | tf_op jit(solution)/shard_map/ppermute | solution.py:169
  127.9 18.4 %collective-permute-start.6 = (bf16[1,12,128,128]{3,2,1,0:T(8,128)(2,1)}, bf16[1,12,128,128]{3,2,1,0:T(8,128)(2,1)}, u32[]{:S(2)}, u32[]{:S(2)}) collective-permute-start(bf16[1,12,128,128]{3,2,1,0:T(8,128)(2,1)} %get-tuple-element.24), channel_id=1, source_target_pairs={{0,9},{1,8},{2,11},{3,10},{4,1},{5,0},{6,3},{7,2},{8,13},{9,12},{1... | collective-permute-start | bytes 1179656 | tf_op jit(solution)/shard_map/ppermute | solution.py:169
  127.9 28.3 %collective-permute-start.7 = (bf16[1,12,128,128]{3,2,1,0:T(8,128)(2,1)}, bf16[1,12,128,128]{3,2,1,0:T(8,128)(2,1)}, u32[]{:S(2)}, u32[]{:S(2)}) collective-permute-start(bf16[1,12,128,128]{3,2,1,0:T(8,128)(2,1)} %get-tuple-element.25), channel_id=1, source_target_pairs={{0,10},{1,11},{2,8},{3,9},{4,2},{5,3},{6,0},{7,1},{8,14},{9,15},{1... | collective-permute-start | bytes 1179656 | tf_op jit(solution)/shard_map/ppermute | solution.py:169
  131.8 32.4 %collective-permute-start.8 = (bf16[1,12,128,128]{3,2,1,0:T(8,128)(2,1)}, bf16[1,12,128,128]{3,2,1,0:T(8,128)(2,1)}, u32[]{:S(2)}, u32[]{:S(2)}) collective-permute-start(bf16[1,12,128,128]{3,2,1,0:T(8,128)(2,1)} %get-tuple-element.26), channel_id=1, source_target_pairs={{0,11},{1,10},{2,9},{3,8},{4,3},{5,2},{6,1},{7,0},{8,15},{9,14},{1... | collective-permute-start | bytes 1179656 | tf_op jit(solution)/shard_map/ppermute | solution.py:169
  164.1 0.7 copy-start.3
  164.8 0.6 copy-start.4
  165.4 0.6 copy-start.5

commit v5 on v4

--- a/solution.py
+++ b/solution.py
@@ -35,18 +35,38 @@
     )(rows, tiles)
 
 
-def fetch_rows(total, source_ref, row_ref, sources, target_ref, sems):
+def start_rows(total, source_ref, row_ref, sources, target_ref, sems):
     for k in range(total):
         for at, ref in enumerate(sources):
-
             last = at == len(sources) - 1
 
             @pl.when(source_ref[k] >= at if last else source_ref[k] == at)
             def _():
                 pltpu.make_async_copy(ref.at[row_ref[k]], target_ref.at[k], sems.at[k]).start()
 
+
+def wait_rows(total, sources, target_ref, sems):
     for k in range(total):
         pltpu.make_async_copy(sources[0].at[0], target_ref.at[k], sems.at[k]).wait()
+
+
+def stack_kernel(total, source_ref, row_ref, *refs):
+    *sources, out_ref, sems = refs
+    start_rows(total, source_ref, row_ref, sources, out_ref, sems)
+    wait_rows(total, sources, out_ref, sems)
+
+
+def stack_rows(source_ids, row_ids, *sources):
+    total = source_ids.shape[0]
+    return pl.pallas_call(
+        functools.partial(stack_kernel, total),
+        out_shape=jax.ShapeDtypeStruct((total,) + sources[0].shape[1:], sources[0].dtype),
+        in_specs=[SMEM, SMEM] + [HBM] * len(sources),
+        out_specs=VMEM,
+        scratch_shapes=[pltpu.SemaphoreType.DMA((total,))],
+        compiler_params=PARAMS,
+        name="stack_rows",
+    )(source_ids, row_ids, *sources)
 
 
 def collect_kernel(total, source_ref, row_ref, *refs):
@@ -75,58 +95,92 @@
     )(source[None], rows, *sources)
 
 
-def blocks_kernel(total, owner_ref, slot_ref, source_ref, row_ref, tiles_ref, scale_row_ref, scale_got_ref, *refs):
-    *sources, out_ref, fetched_ref, sems = refs
+def blocks_kernel(total, prior, place_ref, slot_ref, source_ref, row_ref, tiles_ref, scale_row_ref, scale_got_ref, *refs):
+    *sources, out_ref, fetched_ref, scale_ref, stage_ref, list_ref, sems, out_sems = refs
+    if prior:
+        sources = sources[1:]
     local_rows, slots, side, _ = tiles_ref.shape
     cands = out_ref.shape[1]
-    together = 2 if cands % 2 == 0 else 1
-    fetch_rows(total, source_ref, row_ref, sources, fetched_ref, sems)
-
-    def one_row(i, carry):
-        left = jnp.concatenate([tiles_ref[i, r] for r in range(slots)], axis=1)
-        scale_x = jnp.broadcast_to(scale_row_ref[i], (side, side)).T
-
-        def some_blocks(step, inner):
-            right = []
-            for k in range(together):
-                block = i * cands + step * together + k
-                owner = owner_ref[block]
-                picked = []
-                for r in range(slots):
-                    s = slot_ref[block * slots + r]
-                    tile = fetched_ref[owner, jnp.maximum(s, 0)]
-                    picked.append(jnp.where(s >= 0, tile, jnp.zeros_like(tile)))
-                right.append(jnp.concatenate(picked, axis=1))
-            right = jnp.concatenate(right, axis=0)
-            shared = lax.dot_general(left, right, (((1,), (1,)), ((), ())), preferred_element_type=jnp.float32)
-            for k in range(together):
-                q = step * together + k
-                scale = scale_x * scale_got_ref[owner_ref[i * cands + q]]
-                out_ref[i, q] = (shared[:, k * side : (k + 1) * side] * scale).astype(out_ref.dtype)
-            return inner
-
-        return lax.fori_loop(0, cands // together, some_blocks, carry)
-
-    lax.fori_loop(0, local_rows, one_row, 0)
-
-
-def blocks(owners, slot_of, source_ids, row_ids, tiles, scale_row, scale_got, sources):
+    start_rows(total, source_ref, row_ref, sources, fetched_ref, sems)
+
+    def note_block(block, count):
+        place = place_ref[block]
+
+        @pl.when(place >= 0)
+        def _():
+            list_ref[count] = block
+
+        return count + (place >= 0).astype(jnp.int32)
+
+    count = lax.fori_loop(0, local_rows * cands, note_block, jnp.int32(0))
+    for i in range(local_rows):
+        scale_ref[i] = jnp.broadcast_to(scale_row_ref[i], (side, side)).T
+    wait_rows(total, sources, fetched_ref, sems)
+
+    def two_blocks(step, carry):
+        for k in (0, 1):
+            at = 2 * step + k
+            block = list_ref[jnp.minimum(at, count - 1)]
+            i, place = block // cands, place_ref[block]
+            left, right = [], []
+            for r in range(slots):
+                s = slot_ref[block * slots + r]
+                tile = fetched_ref[place, jnp.maximum(s, 0)]
+                right.append(jnp.where(s >= 0, tile, jnp.zeros_like(tile)))
+                left.append(tiles_ref[i, r])
+            shared = lax.dot_general(
+                jnp.concatenate(left, axis=1), jnp.concatenate(right, axis=1), (((1,), (1,)), ((), ())),
+                preferred_element_type=jnp.float32,
+            )
+            stage_ref[at] = (shared * (scale_ref[i] * scale_got_ref[place])).astype(stage_ref.dtype)
+        for k in (0, 1):
+            at = 2 * step + k
+
+            @pl.when(at < count)
+            def _():
+                block = list_ref[at]
+                to = out_ref.at[block // cands, lax.rem(block, cands)]
+                pltpu.make_async_copy(stage_ref.at[at], to, out_sems.at[at]).start()
+
+        return carry
+
+    lax.fori_loop(0, (count + 1) // 2, two_blocks, 0)
+
+    def wait_block(at, carry):
+        pltpu.make_async_copy(stage_ref.at[at], out_ref.at[0, 0], out_sems.at[at]).wait()
+        return carry
+
+    lax.fori_loop(0, count, wait_block, 0)
+
+
+def blocks(place, slot_of, source_ids, row_ids, tiles, scale_row, scale_got, sources, prior=None):
     local_rows, slots, side, _ = tiles.shape
-    total = source_ids.shape[0]
+    total, cands = source_ids.shape[0], place.shape[1]
+    every = local_rows * cands
+    extra = [] if prior is None else [prior]
     return pl.pallas_call(
-        functools.partial(blocks_kernel, total),
-        out_shape=jax.ShapeDtypeStruct((local_rows, owners.shape[1], side, side), jnp.bfloat16),
-        in_specs=[SMEM] * 4 + [VMEM] * 3 + [HBM] * len(sources),
-        out_specs=VMEM,
+        functools.partial(blocks_kernel, total, prior is not None),
+        out_shape=jax.ShapeDtypeStruct((local_rows, cands, side, side), jnp.bfloat16),
+        in_specs=[SMEM] * 4 + [VMEM] * 3 + [HBM] * (len(extra) + len(sources)),
+        out_specs=HBM,
+        input_output_aliases={7: 0} if extra else {},
         scratch_shapes=[
             pltpu.VMEM((total,) + tiles.shape[1:], tiles.dtype),
+            pltpu.VMEM((local_rows, side, side), jnp.float32),
+            pltpu.VMEM((every + every % 2, side, side), jnp.bfloat16),
+            pltpu.SMEM((every,), jnp.int32),
             pltpu.SemaphoreType.DMA((total,)),
+            pltpu.SemaphoreType.DMA((every,)),
         ],
         compiler_params=PARAMS,
+        cost_estimate=pl.CostEstimate(
+            flops=2 * total * every // 16 * slots * side**3, bytes_accessed=2 * (total + local_rows) * slots * side**2,
+            transcendentals=0,
+        ),
         name="blocks",
     )(
-        owners.reshape(-1), slot_of.reshape(-1), source_ids, row_ids, tiles, scale_row[:, None, :], scale_got[:, None, :],
-        *sources,
+        place.reshape(-1), slot_of.reshape(-1), source_ids, row_ids, tiles, scale_row[:, None, :], scale_got[:, None, :],
+        *extra, *sources,
     )
 
 
@@ -140,7 +194,7 @@
     return [(4 * z + p, 4 * t + (p ^ flip)) for z, t in enumerate(targets) if t is not None for p in range(4)]
 
 
-HALVES = [list(range(8)), list(range(8, 16))]
+PLANES = [[4 * z + p for p in range(4)] for z in range(4)]
 
 
 def relay(wanted_by, me, tiles, middle):
@@ -153,11 +207,16 @@
         of_owner = jnp.sum(jnp.where(peer_ids == owner, wanted_by, 0), axis=1)
         return jnp.sum(jnp.where(readers[:, None] == peer_ids, of_owner, 0), axis=1)
 
-    half = me // 8 * 8 + jnp.arange(8, dtype=jnp.int32)
     beyond = 4 * (plane ^ 3) + (mate ^ flips)
-    half_send, first_send = pick_rows(lookup(jnp.concatenate([half, beyond[:1]]), me), tiles, (8, 1))
-    near = lax.all_to_all(half_send, "col", split_axis=0, concat_axis=0, axis_index_groups=HALVES, tiled=True)
+    readers = jnp.concatenate([4 * (plane ^ 1) + flips, beyond[:1], 4 * plane + flips])
+    mine = lookup(readers, me)
+    beside_send, first_send = pick_rows(mine[:5], tiles, (4, 1))
+    beside = lax.ppermute(beside_send, "col", moves([1, 0, 3, 2]))
     beyond_got = [lax.ppermute(first_send, "col", moves([3, None, None, 0]))]
+    pairs = jnp.arange(8, dtype=jnp.int32)
+    rows = jnp.where(pairs % 2 == 0, jnp.repeat(mine[5:], 2), pairs // 2)
+    plane_send = stack_rows(pairs % 2, rows, tiles, beside)
+    near = lax.all_to_all(plane_send, "col", split_axis=0, concat_axis=0, axis_index_groups=PLANES, tiled=True)
 
     readers = jnp.concatenate(
         [jnp.where(inner, 4 * plane, 4 * (plane ^ 3)) + (mate ^ flips[1:]),
@@ -168,13 +227,14 @@
     beyond_got += [lax.ppermute(sends[m - 1], "col", moves([3, 1, 2, 0], m)) for m in (1, 2, 3)]
     across_got = [lax.ppermute(sends[m + 3], "col", moves([2, 0, 3, 1], m)) for m in range(4)]
 
-    mine_in_middle = lookup(me[None], 4 * (plane ^ 3) + mate)[0]
-    owner_plane, flip = peer_ids // 4, mate ^ (peer_ids % 4)
-    is_near, is_beyond = owner_plane // 2 == plane // 2, owner_plane == plane ^ 3
-    is_middle = is_beyond & inner & (flip == 0)
-    source_ids = jnp.where(is_near, 0, jnp.where(is_middle, 1, jnp.where(is_beyond, 2, 6) + flip))
-    row_ids = jnp.where(is_near, peer_ids % 8, jnp.where(is_middle, mine_in_middle, 0))
-    return source_ids, row_ids, [near, middle, *beyond_got, *across_got]
+    first_owners = jnp.concatenate([jnp.where(pairs % 2 == 0, 4 * plane, 4 * (plane ^ 1)) + pairs // 2, beyond])
+    mine_in_middle = lookup(me[None], beyond[0])
+    sources = jnp.concatenate([jnp.zeros((8,), jnp.int32), jnp.where(inner & (flips == 0), 1, 2 + flips)])
+    rows = jnp.concatenate([pairs, jnp.where(inner & (flips == 0), mine_in_middle, 0)])
+    return [
+        (first_owners, sources, rows, [near, middle, *beyond_got]),
+        (4 * (plane ^ 2) + (mate ^ flips), flips, jnp.zeros_like(flips), across_got),
+    ]
 
 
 def local(tiles, tile_cols, tile_count, candidates, degree):
@@ -220,11 +280,16 @@
     scale_other = lax.rsqrt(degree_got.astype(jnp.float32))
 
     if relayed:
-        source_ids, row_ids, sources = relay(wanted_by, me, tiles, middle)
+        parts = relay(wanted_by, me, tiles, middle)
     else:
-        sources = [exchange_direct(wanted_by, me, tiles)]
-        source_ids, row_ids = jnp.zeros_like(peer_ids), peer_ids
-    return blocks(owners, slot_of, source_ids, row_ids, tiles, scale_row, scale_other, sources)
+        parts = [(peer_ids, jnp.zeros_like(peer_ids), peer_ids, [exchange_direct(wanted_by, me, tiles)])]
+    done = None
+    for owner_ids, source_ids, row_ids, sources in parts:
+        at = jnp.arange(owner_ids.shape[0], dtype=jnp.int32)
+        place = jnp.sum(jnp.where(owners[:, :, None] == owner_ids, at + 1, 0), axis=2) - 1
+        scale_got = jnp.sum(jnp.where((owner_ids[:, None] == peer_ids)[:, :, None], scale_other, 0.0), axis=1)
+        done = blocks(place, slot_of, source_ids, row_ids, tiles, scale_row, scale_got, sources, done)
+    return done
 
 
 def solution(mesh):

time: 187 us -> 151 us (0.81)
  starting transfers between devices: 110 us -> 39.3 us
  waiting for transfers between devices: 30.2 us -> 54.9 us
  Pallas kernels: 26.3 us -> 31.2 us
  local copies, waits for them, and re-layouts: 10.5 us -> 13.6 us
    ppermute x4, starting transfers between devices: 85.7 us -> 14 us  [relay(): lax.ppermute(sends[m + 3], 'col', moves([2, 0, 3, 1], m))]
    ppermute x0 -> x1, waiting for transfers between devices: none -> 33.8 us  [relay(): beside = lax.ppermute(beside_send, 'col', moves([1, 0, 3, 2]))]
    ppermute x4, waiting for transfers between devices: 23.6 us -> 2.96 us  [relay(): lax.ppermute(sends[m + 3], 'col', moves([2, 0, 3, 1], m))]
    ppermute x3, waiting for transfers between devices: 0.01 us -> 12 us  [relay(): lax.ppermute(sends[m - 1], 'col', moves([3, 1, 2, 0], m))]
    pallas_call x1 -> x3, Pallas kernels: 20.2 us -> 26.2 us  [the longest x2 21.9 us: blocks(): pl.pallas_call(functools.partial(blocks_kernel, total, prior is not None)...]
    all_to_all x1, waiting for transfers between devices: 6.6 us -> 2.11 us  [local(): notes = lax.all_to_all(note, 'col', split_axis=0, concat_axis=0, tiled=True)]
    all_to_all x1, waiting for transfers between devices: 0.01 us -> 4.06 us  [relay(): lax.all_to_all(plane_send, 'col', split_axis=0, concat_axis=0, axis_index...]
    unnamed x27 -> x33, local copies, waits for them, and re-layouts: 5.25 us -> 8.82 us
  transfers between devices with their start and end apart: 11 -> 12, of which waited for: 4 -> 6; matrix products, arithmetic and copies ran while one was open for 6% -> 8% of each run, Pallas kernels for 2% -> 16%
where the time goes in v5:
time: 151 us; the launch traced here: 150 us
  waiting for transfers between devices  54.9 us (36%)
  starting transfers between devices  39.3 us (26%)
  Pallas kernels  31.2 us (21%)
  local copies, waits for them, and re-layouts  13.6 us (9%)
  other arithmetic  10.6 us (7%)
    ppermute x1, waiting for transfers between devices, relay(): beside = lax.ppermute(beside_send, 'col', moves([1, 0, 3, 2]))  33.8 us
    pallas_call x2, Pallas kernels, blocks(): pl.pallas_call(functools.partial(blocks_kernel, total, prior is not None)...  21.9 us
    ppermute x4, starting transfers between devices, relay(): lax.ppermute(sends[m + 3], 'col', moves([2, 0, 3, 1], m))  14 us
    ppermute x3, waiting for transfers between devices, relay(): lax.ppermute(sends[m - 1], 'col', moves([3, 1, 2, 0], m))  12 us
    unnamed x33, local copies, waits for them, and re-layouts  8.82 us
    all_to_all x1, starting transfers between devices, local(): notes = lax.all_to_all(note, 'col', split_axis=0, concat_axis=0, tiled=True)  7.39 us
    ppermute x3, starting transfers between devices, relay(): lax.ppermute(sends[m - 1], 'col', moves([3, 1, 2, 0], m))  5.87 us
    all_to_all x1, starting transfers between devices, relay(): lax.all_to_all(plane_send, 'col', split_axis=0, concat_axis=0, axis_index...  4.65 us
  transfers between devices with their start and end apart: 12, of which 6 were waited for; matrix products, arithmetic and copies ran while one was open for 8% of the time, Pallas kernels for 16%

profile of v5, /device:TPU:0, one launch (start us, length us, event | category | flops | bytes accessed | tf_op | source)
XLA Modules:
  0.0 149.9 jit_solution(4670575469419135654)
XLA Ops:
  0.0 0.8 reshape.123
  0.8 0.7 add_select_fusion
  1.6 0.8 pad_add_fusion
  2.4 0.7 all_to_all.11
  3.1 7.4 %all-to-all-start = ((s32[16,1,896]{2,1,0:T(1,128)}), s32[16,1,896]{2,1,0:T(1,128)S(1)}, u32[]{:S(2)}, u32[]{:S(2)}) async-start(s32[16,1,896]{2,1,0:T(1,128)} %all_to_all.11), calls=%async_computation | async-start | bytes 114688 | tf_op jit(solution)/shard_map/all_to_all | solution.py:257
  10.5 2.1 %collective-permute-start.1 = (bf16[6,12,128,128]{3,2,1,0:T(8,128)(2,1)}, bf16[6,12,128,128]{3,2,1,0:T(8,128)(2,1)}, u32[]{:S(2)}, u32[]{:S(2)}) collective-permute-start(bf16[6,12,128,128]{3,2,1,0:T(8,128)(2,1)} %tiles_ref.5), channel_id=1, source_target_pairs={{4,8},{5,9},{6,10},{7,11},{8,4},{9,5},{10,6},{11,7},{20,24},{21,25... | collective-permute-start | bytes 7077896 | tf_op jit(solution)/shard_map/ppermute | solution.py:259
  12.6 0.7 convert_rsqrt_fusion.1
  13.4 0.6 concatenate.20.source_ref
  14.2 0.7 sub.36.place_ref
  15.2 2.1 %all-to-all-done = s32[16,1,896]{2,1,0:T(1,128)S(1)} async-done(((s32[16,1,896]{2,1,0:T(1,128)}), s32[16,1,896]{2,1,0:T(1,128)S(1)}, u32[]{:S(2)}, u32[]{:S(2)}) %all-to-all-start) | async-done | bytes 57376 | tf_op jit(solution)/shard_map/all_to_all | solution.py:257
  17.7 1.7 %copy-done = bf16[6,12,128,128]{3,2,1,0:T(8,128)(2,1)S(1)} copy-done((bf16[6,12,128,128]{3,2,1,0:T(8,128)(2,1)S(1)}, bf16[6,12,128,128]{3,2,1,0:T(8,128)(2,1)}, u32[]{:S(2)}) %copy-start) | copy-done | bytes 2359320
  19.3 1.7 %pick_rows.1 = (bf16[4,12,128,128]{3,2,1,0:T(8,128)(2,1)}, bf16[1,12,128,128]{3,2,1,0:T(8,128)(2,1)S(1)}) custom-call(s32[5]{0:T(128)S(1)} %bitcast.10, bf16[6,12,128,128]{3,2,1,0:T(8,128)(2,1)S(1)} %copy-done), custom_call_target="tpu_custom_call" | custom-call | tf_op jit(solution)/shard_map/pick_rows/pallas_call | solution.py:27
  21.1 1.3 collective-permute-start
  22.3 0.6 sub.41.place_ref
  23.5 33.8 %collective-permute-done.refs_1_ = bf16[4,12,128,128]{3,2,1,0:T(8,128)(2,1)} collective-permute-done((bf16[4,12,128,128]{3,2,1,0:T(8,128)(2,1)}, bf16[4,12,128,128]{3,2,1,0:T(8,128)(2,1)}, u32[]{:S(2)}, u32[]{:S(2)}) %collective-permute-start) | collective-permute-done | bytes 1572896 | tf_op jit(solution)/shard_map/ppermute | solution.py:214
  57.3 4.2 %stack_rows.1 = bf16[8,12,128,128]{3,2,1,0:T(8,128)(2,1)} custom-call(s32[8]{0:T(128)S(1)} %and_select_fusion.1.source_ref, s32[8]{0:T(128)S(1)} %compare_select_fusion.1.row_ref, bf16[6,12,128,128]{3,2,1,0:T(8,128)(2,1)S(1)} %copy-done.1, bf16[4,12,128,128]{3,2,1,0:T(8,128)(2,1)} %collective-permute-done.refs_1_), custom_call_target="tpu_custom_call" | custom-call | tf_op jit(solution)/shard_map/stack_rows/pallas_call | solution.py:61
  61.6 4.6 %all-to-all-start.1 = ((bf16[8,12,128,128]{3,2,1,0:T(8,128)(2,1)}), bf16[8,12,128,128]{3,2,1,0:T(8,128)(2,1)}, u32[]{:S(2)}, u32[]{:S(2)}) async-start(bf16[8,12,128,128]{3,2,1,0:T(8,128)(2,1)} %stack_rows.1), calls=%async_computation.1 | async-start | bytes 6291456 | tf_op jit(solution)/shard_map/all_to_all | solution.py:219
  66.2 0.6 iota_compare_fusion.7
  67.2 4.1 %collective-permute-start.2 = (bf16[1,12,128,128]{3,2,1,0:T(8,128)(2,1)S(1)}, bf16[1,12,128,128]{3,2,1,0:T(8,128)(2,1)S(1)}, u32[]{:S(2)}, u32[]{:S(2)}) collective-permute-start(bf16[1,12,128,128]{3,2,1,0:T(8,128)(2,1)S(1)} %get-tuple-element.19), channel_id=1, source_target_pairs={{0,12},{1,13},{2,14},{3,15},{12,0},{13,1},{14,2},{15,3},{16,28},{1... | collective-permute-start | bytes 1179656 | tf_op jit(solution)/shard_map/ppermute | solution.py:215
  71.9 0.3 select_reduce_fusion.1
  72.2 1.4 select_reduce_fusion
  73.5 0.6 broadcast_add_fusion
  74.2 3.3 %collect.1 = (bf16[1,12,128,128]{3,2,1,0:T(8,128)(2,1)S(1)}, bf16[1,12,128,128]{3,2,1,0:T(8,128)(2,1)S(1)}, bf16[1,12,128,128]{3,2,1,0:T(8,128)(2,1)}, bf16[1,12...) custom-call(s32[1]{0:T(128)} %bitcast.3.source_ref, ...), custom_call_target="tpu_custom_call" | custom-call | tf_op jit(solution)/shard_map/collect/pallas_call | solution.py:87
  77.5 1.5 collective-permute-start.3
  79.0 3.3 %collective-permute-start.4 = (bf16[1,12,128,128]{3,2,1,0:T(8,128)(2,1)S(1)}, bf16[1,12,128,128]{3,2,1,0:T(8,128)(2,1)S(1)}, u32[]{:S(2)}, u32[]{:S(2)}) collective-permute-start(bf16[1,12,128,128]{3,2,1,0:T(8,128)(2,1)S(1)} %get-tuple-element.21), channel_id=1, source_target_pairs={{0,14},{1,15},{2,12},{3,13},{4,6},{5,7},{6,4},{7,5},{8,10},{9,11},... | collective-permute-start | bytes 1179656 | tf_op jit(solution)/shard_map/ppermute | solution.py:227
  82.3 0.6 fusion.5
  82.9 1.1 collective-permute-start.5
  84.0 0.6 broadcast_select_fusion
  84.9 0.7 copy-done.2
  85.6 2.5 %collective-permute-start.7 = (bf16[1,12,128,128]{3,2,1,0:T(8,128)(2,1)}, bf16[1,12,128,128]{3,2,1,0:T(8,128)(2,1)S(1)}, u32[]{:S(2)}, u32[]{:S(2)}) collective-permute-start(bf16[1,12,128,128]{3,2,1,0:T(8,128)(2,1)} %get-tuple-element.24), channel_id=1, source_target_pairs={{0,9},{1,8},{2,11},{3,10},{4,1},{5,0},{6,3},{7,2},{8,13},{9,12},{1... | collective-permute-start | bytes 1179656 | tf_op jit(solution)/shard_map/ppermute | solution.py:228
  88.1 2.5 %collective-permute-done.3.refs_3_ = bf16[1,12,128,128]{3,2,1,0:T(8,128)(2,1)S(1)} collective-permute-done((bf16[1,12,128,128]{3,2,1,0:T(8,128)(2,1)S(1)}, bf16[1,12,128,128]{3,2,1,0:T(8,128)(2,1)S(1)}, u32[]{:S(2)}, u32[]{:S(2)}) %collective-permute-start.3) | collective-permute-done | bytes 393248 | tf_op jit(solution)/shard_map/ppermute | solution.py:227
  90.6 0.7 copy-done.4
  91.4 9.5 %collective-permute-done.4.refs_4_ = bf16[1,12,128,128]{3,2,1,0:T(8,128)(2,1)S(1)} collective-permute-done((bf16[1,12,128,128]{3,2,1,0:T(8,128)(2,1)S(1)}, bf16[1,12,128,128]{3,2,1,0:T(8,128)(2,1)S(1)}, u32[]{:S(2)}, u32[]{:S(2)}) %collective-permute-start.4) | collective-permute-done | bytes 393248 | tf_op jit(solution)/shard_map/ppermute | solution.py:227
  100.9 0.7 copy-done.6
  101.6 11.4 %collective-permute-start.9 = (bf16[1,12,128,128]{3,2,1,0:T(8,128)(2,1)}, bf16[1,12,128,128]{3,2,1,0:T(8,128)(2,1)}, u32[]{:S(2)}, u32[]{:S(2)}) collective-permute-start(bf16[1,12,128,128]{3,2,1,0:T(8,128)(2,1)} %get-tuple-element.26), channel_id=1, source_target_pairs={{0,11},{1,10},{2,9},{3,8},{4,3},{5,2},{6,1},{7,0},{8,15},{9,14},{1... | collective-permute-start | bytes 1179656 | tf_op jit(solution)/shard_map/ppermute | solution.py:228
  113.1 0.7 pad_add_fusion.2.row_ref
  113.7 0.9 sub.38.slot_ref
  114.6 1.4 select_reduce_fusion.7
  116.0 4.1 %all-to-all-done.1.refs_0_ = bf16[8,12,128,128]{3,2,1,0:T(8,128)(2,1)} async-done(((bf16[8,12,128,128]{3,2,1,0:T(8,128)(2,1)}), bf16[8,12,128,128]{3,2,1,0:T(8,128)(2,1)}, u32[]{:S(2)}, u32[]{:S(2)}) %all-to-all-start.1) | async-done | bytes 3145760 | tf_op jit(solution)/shard_map/all_to_all | solution.py:219
  120.1 1.0 copy-done.3
  121.1 1.0 copy-done.5
  122.1 1.0 copy-done.7
  123.1 0.6 copy-done.10
  123.7 0.7 copy-done.11
  124.3 0.7 copy-done.12
  125.0 14.8 %blocks.2.refs_0_ = bf16[6,12,128,128]{3,2,1,0:T(8,128)(2,1)} custom-call(s32[72]{0:T(128)S(1)} %copy-done.10, s32[864]{0:T(1024)S(1)} %sub.38.slot_ref, s32[12]{0:T(128)S(1)} %copy-done.11, s32[12]{0:T(128)S(1)} %copy-done.12, bf16[6,12,128,128]{3,2,1,0:T(8,128)(2,1)S(1)} %copy-done.1, f32[6,1,128]{2,1,0:T(1,128)S(1)} %broadcast_in_dim.241.scale_row_ref, ...), custom_call_target="tpu_custom_call" | custom-call | flops 2717908992 | bytes 7077888 | tf_op jit(solution)/shard_map/blocks/pallas_call | solution.py:161
  139.8 3.0 %collective-permute-done.9.refs_4_ = bf16[1,12,128,128]{3,2,1,0:T(8,128)(2,1)} collective-permute-done((bf16[1,12,128,128]{3,2,1,0:T(8,128)(2,1)}, bf16[1,12,128,128]{3,2,1,0:T(8,128)(2,1)}, u32[]{:S(2)}, u32[]{:S(2)}) %collective-permute-start.9) | collective-permute-done | bytes 393248 | tf_op jit(solution)/shard_map/ppermute | solution.py:228
  142.8 7.1 %blocks.3 = bf16[6,12,128,128]{3,2,1,0:T(8,128)(2,1)} custom-call(s32[72]{0:T(128)S(1)} %copy-done.9, s32[864]{0:T(1024)S(1)} %sub.38.slot_ref, s32[4]{0:T(128)S(1)} %iota.84.source_ref, s32[4]{0:T(128)S(1)} %broadcast_17_row_ref.2.row_ref, bf16[6,12,128,128]{3,2,1,0:T(8,128)(2,1)S(1)} %copy-done.1, ...), custom_call_target="tpu_custom_call", output_to_operand_aliasing={{}: (7, {})} | custom-call | flops 905969664 | bytes 3932160 | tf_op jit(solution)/shard_map/blocks/pallas_call | solution.py:161
  (79 shorter events, 2.9 us)
Async XLA Ops:
  0.0 23.2 %copy-start.14 = (s32[6,12]{1,0:T(8,128)S(1)}, s32[6,12]{1,0:T(8,128)}, u32[]{:S(2)}) copy-start(s32[6,12]{1,0:T(8,128)} %param.6) | copy-start | bytes 868
  0.0 23.2 %copy-start.15 = (s32[6]{0:T(128)S(1)}, s32[6]{0:T(128)}, u32[]{:S(2)}) copy-start(s32[6]{0:T(128)} %param.7) | copy-start | bytes 76
  3.1 14.2 %all-to-all-start = ((s32[16,1,896]{2,1,0:T(1,128)}), s32[16,1,896]{2,1,0:T(1,128)S(1)}, u32[]{:S(2)}, u32[]{:S(2)}) async-start(s32[16,1,896]{2,1,0:T(1,128)} %all_to_all.11), calls=%async_computation | async-start | bytes 114688 | tf_op jit(solution)/shard_map/all_to_all | solution.py:257
  10.5 63.7 %collective-permute-start.1 = (bf16[6,12,128,128]{3,2,1,0:T(8,128)(2,1)}, bf16[6,12,128,128]{3,2,1,0:T(8,128)(2,1)}, u32[]{:S(2)}, u32[]{:S(2)}) collective-permute-start(bf16[6,12,128,128]{3,2,1,0:T(8,128)(2,1)} %tiles_ref.5), channel_id=1, source_target_pairs={{4,8},{5,9},{6,10},{7,11},{8,4},{9,5},{10,6},{11,7},{20,24},{21,25... | collective-permute-start | bytes 7077896 | tf_op jit(solution)/shard_map/ppermute | solution.py:259
  17.7 1.7 %copy-start = (bf16[6,12,128,128]{3,2,1,0:T(8,128)(2,1)S(1)}, bf16[6,12,128,128]{3,2,1,0:T(8,128)(2,1)}, u32[]{:S(2)}) copy-start(bf16[6,12,128,128]{3,2,1,0:T(8,128)(2,1)} %tiles_ref.5) | copy-start | bytes 7077892
  19.3 38.0 %copy-start.1 = (bf16[6,12,128,128]{3,2,1,0:T(8,128)(2,1)S(1)}, bf16[6,12,128,128]{3,2,1,0:T(8,128)(2,1)}, u32[]{:S(2)}) copy-start(bf16[6,12,128,128]{3,2,1,0:T(8,128)(2,1)} %tiles_ref.5) | copy-start | bytes 7077892
  21.1 36.3 %collective-permute-start = (bf16[4,12,128,128]{3,2,1,0:T(8,128)(2,1)}, bf16[4,12,128,128]{3,2,1,0:T(8,128)(2,1)}, u32[]{:S(2)}, u32[]{:S(2)}) collective-permute-start(bf16[4,12,128,128]{3,2,1,0:T(8,128)(2,1)} %get-tuple-element.17), channel_id=1, source_target_pairs={{0,4},{1,5},{2,6},{3,7},{4,0},{5,1},{6,2},{7,3},{8,12},{9,13},{10,... | collective-permute-start | bytes 4718600 | tf_op jit(solution)/shard_map/ppermute | solution.py:214
  61.6 58.5 %all-to-all-start.1 = ((bf16[8,12,128,128]{3,2,1,0:T(8,128)(2,1)}), bf16[8,12,128,128]{3,2,1,0:T(8,128)(2,1)}, u32[]{:S(2)}, u32[]{:S(2)}) async-start(bf16[8,12,128,128]{3,2,1,0:T(8,128)(2,1)} %stack_rows.1), calls=%async_computation.1 | async-start | bytes 6291456 | tf_op jit(solution)/shard_map/all_to_all | solution.py:219
  67.2 17.7 %collective-permute-start.2 = (bf16[1,12,128,128]{3,2,1,0:T(8,128)(2,1)S(1)}, bf16[1,12,128,128]{3,2,1,0:T(8,128)(2,1)S(1)}, u32[]{:S(2)}, u32[]{:S(2)}) collective-permute-start(bf16[1,12,128,128]{3,2,1,0:T(8,128)(2,1)S(1)} %get-tuple-element.19), channel_id=1, source_target_pairs={{0,12},{1,13},{2,14},{3,15},{12,0},{13,1},{14,2},{15,3},{16,28},{1... | collective-permute-start | bytes 1179656 | tf_op jit(solution)/shard_map/ppermute | solution.py:215
  77.5 13.1 %collective-permute-start.3 = (bf16[1,12,128,128]{3,2,1,0:T(8,128)(2,1)S(1)}, bf16[1,12,128,128]{3,2,1,0:T(8,128)(2,1)S(1)}, u32[]{:S(2)}, u32[]{:S(2)}) collective-permute-start(bf16[1,12,128,128]{3,2,1,0:T(8,128)(2,1)S(1)} %get-tuple-element.20), channel_id=1, source_target_pairs={{0,13},{1,12},{2,15},{3,14},{4,5},{5,4},{6,7},{7,6},{8,9},{9,8},{1... | collective-permute-start | bytes 1179656 | tf_op jit(solution)/shard_map/ppermute | solution.py:227
  79.0 21.9 %collective-permute-start.4 = (bf16[1,12,128,128]{3,2,1,0:T(8,128)(2,1)S(1)}, bf16[1,12,128,128]{3,2,1,0:T(8,128)(2,1)S(1)}, u32[]{:S(2)}, u32[]{:S(2)}) collective-permute-start(bf16[1,12,128,128]{3,2,1,0:T(8,128)(2,1)S(1)} %get-tuple-element.21), channel_id=1, source_target_pairs={{0,14},{1,15},{2,12},{3,13},{4,6},{5,7},{6,4},{7,5},{8,10},{9,11},... | collective-permute-start | bytes 1179656 | tf_op jit(solution)/shard_map/ppermute | solution.py:227
  82.3 31.4 %copy-start.13 = (f32[16,128]{1,0:T(8,128)}, f32[16,128]{1,0:T(8,128)S(1)}, u32[]{:S(2)}) copy-start(f32[16,128]{1,0:T(8,128)S(1)} %convert_rsqrt_fusion) | copy-start | bytes 24580
  82.9 33.1 %collective-permute-start.5 = (bf16[1,12,128,128]{3,2,1,0:T(8,128)(2,1)}, bf16[1,12,128,128]{3,2,1,0:T(8,128)(2,1)}, u32[]{:S(2)}, u32[]{:S(2)}) collective-permute-start(bf16[1,12,128,128]{3,2,1,0:T(8,128)(2,1)} %get-tuple-element.22), channel_id=1, source_target_pairs={{0,15},{1,14},{2,13},{3,12},{4,7},{5,6},{6,5},{7,4},{8,11},{9,10},... | collective-permute-start | bytes 1179656 | tf_op jit(solution)/shard_map/ppermute | solution.py:227
  84.8 55.0 %collective-permute-start.6 = (bf16[1,12,128,128]{3,2,1,0:T(8,128)(2,1)}, bf16[1,12,128,128]{3,2,1,0:T(8,128)(2,1)S(1)}, u32[]{:S(2)}, u32[]{:S(2)}) collective-permute-start(bf16[1,12,128,128]{3,2,1,0:T(8,128)(2,1)} %get-tuple-element.23), channel_id=1, source_target_pairs={{0,8},{1,9},{2,10},{3,11},{4,0},{5,1},{6,2},{7,3},{8,12},{9,13},{1... | collective-permute-start | bytes 1179656 | tf_op jit(solution)/shard_map/ppermute | solution.py:228
  84.9 0.7 copy-start.2
  85.6 54.2 %collective-permute-start.7 = (bf16[1,12,128,128]{3,2,1,0:T(8,128)(2,1)}, bf16[1,12,128,128]{3,2,1,0:T(8,128)(2,1)S(1)}, u32[]{:S(2)}, u32[]{:S(2)}) collective-permute-start(bf16[1,12,128,128]{3,2,1,0:T(8,128)(2,1)} %get-tuple-element.24), channel_id=1, source_target_pairs={{0,9},{1,8},{2,11},{3,10},{4,1},{5,0},{6,3},{7,2},{8,13},{9,12},{1... | collective-permute-start | bytes 1179656 | tf_op jit(solution)/shard_map/ppermute | solution.py:228
  90.6 0.7 copy-start.4
  91.4 48.5 %collective-permute-start.8 = (bf16[1,12,128,128]{3,2,1,0:T(8,128)(2,1)}, bf16[1,12,128,128]{3,2,1,0:T(8,128)(2,1)S(1)}, u32[]{:S(2)}, u32[]{:S(2)}) collective-permute-start(bf16[1,12,128,128]{3,2,1,0:T(8,128)(2,1)} %get-tuple-element.25), channel_id=1, source_target_pairs={{0,10},{1,11},{2,8},{3,9},{4,2},{5,3},{6,0},{7,1},{8,14},{9,15},{1... | collective-permute-start | bytes 1179656 | tf_op jit(solution)/shard_map/ppermute | solution.py:228
  100.9 0.7 copy-start.6
  101.6 41.2 %collective-permute-start.9 = (bf16[1,12,128,128]{3,2,1,0:T(8,128)(2,1)}, bf16[1,12,128,128]{3,2,1,0:T(8,128)(2,1)}, u32[]{:S(2)}, u32[]{:S(2)}) collective-permute-start(bf16[1,12,128,128]{3,2,1,0:T(8,128)(2,1)} %get-tuple-element.26), channel_id=1, source_target_pairs={{0,11},{1,10},{2,9},{3,8},{4,3},{5,2},{6,1},{7,0},{8,15},{9,14},{1... | collective-permute-start | bytes 1179656 | tf_op jit(solution)/shard_map/ppermute | solution.py:228
  120.1 1.0 copy-start.3
  121.1 1.0 copy-start.5
  122.1 1.0 copy-start.7
  123.1 0.6 copy-start.10
  123.6 0.7 copy-start.11
  124.3 0.7 copy-start.12
  125.0 17.8 %copy-start.8 = (f32[4,128]{1,0:T(4,128)S(1)}, f32[4,128]{1,0:T(4,128)}, u32[]{:S(2)}) copy-start(f32[4,128]{1,0:T(4,128)} %select_reduce_fusion.7) | copy-start | bytes 6148
  125.0 17.8 %copy-start.9 = (s32[72]{0:T(128)S(1)}, s32[72]{0:T(128)}, u32[]{:S(2)}) copy-start(s32[72]{0:T(128)} %sub.36.place_ref) | copy-start | bytes 868

commit v6 on v5

--- a/solution.py
+++ b/solution.py
@@ -208,15 +208,13 @@
         return jnp.sum(jnp.where(readers[:, None] == peer_ids, of_owner, 0), axis=1)
 
     beyond = 4 * (plane ^ 3) + (mate ^ flips)
-    readers = jnp.concatenate([4 * (plane ^ 1) + flips, beyond[:1], 4 * plane + flips])
-    mine = lookup(readers, me)
-    beside_send, first_send = pick_rows(mine[:5], tiles, (4, 1))
+    mine = lookup(jnp.concatenate([4 * (plane ^ 1) + flips, 4 * plane + flips, beyond[:1]]), me)
+    (beside_send,) = pick_rows(mine[:4], tiles, (4,))
     beside = lax.ppermute(beside_send, "col", moves([1, 0, 3, 2]))
+    own_send, first_send = pick_rows(mine[4:], tiles, (4, 1))
+    own = lax.all_to_all(own_send, "col", split_axis=0, concat_axis=0, axis_index_groups=PLANES, tiled=True)
+    near = lax.all_to_all(beside, "col", split_axis=0, concat_axis=0, axis_index_groups=PLANES, tiled=True)
     beyond_got = [lax.ppermute(first_send, "col", moves([3, None, None, 0]))]
-    pairs = jnp.arange(8, dtype=jnp.int32)
-    rows = jnp.where(pairs % 2 == 0, jnp.repeat(mine[5:], 2), pairs // 2)
-    plane_send = stack_rows(pairs % 2, rows, tiles, beside)
-    near = lax.all_to_all(plane_send, "col", split_axis=0, concat_axis=0, axis_index_groups=PLANES, tiled=True)
 
     readers = jnp.concatenate(
         [jnp.where(inner, 4 * plane, 4 * (plane ^ 3)) + (mate ^ flips[1:]),
@@ -227,13 +225,19 @@
     beyond_got += [lax.ppermute(sends[m - 1], "col", moves([3, 1, 2, 0], m)) for m in (1, 2, 3)]
     across_got = [lax.ppermute(sends[m + 3], "col", moves([2, 0, 3, 1], m)) for m in range(4)]
 
-    first_owners = jnp.concatenate([jnp.where(pairs % 2 == 0, 4 * plane, 4 * (plane ^ 1)) + pairs // 2, beyond])
-    mine_in_middle = lookup(me[None], beyond[0])
-    sources = jnp.concatenate([jnp.zeros((8,), jnp.int32), jnp.where(inner & (flips == 0), 1, 2 + flips)])
-    rows = jnp.concatenate([pairs, jnp.where(inner & (flips == 0), mine_in_middle, 0)])
+    near_owners = jnp.concatenate([4 * plane + flips, 4 * (plane ^ 1) + flips])
+    across = 4 * (plane ^ 2) + (mate ^ flips)
+    from_middle = inner & (flips == 0)
+    two, none = flips[:2], 0 * flips
     return [
-        (first_owners, sources, rows, [near, middle, *beyond_got]),
-        (4 * (plane ^ 2) + (mate ^ flips), flips, jnp.zeros_like(flips), across_got),
+        (near_owners, jnp.concatenate([none, none + 1]), jnp.concatenate([flips, flips]), [own, near]),
+        (
+            jnp.concatenate([beyond, across[:2]]),
+            jnp.concatenate([jnp.where(from_middle, 0, 1 + flips), 5 + two]),
+            jnp.concatenate([jnp.where(from_middle, lookup(me[None], beyond[0]), 0), none[:2]]),
+            [middle, *beyond_got, *across_got[:2]],
+        ),
+        (across[2:], two, none[:2], across_got[2:]),
     ]
 
 

time: 151 us -> 144 us (0.954)
  waiting for transfers between devices: 54.9 us -> 43.3 us
  other arithmetic: 10.6 us -> 13.1 us
    ppermute x1, waiting for transfers between devices: 33.8 us -> 7.21 us  [relay(): beside = lax.ppermute(beside_send, 'col', moves([1, 0, 3, 2]))]
    ppermute x4, waiting for transfers between devices: 2.96 us -> 18.2 us  [relay(): lax.ppermute(sends[m + 3], 'col', moves([2, 0, 3, 1], m))]
    all_to_all x1 -> x2, waiting for transfers between devices: 4.06 us -> 13.4 us  [the longest x1 13.4 us: relay(): lax.all_to_all(own_send, 'col', split_axis=0, concat_axis=0, axis_index_g...]
    ppermute x3, waiting for transfers between devices: 12 us -> 3.8 us  [relay(): lax.ppermute(sends[m - 1], 'col', moves([3, 1, 2, 0], m))]
    pallas_call x1 -> x0, Pallas kernels: 4.22 us -> none  [stack_rows(): pl.pallas_call(functools.partial(stack_kernel, total), out_shape=jax.Shap...]
    all_to_all x1 -> x2, starting transfers between devices: 4.65 us -> 8.71 us  [the longest x1 4.37 us: relay(): lax.all_to_all(beside, 'col', split_axis=0, concat_axis=0, axis_index_gro...]
    ppermute x4, starting transfers between devices: 14 us -> 10 us  [relay(): lax.ppermute(sends[m + 3], 'col', moves([2, 0, 3, 1], m))]
    pallas_call x2 -> x3, Pallas kernels: 21.9 us -> 25.2 us  [blocks(): pl.pallas_call(functools.partial(blocks_kernel, total, prior is not None)...]
  transfers between devices with their start and end apart: 12 -> 13, of which waited for: 6 -> 8; matrix products, arithmetic and copies ran while one was open for 8% -> 11% of each run, Pallas kernels for 16% -> 19%
where the time goes in v6:
time: 144 us; the launch traced here: 143 us
  waiting for transfers between devices  43.3 us (30%)
  starting transfers between devices  40.5 us (28%)
  Pallas kernels  32 us (22%)
  local copies, waits for them, and re-layouts  13.7 us (10%)
  other arithmetic  13.1 us (9%)
    pallas_call x3, Pallas kernels, blocks(): pl.pallas_call(functools.partial(blocks_kernel, total, prior is not None)...  25.2 us
    ppermute x4, waiting for transfers between devices, relay(): lax.ppermute(sends[m + 3], 'col', moves([2, 0, 3, 1], m))  18.2 us
    all_to_all x1, waiting for transfers between devices, relay(): lax.all_to_all(own_send, 'col', split_axis=0, concat_axis=0, axis_index_g...  13.4 us
    ppermute x4, starting transfers between devices, relay(): lax.ppermute(sends[m + 3], 'col', moves([2, 0, 3, 1], m))  10 us
    unnamed x41, local copies, waits for them, and re-layouts  8.55 us
    all_to_all x1, starting transfers between devices, local(): notes = lax.all_to_all(note, 'col', split_axis=0, concat_axis=0, tiled=True)  7.39 us
    ppermute x1, waiting for transfers between devices, relay(): beside = lax.ppermute(beside_send, 'col', moves([1, 0, 3, 2]))  7.21 us
    ppermute x3, starting transfers between devices, relay(): lax.ppermute(sends[m - 1], 'col', moves([3, 1, 2, 0], m))  6.34 us
  transfers between devices with their start and end apart: 13, of which 8 were waited for; matrix products, arithmetic and copies ran while one was open for 11% of the time, Pallas kernels for 19%

profile of v6, /device:TPU:0, one launch (start us, length us, event | category | flops | bytes accessed | tf_op | source)
XLA Modules:
  0.0 142.9 jit_solution(10228287990942506065)
XLA Ops:
  0.0 0.8 reshape.139
  0.8 0.7 add_select_fusion
  1.6 0.8 pad_add_fusion
  2.4 0.7 all_to_all.14
  3.0 7.4 %all-to-all-start = ((s32[16,1,896]{2,1,0:T(1,128)}), s32[16,1,896]{2,1,0:T(1,128)S(1)}, u32[]{:S(2)}, u32[]{:S(2)}) async-start(s32[16,1,896]{2,1,0:T(1,128)} %all_to_all.14), calls=%async_computation | async-start | bytes 114688 | tf_op jit(solution)/shard_map/all_to_all | solution.py:261
  10.4 2.1 %collective-permute-start.1 = (bf16[6,12,128,128]{3,2,1,0:T(8,128)(2,1)}, bf16[6,12,128,128]{3,2,1,0:T(8,128)(2,1)}, u32[]{:S(2)}, u32[]{:S(2)}) collective-permute-start(bf16[6,12,128,128]{3,2,1,0:T(8,128)(2,1)} %tiles_ref.9), channel_id=1, source_target_pairs={{4,8},{5,9},{6,10},{7,11},{8,4},{9,5},{10,6},{11,7},{20,24},{21,25... | collective-permute-start | bytes 7077896 | tf_op jit(solution)/shard_map/ppermute | solution.py:263
  12.6 0.7 convert_rsqrt_fusion.1
  16.5 0.7 all-to-all-done
  17.6 1.7 %copy-done = bf16[6,12,128,128]{3,2,1,0:T(8,128)(2,1)S(1)} copy-done((bf16[6,12,128,128]{3,2,1,0:T(8,128)(2,1)S(1)}, bf16[6,12,128,128]{3,2,1,0:T(8,128)(2,1)}, u32[]{:S(2)}) %copy-start) | copy-done | bytes 2359320
  19.3 1.8 %pick_rows.3 = bf16[4,12,128,128]{3,2,1,0:T(8,128)(2,1)} custom-call(s32[4]{0:T(128)S(1)} %bitcast.12, bf16[6,12,128,128]{3,2,1,0:T(8,128)(2,1)S(1)} %copy-done), custom_call_target="tpu_custom_call" | custom-call | tf_op jit(solution)/shard_map/pick_rows/pallas_call | solution.py:27
  21.0 2.6 %collective-permute-start = (bf16[4,12,128,128]{3,2,1,0:T(8,128)(2,1)}, bf16[4,12,128,128]{3,2,1,0:T(8,128)(2,1)}, u32[]{:S(2)}, u32[]{:S(2)}) collective-permute-start(bf16[4,12,128,128]{3,2,1,0:T(8,128)(2,1)} %pick_rows.3), channel_id=1, source_target_pairs={{0,4},{1,5},{2,6},{3,7},{4,0},{5,1},{6,2},{7,3},{8,12},{9,13},{10,... | collective-permute-start | bytes 4718600 | tf_op jit(solution)/shard_map/ppermute | solution.py:213
  23.8 2.1 %pick_rows.2 = (bf16[4,12,128,128]{3,2,1,0:T(8,128)(2,1)S(1)}, bf16[1,12,128,128]{3,2,1,0:T(8,128)(2,1)}) custom-call(s32[5]{0:T(128)S(1)} %slice.44.rows_ref, bf16[6,12,128,128]{3,2,1,0:T(8,128)(2,1)S(1)} %copy-done.1), custom_call_target="tpu_custom_call" | custom-call | tf_op jit(solution)/shard_map/pick_rows/pallas_call | solution.py:27
  25.9 1.1 copy-done.2
  27.1 4.3 %all-to-all-start.1 = ((bf16[4,12,128,128]{3,2,1,0:T(8,128)(2,1)}), bf16[4,12,128,128]{3,2,1,0:T(8,128)(2,1)}, u32[]{:S(2)}, u32[]{:S(2)}) async-start(bf16[4,12,128,128]{3,2,1,0:T(8,128)(2,1)} %copy-done.2), calls=%async_computation.1 | async-start | bytes 3145728 | tf_op jit(solution)/shard_map/all_to_all | solution.py:215
  32.0 0.6 sub.40.place_ref
  33.3 0.6 sub.34.place_ref
  34.3 3.4 %collective-permute-start.2 = (bf16[1,12,128,128]{3,2,1,0:T(8,128)(2,1)}, bf16[1,12,128,128]{3,2,1,0:T(8,128)(2,1)S(1)}, u32[]{:S(2)}, u32[]{:S(2)}) collective-permute-start(bf16[1,12,128,128]{3,2,1,0:T(8,128)(2,1)} %get-tuple-element.19), channel_id=1, source_target_pairs={{0,12},{1,13},{2,14},{3,15},{12,0},{13,1},{14,2},{15,3},{16,28},{1... | collective-permute-start | bytes 1179656 | tf_op jit(solution)/shard_map/ppermute | solution.py:217
  38.2 13.4 %all-to-all-done.1.refs_0_ = bf16[4,12,128,128]{3,2,1,0:T(8,128)(2,1)} async-done(((bf16[4,12,128,128]{3,2,1,0:T(8,128)(2,1)}), bf16[4,12,128,128]{3,2,1,0:T(8,128)(2,1)}, u32[]{:S(2)}, u32[]{:S(2)}) %all-to-all-start.1) | async-done | bytes 1572896 | tf_op jit(solution)/shard_map/all_to_all | solution.py:215
  51.6 7.2 %collective-permute-done = bf16[4,12,128,128]{3,2,1,0:T(8,128)(2,1)} collective-permute-done((bf16[4,12,128,128]{3,2,1,0:T(8,128)(2,1)}, bf16[4,12,128,128]{3,2,1,0:T(8,128)(2,1)}, u32[]{:S(2)}, u32[]{:S(2)}) %collective-permute-start) | collective-permute-done | bytes 1572896 | tf_op jit(solution)/shard_map/ppermute | solution.py:213
  58.8 4.4 %all-to-all-start.2 = ((bf16[4,12,128,128]{3,2,1,0:T(8,128)(2,1)}), bf16[4,12,128,128]{3,2,1,0:T(8,128)(2,1)}, u32[]{:S(2)}, u32[]{:S(2)}) async-start(bf16[4,12,128,128]{3,2,1,0:T(8,128)(2,1)} %collective-permute-done), calls=%async_computation.2 | async-start | bytes 3145728 | tf_op jit(solution)/shard_map/all_to_all | solution.py:216
  63.7 1.4 select_reduce_fusion
  65.0 0.7 fusion.5
  65.8 2.9 %collect.1 = (bf16[1,12,128,128]{3,2,1,0:T(8,128)(2,1)}, bf16[1,12,128,128]{3,2,1,0:T(8,128)(2,1)}, bf16[1,12,128,128]{3,2,1,0:T(8,128)(2,1)S(1)}, bf16[1,12,128...) custom-call(s32[1]{0:T(128)} %bitcast.4.source_ref, ...), custom_call_target="tpu_custom_call" | custom-call | tf_op jit(solution)/shard_map/collect/pallas_call | solution.py:87
  68.6 0.7 copy-done.12
  69.4 0.7 copy-done.13
  70.1 0.8 copy-done.14
  70.9 0.7 copy-done.15
  71.7 0.8 copy-done.16
  72.4 2.2 %collective-permute-start.3 = (bf16[1,12,128,128]{3,2,1,0:T(8,128)(2,1)}, bf16[1,12,128,128]{3,2,1,0:T(8,128)(2,1)S(1)}, u32[]{:S(2)}, u32[]{:S(2)}) collective-permute-start(bf16[1,12,128,128]{3,2,1,0:T(8,128)(2,1)} %get-tuple-element.20), channel_id=1, source_target_pairs={{0,13},{1,12},{2,15},{3,14},{4,5},{5,4},{6,7},{7,6},{8,9},{9,8},{1... | collective-permute-start | bytes 1179656 | tf_op jit(solution)/shard_map/ppermute | solution.py:225
  74.6 2.8 %collective-permute-start.4 = (bf16[1,12,128,128]{3,2,1,0:T(8,128)(2,1)}, bf16[1,12,128,128]{3,2,1,0:T(8,128)(2,1)S(1)}, u32[]{:S(2)}, u32[]{:S(2)}) collective-permute-start(bf16[1,12,128,128]{3,2,1,0:T(8,128)(2,1)} %get-tuple-element.21), channel_id=1, source_target_pairs={{0,14},{1,15},{2,12},{3,13},{4,6},{5,7},{6,4},{7,5},{8,10},{9,11},... | collective-permute-start | bytes 1179656 | tf_op jit(solution)/shard_map/ppermute | solution.py:225
  77.4 0.7 broadcast_select_fusion
  78.7 0.6 broadcast_add_fusion
  79.3 0.9 sub.36.slot_ref
  80.2 1.3 collective-permute-start.5
  81.6 7.4 %collective-permute-start.6 = (bf16[1,12,128,128]{3,2,1,0:T(8,128)(2,1)}, bf16[1,12,128,128]{3,2,1,0:T(8,128)(2,1)}, u32[]{:S(2)}, u32[]{:S(2)}) collective-permute-start(bf16[1,12,128,128]{3,2,1,0:T(8,128)(2,1)} %copy-done.15), channel_id=1, source_target_pairs={{0,8},{1,9},{2,10},{3,11},{4,0},{5,1},{6,2},{7,3},{8,12},{9,13},{1... | collective-permute-start | bytes 1179656 | tf_op jit(solution)/shard_map/ppermute | solution.py:226
  89.0 0.8 select_reduce_fusion.2
  89.8 2.5 %collective-permute-start.8 = (bf16[1,12,128,128]{3,2,1,0:T(8,128)(2,1)}, bf16[1,12,128,128]{3,2,1,0:T(8,128)(2,1)}, u32[]{:S(2)}, u32[]{:S(2)}) collective-permute-start(bf16[1,12,128,128]{3,2,1,0:T(8,128)(2,1)} %copy-done.13), channel_id=1, source_target_pairs={{0,10},{1,11},{2,8},{3,9},{4,2},{5,3},{6,0},{7,1},{8,14},{9,15},{1... | collective-permute-start | bytes 1179656 | tf_op jit(solution)/shard_map/ppermute | solution.py:226
  92.3 3.8 %collective-permute-done.4.refs_4_ = bf16[1,12,128,128]{3,2,1,0:T(8,128)(2,1)S(1)} collective-permute-done((bf16[1,12,128,128]{3,2,1,0:T(8,128)(2,1)}, bf16[1,12,128,128]{3,2,1,0:T(8,128)(2,1)S(1)}, u32[]{:S(2)}, u32[]{:S(2)}) %collective-permute-start.4) | collective-permute-done | bytes 393248 | tf_op jit(solution)/shard_map/ppermute | solution.py:225
  96.2 1.3 select_reduce_fusion.9
  97.5 0.6 copy-done.6
  98.1 0.7 copy-done.7
  98.8 0.6 copy-done.9
  99.4 10.9 %blocks.3.refs_0_ = bf16[6,12,128,128]{3,2,1,0:T(8,128)(2,1)} custom-call(s32[72]{0:T(128)S(1)} %copy-done.6, s32[864]{0:T(1024)S(1)} %sub.36.slot_ref, s32[8]{0:T(128)S(1)} %copy-done.7, s32[8]{0:T(128)S(1)} %copy-done.9, bf16[6,12,128,128]{3,2,1,0:T(8,128)(2,1)S(1)} %copy-done.1, f32[6,1,128]{2,1,0:T(1,128)S(1)} %broadcast_in_dim.263.scale_row_ref, ...), custom_call_target="tpu_custom_call" | custom-call | flops 1811939328 | bytes 5505024 | tf_op jit(solution)/shard_map/blocks/pallas_call | solution.py:161
  110.3 0.9 collective-permute-done.6.refs_6_
  111.3 8.4 %collective-permute-done.7.refs_7_ = bf16[1,12,128,128]{3,2,1,0:T(8,128)(2,1)} collective-permute-done((bf16[1,12,128,128]{3,2,1,0:T(8,128)(2,1)}, bf16[1,12,128,128]{3,2,1,0:T(8,128)(2,1)}, u32[]{:S(2)}, u32[]{:S(2)}) %collective-permute-start.7) | collective-permute-done | bytes 393248 | tf_op jit(solution)/shard_map/ppermute | solution.py:226
  119.6 9.4 %blocks.4.refs_0_ = bf16[6,12,128,128]{3,2,1,0:T(8,128)(2,1)} custom-call(s32[72]{0:T(128)S(1)} %copy-done.5, s32[864]{0:T(1024)S(1)} %sub.36.slot_ref, s32[6]{0:T(128)S(1)} %copy-done.10, s32[6]{0:T(128)S(1)} %copy-done.11, bf16[6,12,128,128]{3,2,1,0:T(8,128)(2,1)S(1)} %copy-done.1, ...), custom_call_target="tpu_custom_call", output_to_operand_aliasing={{}: (7, {})} | custom-call | flops 1358954496 | bytes 4718592 | tf_op jit(solution)/shard_map/blocks/pallas_call | solution.py:161
  129.5 8.4 %collective-permute-done.9.refs_2_ = bf16[1,12,128,128]{3,2,1,0:T(8,128)(2,1)} collective-permute-done((bf16[1,12,128,128]{3,2,1,0:T(8,128)(2,1)}, bf16[1,12,128,128]{3,2,1,0:T(8,128)(2,1)}, u32[]{:S(2)}, u32[]{:S(2)}) %collective-permute-start.9) | collective-permute-done | bytes 393248 | tf_op jit(solution)/shard_map/ppermute | solution.py:226
  137.9 5.0 %blocks.5 = bf16[6,12,128,128]{3,2,1,0:T(8,128)(2,1)} custom-call(s32[72]{0:T(128)S(1)} %copy-done.4, s32[864]{0:T(1024)S(1)} %sub.36.slot_ref, s32[2]{0:T(128)S(1)} %copy-done.8, s32[2]{0:T(128)S(1)} %broadcast_15_row_ref.2.row_ref, bf16[6,12,128,128]{3,2,1,0:T(8,128)(2,1)S(1)} %copy-done.1, ...), custom_call_target="tpu_custom_call", output_to_operand_aliasing={{}: (7, {})} | custom-call | flops 452984832 | bytes 3145728 | tf_op jit(solution)/shard_map/blocks/pallas_call | solution.py:161
  (96 shorter events, 7.7 us)
Async XLA Ops:
  3.0 14.2 %all-to-all-start = ((s32[16,1,896]{2,1,0:T(1,128)}), s32[16,1,896]{2,1,0:T(1,128)S(1)}, u32[]{:S(2)}, u32[]{:S(2)}) async-start(s32[16,1,896]{2,1,0:T(1,128)} %all_to_all.14), calls=%async_computation | async-start | bytes 114688 | tf_op jit(solution)/shard_map/all_to_all | solution.py:261
  10.4 55.3 %collective-permute-start.1 = (bf16[6,12,128,128]{3,2,1,0:T(8,128)(2,1)}, bf16[6,12,128,128]{3,2,1,0:T(8,128)(2,1)}, u32[]{:S(2)}, u32[]{:S(2)}) collective-permute-start(bf16[6,12,128,128]{3,2,1,0:T(8,128)(2,1)} %tiles_ref.9), channel_id=1, source_target_pairs={{4,8},{5,9},{6,10},{7,11},{8,4},{9,5},{10,6},{11,7},{20,24},{21,25... | collective-permute-start | bytes 7077896 | tf_op jit(solution)/shard_map/ppermute | solution.py:263
  17.6 1.7 %copy-start = (bf16[6,12,128,128]{3,2,1,0:T(8,128)(2,1)S(1)}, bf16[6,12,128,128]{3,2,1,0:T(8,128)(2,1)}, u32[]{:S(2)}) copy-start(bf16[6,12,128,128]{3,2,1,0:T(8,128)(2,1)} %tiles_ref.9) | copy-start | bytes 7077892
  19.3 4.6 %copy-start.1 = (bf16[6,12,128,128]{3,2,1,0:T(8,128)(2,1)S(1)}, bf16[6,12,128,128]{3,2,1,0:T(8,128)(2,1)}, u32[]{:S(2)}) copy-start(bf16[6,12,128,128]{3,2,1,0:T(8,128)(2,1)} %tiles_ref.9) | copy-start | bytes 7077892
  21.0 37.8 %collective-permute-start = (bf16[4,12,128,128]{3,2,1,0:T(8,128)(2,1)}, bf16[4,12,128,128]{3,2,1,0:T(8,128)(2,1)}, u32[]{:S(2)}, u32[]{:S(2)}) collective-permute-start(bf16[4,12,128,128]{3,2,1,0:T(8,128)(2,1)} %pick_rows.3), channel_id=1, source_target_pairs={{0,4},{1,5},{2,6},{3,7},{4,0},{5,1},{6,2},{7,3},{8,12},{9,13},{10,... | collective-permute-start | bytes 4718600 | tf_op jit(solution)/shard_map/ppermute | solution.py:213
  23.8 10.1 %copy-start.18 = (s32[6,12]{1,0:T(8,128)S(1)}, s32[6,12]{1,0:T(8,128)}, u32[]{:S(2)}) copy-start(s32[6,12]{1,0:T(8,128)} %param.6) | copy-start | bytes 868
  23.8 10.1 %copy-start.19 = (s32[6]{0:T(128)S(1)}, s32[6]{0:T(128)}, u32[]{:S(2)}) copy-start(s32[6]{0:T(128)} %param.7) | copy-start | bytes 76
  25.9 1.1 copy-start.2
  27.1 24.5 %all-to-all-start.1 = ((bf16[4,12,128,128]{3,2,1,0:T(8,128)(2,1)}), bf16[4,12,128,128]{3,2,1,0:T(8,128)(2,1)}, u32[]{:S(2)}, u32[]{:S(2)}) async-start(bf16[4,12,128,128]{3,2,1,0:T(8,128)(2,1)} %copy-done.2), calls=%async_computation.1 | async-start | bytes 3145728 | tf_op jit(solution)/shard_map/all_to_all | solution.py:215
  34.3 54.7 %collective-permute-start.2 = (bf16[1,12,128,128]{3,2,1,0:T(8,128)(2,1)}, bf16[1,12,128,128]{3,2,1,0:T(8,128)(2,1)S(1)}, u32[]{:S(2)}, u32[]{:S(2)}) collective-permute-start(bf16[1,12,128,128]{3,2,1,0:T(8,128)(2,1)} %get-tuple-element.19), channel_id=1, source_target_pairs={{0,12},{1,13},{2,14},{3,15},{12,0},{13,1},{14,2},{15,3},{16,28},{1... | collective-permute-start | bytes 1179656 | tf_op jit(solution)/shard_map/ppermute | solution.py:217
  38.0 30.7 %copy-start.17 = (f32[16,128]{1,0:T(8,128)}, f32[16,128]{1,0:T(8,128)S(1)}, u32[]{:S(2)}) copy-start(f32[16,128]{1,0:T(8,128)S(1)} %convert_rsqrt_fusion) | copy-start | bytes 24580
  58.8 38.7 %all-to-all-start.2 = ((bf16[4,12,128,128]{3,2,1,0:T(8,128)(2,1)}), bf16[4,12,128,128]{3,2,1,0:T(8,128)(2,1)}, u32[]{:S(2)}, u32[]{:S(2)}) async-start(bf16[4,12,128,128]{3,2,1,0:T(8,128)(2,1)} %collective-permute-done), calls=%async_computation.2 | async-start | bytes 3145728 | tf_op jit(solution)/shard_map/all_to_all | solution.py:216
  68.6 0.8 copy-start.12
  69.4 0.7 copy-start.13
  70.1 0.8 copy-start.14
  70.9 0.7 copy-start.15
  71.7 0.8 copy-start.16
  72.4 17.3 %collective-permute-start.3 = (bf16[1,12,128,128]{3,2,1,0:T(8,128)(2,1)}, bf16[1,12,128,128]{3,2,1,0:T(8,128)(2,1)S(1)}, u32[]{:S(2)}, u32[]{:S(2)}) collective-permute-start(bf16[1,12,128,128]{3,2,1,0:T(8,128)(2,1)} %get-tuple-element.20), channel_id=1, source_target_pairs={{0,13},{1,12},{2,15},{3,14},{4,5},{5,4},{6,7},{7,6},{8,9},{9,8},{1... | collective-permute-start | bytes 1179656 | tf_op jit(solution)/shard_map/ppermute | solution.py:225
  74.6 21.5 %collective-permute-start.4 = (bf16[1,12,128,128]{3,2,1,0:T(8,128)(2,1)}, bf16[1,12,128,128]{3,2,1,0:T(8,128)(2,1)S(1)}, u32[]{:S(2)}, u32[]{:S(2)}) collective-permute-start(bf16[1,12,128,128]{3,2,1,0:T(8,128)(2,1)} %get-tuple-element.21), channel_id=1, source_target_pairs={{0,14},{1,15},{2,12},{3,13},{4,6},{5,7},{6,4},{7,5},{8,10},{9,11},... | collective-permute-start | bytes 1179656 | tf_op jit(solution)/shard_map/ppermute | solution.py:225
  80.2 30.1 %collective-permute-start.5 = (bf16[1,12,128,128]{3,2,1,0:T(8,128)(2,1)}, bf16[1,12,128,128]{3,2,1,0:T(8,128)(2,1)}, u32[]{:S(2)}, u32[]{:S(2)}) collective-permute-start(bf16[1,12,128,128]{3,2,1,0:T(8,128)(2,1)} %copy-done.16), channel_id=1, source_target_pairs={{0,15},{1,14},{2,13},{3,12},{4,7},{5,6},{6,5},{7,4},{8,11},{9,10},... | collective-permute-start | bytes 1179656 | tf_op jit(solution)/shard_map/ppermute | solution.py:225
  81.6 29.7 %collective-permute-start.6 = (bf16[1,12,128,128]{3,2,1,0:T(8,128)(2,1)}, bf16[1,12,128,128]{3,2,1,0:T(8,128)(2,1)}, u32[]{:S(2)}, u32[]{:S(2)}) collective-permute-start(bf16[1,12,128,128]{3,2,1,0:T(8,128)(2,1)} %copy-done.15), channel_id=1, source_target_pairs={{0,8},{1,9},{2,10},{3,11},{4,0},{5,1},{6,2},{7,3},{8,12},{9,13},{1... | collective-permute-start | bytes 1179656 | tf_op jit(solution)/shard_map/ppermute | solution.py:226
  89.0 30.7 %collective-permute-start.7 = (bf16[1,12,128,128]{3,2,1,0:T(8,128)(2,1)}, bf16[1,12,128,128]{3,2,1,0:T(8,128)(2,1)}, u32[]{:S(2)}, u32[]{:S(2)}) collective-permute-start(bf16[1,12,128,128]{3,2,1,0:T(8,128)(2,1)} %copy-done.14), channel_id=1, source_target_pairs={{0,9},{1,8},{2,11},{3,10},{4,1},{5,0},{6,3},{7,2},{8,13},{9,12},{1... | collective-permute-start | bytes 1179656 | tf_op jit(solution)/shard_map/ppermute | solution.py:226
  89.8 39.8 %collective-permute-start.8 = (bf16[1,12,128,128]{3,2,1,0:T(8,128)(2,1)}, bf16[1,12,128,128]{3,2,1,0:T(8,128)(2,1)}, u32[]{:S(2)}, u32[]{:S(2)}) collective-permute-start(bf16[1,12,128,128]{3,2,1,0:T(8,128)(2,1)} %copy-done.13), channel_id=1, source_target_pairs={{0,10},{1,11},{2,8},{3,9},{4,2},{5,3},{6,0},{7,1},{8,14},{9,15},{1... | collective-permute-start | bytes 1179656 | tf_op jit(solution)/shard_map/ppermute | solution.py:226
  96.1 41.8 %collective-permute-start.9 = (bf16[1,12,128,128]{3,2,1,0:T(8,128)(2,1)}, bf16[1,12,128,128]{3,2,1,0:T(8,128)(2,1)}, u32[]{:S(2)}, u32[]{:S(2)}) collective-permute-start(bf16[1,12,128,128]{3,2,1,0:T(8,128)(2,1)} %copy-done.12), channel_id=1, source_target_pairs={{0,11},{1,10},{2,9},{3,8},{4,3},{5,2},{6,1},{7,0},{8,15},{9,14},{1... | collective-permute-start | bytes 1179656 | tf_op jit(solution)/shard_map/ppermute | solution.py:226
  97.5 0.6 copy-start.6
  98.1 0.7 copy-start.7
  98.8 0.6 copy-start.9
  99.4 20.2 %copy-start.5 = (s32[72]{0:T(128)S(1)}, s32[72]{0:T(128)}, u32[]{:S(2)}) copy-start(s32[72]{0:T(128)} %sub.38.place_ref) | copy-start | bytes 868
  99.4 20.2 %copy-start.10 = (s32[6]{0:T(128)S(1)}, s32[6]{0:T(128)}, u32[]{:S(2)}) copy-start(s32[6]{0:T(128)} %pad_add_fusion.2.source_ref) | copy-start | bytes 76
  99.4 20.2 %copy-start.11 = (s32[6]{0:T(128)S(1)}, s32[6]{0:T(128)}, u32[]{:S(2)}) copy-start(s32[6]{0:T(128)} %concatenate.27.row_ref) | copy-start | bytes 76
  110.3 27.6 %copy-start.3 = (f32[2,128]{1,0:T(2,128)S(1)}, f32[2,128]{1,0:T(2,128)}, u32[]{:S(2)}) copy-start(f32[2,128]{1,0:T(2,128)} %select_reduce_fusion.9) | copy-start | bytes 3076
  110.3 27.6 %copy-start.4 = (s32[72]{0:T(128)S(1)}, s32[72]{0:T(128)}, u32[]{:S(2)}) copy-start(s32[72]{0:T(128)} %sub.34.place_ref) | copy-start | bytes 868
  110.3 27.6 %copy-start.8 = (s32[2]{0:T(128)S(1)}, s32[2]{0:T(128)}, u32[]{:S(2)}) copy-start(s32[2]{0:T(128)} %get-tuple-element.33.source_ref) | copy-start | bytes 28

commit v7 on v6

--- a/solution.py
+++ b/solution.py
@@ -12,27 +12,7 @@
 VMEM = pl.BlockSpec(memory_space=pltpu.VMEM)
 HBM = pl.BlockSpec(memory_space=pl.ANY)
 PARAMS = pltpu.CompilerParams(vmem_limit_bytes=VMEM_LIMIT)
-
-
-def pick_rows_kernel(sizes, rows_ref, tiles_ref, *refs):
-    outs, sems = refs[:-1], refs[-1]
-    places = [(ref, k) for ref, size in zip(outs, sizes) for k in range(size)]
-    for at, (ref, k) in enumerate(places):
-        pltpu.make_async_copy(tiles_ref.at[rows_ref[at]], ref.at[k], sems.at[at]).start()
-    for at, (ref, k) in enumerate(places):
-        pltpu.make_async_copy(tiles_ref.at[0], ref.at[k], sems.at[at]).wait()
-
-
-def pick_rows(rows, tiles, sizes):
-    return pl.pallas_call(
-        functools.partial(pick_rows_kernel, sizes),
-        out_shape=[jax.ShapeDtypeStruct((size,) + tiles.shape[1:], tiles.dtype) for size in sizes],
-        in_specs=[SMEM, VMEM],
-        out_specs=[HBM] * len(sizes),
-        scratch_shapes=[pltpu.SemaphoreType.DMA((sum(sizes),))],
-        compiler_params=PARAMS,
-        name="pick_rows",
-    )(rows, tiles)
+WHOLE_VMEM = pltpu.CompilerParams(vmem_limit_bytes=62 * 1024 * 1024)
 
 
 def start_rows(total, source_ref, row_ref, sources, target_ref, sems):
@@ -50,49 +30,37 @@
         pltpu.make_async_copy(sources[0].at[0], target_ref.at[k], sems.at[k]).wait()
 
 
-def stack_kernel(total, source_ref, row_ref, *refs):
-    *sources, out_ref, sems = refs
-    start_rows(total, source_ref, row_ref, sources, out_ref, sems)
-    wait_rows(total, sources, out_ref, sems)
-
-
-def stack_rows(source_ids, row_ids, *sources):
-    total = source_ids.shape[0]
+def move_rows_kernel(sizes, source_ref, row_ref, *refs):
+    *sources, stage_ref, sems, out_sems = refs
+    sources, outs = sources[: -len(sizes)], sources[-len(sizes) :]
+    places = [ref.at[k] for ref, size in zip(outs, sizes) for k in range(size)]
+    start_rows(len(places), source_ref, row_ref, sources, stage_ref, sems)
+    for k, place in enumerate(places):
+        pltpu.make_async_copy(sources[0].at[0], stage_ref.at[k], sems.at[k]).wait()
+        pltpu.make_async_copy(stage_ref.at[k], place, out_sems.at[k]).start()
+    for k, place in enumerate(places):
+        pltpu.make_async_copy(stage_ref.at[k], place, out_sems.at[k]).wait()
+
+
+def move_rows(source_ids, row_ids, sizes, *sources):
+    row, dtype = sources[0].shape[1:], sources[0].dtype
     return pl.pallas_call(
-        functools.partial(stack_kernel, total),
-        out_shape=jax.ShapeDtypeStruct((total,) + sources[0].shape[1:], sources[0].dtype),
+        functools.partial(move_rows_kernel, sizes),
+        out_shape=[jax.ShapeDtypeStruct((size,) + row, dtype) for size in sizes],
         in_specs=[SMEM, SMEM] + [HBM] * len(sources),
-        out_specs=VMEM,
-        scratch_shapes=[pltpu.SemaphoreType.DMA((total,))],
-        compiler_params=PARAMS,
-        name="stack_rows",
+        out_specs=[HBM] * len(sizes),
+        scratch_shapes=[
+            pltpu.VMEM((sum(sizes),) + row, dtype),
+            pltpu.SemaphoreType.DMA((sum(sizes),)),
+            pltpu.SemaphoreType.DMA((sum(sizes),)),
+        ],
+        compiler_params=WHOLE_VMEM,
+        name="move_rows",
     )(source_ids, row_ids, *sources)
 
 
-def collect_kernel(total, source_ref, row_ref, *refs):
-    sources, outs, sems = refs[: -1 - total], refs[-1 - total : -1], refs[-1]
-    for at, ref in enumerate(sources):
-
-        @pl.when(source_ref[0] == at)
-        def _():
-            for k in range(total):
-                pltpu.make_async_copy(ref.at[row_ref[k]], outs[k].at[0], sems.at[k]).start()
-
-    for k in range(total):
-        pltpu.make_async_copy(sources[0].at[0], outs[k].at[0], sems.at[k]).wait()
-
-
-def collect_each(source, rows, *sources):
-    total = rows.shape[0]
-    return pl.pallas_call(
-        functools.partial(collect_kernel, total),
-        out_shape=[jax.ShapeDtypeStruct((1,) + sources[0].shape[1:], sources[0].dtype)] * total,
-        in_specs=[SMEM, SMEM] + [HBM] * len(sources),
-        out_specs=[VMEM] * total,
-        scratch_shapes=[pltpu.SemaphoreType.DMA((total,))],
-        compiler_params=PARAMS,
-        name="collect",
-    )(source[None], rows, *sources)
+def pick_rows(rows, tiles, sizes):
+    return move_rows(jnp.zeros_like(rows), rows, sizes, tiles)
 
 
 def blocks_kernel(total, prior, place_ref, slot_ref, source_ref, row_ref, tiles_ref, scale_row_ref, scale_got_ref, *refs):
@@ -221,7 +189,7 @@
          jnp.where(inner, 4 * (plane ^ 1), 4 * (plane ^ 2)) + (mate ^ flips)]
     )
     rows = lookup(readers, jnp.where(inner, 4 * (plane ^ 3) + mate, me))
-    sends = collect_each(jnp.where(inner, 1, 0), rows, tiles, middle)
+    sends = move_rows(jnp.where(inner, 1, 0) + 0 * rows, rows, (1,) * 7, tiles, middle)
     beyond_got += [lax.ppermute(sends[m - 1], "col", moves([3, 1, 2, 0], m)) for m in (1, 2, 3)]
     across_got = [lax.ppermute(sends[m + 3], "col", moves([2, 0, 3, 1], m)) for m in range(4)]
 
@@ -241,6 +209,38 @@
     ]
 
 
+def note_kernel(peers, candidates_ref, count_ref, cols_ref, degree_ref, out_ref):
+    local_rows, cands = candidates_ref.shape
+    side, slots = degree_ref.shape[1], cols_ref.shape[1]
+    words = out_ref.shape[1] - local_rows
+    lane = lax.broadcasted_iota(jnp.int32, (words, side), 0) * side
+    lane = lane + lax.broadcasted_iota(jnp.int32, (words, side), 1)
+    line = jnp.zeros_like(lane)
+    for i in range(local_rows):
+        for q in range(cands):
+            candidate = candidates_ref[i, q]
+            owner = candidate // local_rows
+            line = jnp.where(lane == owner, candidate - owner * local_rows, line)
+        line = jnp.where(lane == peers + i, count_ref[i], line)
+        for r in range(slots):
+            line = jnp.where(lane == peers + local_rows + i * slots + r, cols_ref[i, r], line)
+    note = jnp.concatenate([degree_ref[...], line], axis=0)
+    for peer in range(peers):
+        out_ref[peer] = note
+
+
+def write_note(candidates, tile_count, tile_cols, degree, peers):
+    local_rows, side = degree.shape
+    words = -(-(peers + local_rows + tile_cols.size) // side)
+    return pl.pallas_call(
+        functools.partial(note_kernel, peers),
+        out_shape=jax.ShapeDtypeStruct((peers, local_rows + words, side), jnp.int32),
+        in_specs=[SMEM, SMEM, SMEM, VMEM],
+        out_specs=VMEM,
+        name="write_note",
+    )(candidates, tile_count, tile_cols, degree)
+
+
 def local(tiles, tile_cols, tile_count, candidates, degree):
     local_rows, slots, side, _ = tiles.shape
     peers = lax.axis_size("col")
@@ -250,24 +250,19 @@
     row_ids = jnp.arange(local_rows, dtype=jnp.int32)
 
     matches = owners[:, :, None] == peer_ids
-    wanted = jnp.max(jnp.where(matches, (candidates % local_rows)[:, :, None], 0), axis=(0, 1))
-
-    note = jnp.concatenate([wanted, tile_count, tile_cols.reshape(-1), degree.reshape(-1)])
-    note = jnp.pad(note, (0, -note.shape[0] % 128))
-    note = jnp.broadcast_to(note, (peers, note.shape[0]))
+    note = write_note(candidates, tile_count, tile_cols, degree, peers)
+    notes = lax.all_to_all(note, "col", split_axis=0, concat_axis=0, tiled=True)
     relayed = peers == 16
     if relayed:
-        tiles_behind, note = lax.optimization_barrier((tiles, note))
-    notes = lax.all_to_all(note, "col", split_axis=0, concat_axis=0, tiled=True)
-    if relayed:
-        middle = lax.ppermute(tiles_behind, "col", moves([None, 2, 1, None]))
+        middle = lax.ppermute(tiles, "col", moves([None, 2, 1, None]))
+    degree_all = notes[:, :local_rows]
+    notes = notes[:, local_rows:].reshape(peers, -1)
+    wanted = jnp.max(jnp.where(matches, (candidates % local_rows)[:, :, None], 0), axis=(0, 1))
     wanted_by = notes[:, :peers]
     at = peers
     counts_all = notes[:, at : at + local_rows]
     at += local_rows
     cols_all = notes[:, at : at + local_rows * slots].reshape(peers, local_rows, slots)
-    at += local_rows * slots
-    degree_all = notes[:, at : at + local_rows * side].reshape(peers, local_rows, side)
 
     mine = wanted[:, None] == row_ids
     count_got = jnp.sum(jnp.where(mine, counts_all, 0), axis=1)

time: 144 us -> 142 us (0.986)
  local copies, waits for them, and re-layouts: 13.7 us -> 4.97 us
  waiting for transfers between devices: 43.3 us -> 51.5 us
  Pallas kernels: 32 us -> 37.6 us
  starting transfers between devices: 40.5 us -> 36.6 us
  other arithmetic: 13.1 us -> 10.5 us
    unnamed x41 -> x20, local copies, waits for them, and re-layouts: 8.55 us -> 2.31 us
    pallas_call x3 -> x4, Pallas kernels: 6.71 us -> 12.3 us  [the longest x3 10.5 us: move_rows(): pl.pallas_call(functools.partial(move_rows_kernel, sizes), out_shape=[jax...]
    ppermute x3, waiting for transfers between devices: 3.8 us -> 7.95 us  [relay(): lax.ppermute(sends[m - 1], 'col', moves([3, 1, 2, 0], m))]
    ppermute x4, starting transfers between devices: 10 us -> 7.61 us  [relay(): lax.ppermute(sends[m + 3], 'col', moves([2, 0, 3, 1], m))]
    all_to_all x1, waiting for transfers between devices: 13.4 us -> 15.8 us  [relay(): lax.all_to_all(own_send, 'col', split_axis=0, concat_axis=0, axis_index_g...]
    reduce_sum x3, other arithmetic: 2.19 us -> 0.27 us  [local(): jnp.sum(jnp.where((owner_ids[:, None] == peer_ids)[:, :, None], scale_oth...]
    sub x3, local copies, waits for them, and re-layouts: 1.85 us -> 0.23 us  [local(): jnp.sum(jnp.where(owners[:, :, None] == owner_ids, at + 1, 0), axis=2) - 1]
    ppermute x4, waiting for transfers between devices: 18.2 us -> 19.6 us  [relay(): lax.ppermute(sends[m + 3], 'col', moves([2, 0, 3, 1], m))]
  transfers between devices with their start and end apart: 13 -> 13, of which waited for: 8 -> 8; matrix products, arithmetic and copies ran while one was open for 11% -> 9% of each run, Pallas kernels for 19% -> 22%
where the time goes in v7:
time: 142 us
  waiting for transfers between devices  51.5 us (36%)
  Pallas kernels  37.6 us (26%)
  starting transfers between devices  36.6 us (26%)
  other arithmetic  10.5 us (7%)
  local copies, waits for them, and re-layouts  4.97 us (4%)
    pallas_call x3, Pallas kernels, blocks(): pl.pallas_call(functools.partial(blocks_kernel, total, prior is not None)...  25.3 us
    ppermute x4, waiting for transfers between devices, relay(): lax.ppermute(sends[m + 3], 'col', moves([2, 0, 3, 1], m))  19.6 us
    all_to_all x1, waiting for transfers between devices, relay(): lax.all_to_all(own_send, 'col', split_axis=0, concat_axis=0, axis_index_g...  15.8 us
    pallas_call x3, Pallas kernels, move_rows(): pl.pallas_call(functools.partial(move_rows_kernel, sizes), out_shape=[jax...  10.5 us
    ppermute x3, waiting for transfers between devices, relay(): lax.ppermute(sends[m - 1], 'col', moves([3, 1, 2, 0], m))  7.95 us
    ppermute x4, starting transfers between devices, relay(): lax.ppermute(sends[m + 3], 'col', moves([2, 0, 3, 1], m))  7.61 us
    all_to_all x1, starting transfers between devices, local(): notes = lax.all_to_all(note, 'col', split_axis=0, concat_axis=0, tiled=True)  7.39 us
    ppermute x3, starting transfers between devices, relay(): lax.ppermute(sends[m - 1], 'col', moves([3, 1, 2, 0], m))  6.79 us
  transfers between devices with their start and end apart: 13, of which 8 were waited for; matrix products, arithmetic and copies ran while one was open for 9% of the time, Pallas kernels for 22%

profile of v7, /device:TPU:0, one launch (start us, length us, event | category | flops | bytes accessed | tf_op | source)
XLA Modules:
  0.0 141.6 jit_solution(9498067554199441682)
XLA Ops:
  0.0 1.9 %write_note.1 = s32[16,7,128]{2,1,0:T(8,128)} custom-call(s32[6,12]{1,0:T(8,128)} %candidates_ref.1, s32[6]{0:T(128)} %count_ref.1, s32[6,12]{1,0:T(8,128)} %cols_ref.1, s32[6,128]{1,0:T(8,128)} %degree_ref.1), custom_call_target="tpu_custom_call" | custom-call | tf_op jit(solution)/shard_map/write_note/pallas_call | solution.py:235
  1.9 7.4 %all-to-all-start = ((s32[16,7,128]{2,1,0:T(8,128)}), s32[16,7,128]{2,1,0:T(8,128)S(1)}, u32[]{:S(2)}, u32[]{:S(2)}) async-start(s32[16,7,128]{2,1,0:T(8,128)} %write_note.1), calls=%async_computation | async-start | bytes 131072 | tf_op jit(solution)/shard_map/all_to_all | solution.py:254
  9.3 2.1 %collective-permute-start.1 = (bf16[6,12,128,128]{3,2,1,0:T(8,128)(2,1)}, bf16[6,12,128,128]{3,2,1,0:T(8,128)(2,1)}, u32[]{:S(2)}, u32[]{:S(2)}) collective-permute-start(bf16[6,12,128,128]{3,2,1,0:T(8,128)(2,1)} %tiles_ref.5), channel_id=1, source_target_pairs={{4,8},{5,9},{6,10},{7,11},{8,4},{9,5},{10,6},{11,7},{20,24},{21,25... | collective-permute-start | bytes 7077896 | tf_op jit(solution)/shard_map/ppermute | solution.py:257
  11.4 0.7 convert_rsqrt_fusion.1
  12.1 0.7 add_select_fusion
  12.9 0.1 pad_add_fusion.4
  13.4 0.1 select_reduce_fusion.5
  14.1 2.1 %all-to-all-done = s32[16,7,128]{2,1,0:T(8,128)S(1)} async-done(((s32[16,7,128]{2,1,0:T(8,128)}), s32[16,7,128]{2,1,0:T(8,128)S(1)}, u32[]{:S(2)}, u32[]{:S(2)}) %all-to-all-start) | async-done | bytes 57376 | tf_op jit(solution)/shard_map/all_to_all | solution.py:254
  16.2 0.6 copy-done.2
  16.8 0.7 select_reduce_fusion.9
  17.5 0.7 select_reduce_fusion.10
  18.2 0.5 broadcast_20_source_ref.2.source_ref
  18.7 2.9 %move_rows.4 = bf16[4,12,128,128]{3,2,1,0:T(8,128)(2,1)} custom-call(s32[4]{0:T(128)} %broadcast_20_source_ref.2.source_ref, s32[4]{0:T(128)} %bitcast.13, bf16[6,12,128,128]{3,2,1,0:T(8,128)(2,1)} %tiles_ref.5), custom_call_target="tpu_custom_call" | custom-call | tf_op jit(solution)/shard_map/move_rows/pallas_call | solution.py:47
  21.6 1.6 %collective-permute-start = (bf16[4,12,128,128]{3,2,1,0:T(8,128)(2,1)}, bf16[4,12,128,128]{3,2,1,0:T(8,128)(2,1)}, u32[]{:S(2)}, u32[]{:S(2)}) collective-permute-start(bf16[4,12,128,128]{3,2,1,0:T(8,128)(2,1)} %move_rows.4), channel_id=1, source_target_pairs={{0,4},{1,5},{2,6},{3,7},{4,0},{5,1},{6,2},{7,3},{8,12},{9,13},{10,... | collective-permute-start | bytes 4718600 | tf_op jit(solution)/shard_map/ppermute | solution.py:181
  23.2 0.6 pad_add_fusion.5
  23.8 0.6 slice.48.row_ref
  24.4 0.5 broadcast_19_source_ref.2.source_ref
  24.9 3.6 %move_rows.3 = (bf16[4,12,128,128]{3,2,1,0:T(8,128)(2,1)}, bf16[1,12,128,128]{3,2,1,0:T(8,128)(2,1)}) custom-call(s32[5]{0:T(128)} %broadcast_19_source_ref.2.source_ref, s32[5]{0:T(128)} %slice.48.row_ref, bf16[6,12,128,128]{3,2,1,0:T(8,128)(2,1)} %tiles_ref.5), custom_call_target="tpu_custom_call" | custom-call | tf_op jit(solution)/shard_map/move_rows/pallas_call | solution.py:47
  28.5 3.7 %all-to-all-start.1 = ((bf16[4,12,128,128]{3,2,1,0:T(8,128)(2,1)}), bf16[4,12,128,128]{3,2,1,0:T(8,128)(2,1)S(1)}, u32[]{:S(2)}, u32[]{:S(2)}) async-start(bf16[4,12,128,128]{3,2,1,0:T(8,128)(2,1)} %get-tuple-element.14), calls=%async_computation.1 | async-start | bytes 3145728 | tf_op jit(solution)/shard_map/all_to_all | solution.py:183
  32.9 3.1 %collective-permute-start.2 = (bf16[1,12,128,128]{3,2,1,0:T(8,128)(2,1)}, bf16[1,12,128,128]{3,2,1,0:T(8,128)(2,1)S(1)}, u32[]{:S(2)}, u32[]{:S(2)}) collective-permute-start(bf16[1,12,128,128]{3,2,1,0:T(8,128)(2,1)} %get-tuple-element.15), channel_id=1, source_target_pairs={{0,12},{1,13},{2,14},{3,15},{12,0},{13,1},{14,2},{15,3},{16,28},{1... | collective-permute-start | bytes 1179656 | tf_op jit(solution)/shard_map/ppermute | solution.py:185
  36.0 0.2 fusion.1
  36.2 0.1 fusion
  36.4 0.1 select_reduce_fusion.3
  36.5 15.8 %all-to-all-done.1.refs_0_ = bf16[4,12,128,128]{3,2,1,0:T(8,128)(2,1)S(1)} async-done(((bf16[4,12,128,128]{3,2,1,0:T(8,128)(2,1)}), bf16[4,12,128,128]{3,2,1,0:T(8,128)(2,1)S(1)}, u32[]{:S(2)}, u32[]{:S(2)}) %all-to-all-start.1) | async-done | bytes 1572896 | tf_op jit(solution)/shard_map/all_to_all | solution.py:183
  52.3 6.0 %collective-permute-done = bf16[4,12,128,128]{3,2,1,0:T(8,128)(2,1)} collective-permute-done((bf16[4,12,128,128]{3,2,1,0:T(8,128)(2,1)}, bf16[4,12,128,128]{3,2,1,0:T(8,128)(2,1)}, u32[]{:S(2)}, u32[]{:S(2)}) %collective-permute-start) | collective-permute-done | bytes 1572896 | tf_op jit(solution)/shard_map/ppermute | solution.py:181
  58.3 4.3 %all-to-all-start.2 = ((bf16[4,12,128,128]{3,2,1,0:T(8,128)(2,1)}), bf16[4,12,128,128]{3,2,1,0:T(8,128)(2,1)}, u32[]{:S(2)}, u32[]{:S(2)}) async-start(bf16[4,12,128,128]{3,2,1,0:T(8,128)(2,1)} %collective-permute-done), calls=%async_computation.2 | async-start | bytes 3145728 | tf_op jit(solution)/shard_map/all_to_all | solution.py:184
  62.6 0.7 select_reduce_fusion.13.row_ref
  63.4 0.3 select_reduce_fusion.1
  63.7 2.0 %select_reduce_fusion = s32[6,12,12]{2,1,0:T(8,128)} fusion(s32[12]{0:T(128)S(1)} %iota_add_fusion.4, s32[6,12,12]{2,1,0:T(8,128)S(1)} %select_reduce_fusion.1, s32[6,12]{1,0:T(8,128)S(1)} %fusion.5), kind=kLoop, calls=%fused_computation | loop fusion | flops 30240 | bytes 7248 | tf_op jit(solution)/shard_map/reduce_sum | solution.py:276
  65.7 0.6 fusion.6
  66.3 0.5 add.106.source_ref
  66.9 4.0 %move_rows.5 = (bf16[1,12,128,128]{3,2,1,0:T(8,128)(2,1)}, bf16[1,12,128,128]{3,2,1,0:T(8,128)(2,1)}, bf16[1,12,128,128]{3,2,1,0:T(8,128)(2,1)}, bf16[1,12,128,1...) custom-call(s32[7]{0:T(128)} %add.106.source_ref, ...), custom_call_target="tpu_custom_call" | custom-call | tf_op jit(solution)/shard_map/move_rows/pallas_call | solution.py:47
  70.9 2.6 %collective-permute-start.3 = (bf16[1,12,128,128]{3,2,1,0:T(8,128)(2,1)}, bf16[1,12,128,128]{3,2,1,0:T(8,128)(2,1)S(1)}, u32[]{:S(2)}, u32[]{:S(2)}) collective-permute-start(bf16[1,12,128,128]{3,2,1,0:T(8,128)(2,1)} %get-tuple-element.16), channel_id=1, source_target_pairs={{0,13},{1,12},{2,15},{3,14},{4,5},{5,4},{6,7},{7,6},{8,9},{9,8},{1... | collective-permute-start | bytes 1179656 | tf_op jit(solution)/shard_map/ppermute | solution.py:193
  73.5 2.8 %collective-permute-start.4 = (bf16[1,12,128,128]{3,2,1,0:T(8,128)(2,1)}, bf16[1,12,128,128]{3,2,1,0:T(8,128)(2,1)S(1)}, u32[]{:S(2)}, u32[]{:S(2)}) collective-permute-start(bf16[1,12,128,128]{3,2,1,0:T(8,128)(2,1)} %get-tuple-element.17), channel_id=1, source_target_pairs={{0,14},{1,15},{2,12},{3,13},{4,6},{5,7},{6,4},{7,5},{8,10},{9,11},... | collective-permute-start | bytes 1179656 | tf_op jit(solution)/shard_map/ppermute | solution.py:193
  76.2 0.6 broadcast_select_fusion
  76.8 0.8 broadcast_add_fusion
  77.7 1.4 %collective-permute-start.5 = (bf16[1,12,128,128]{3,2,1,0:T(8,128)(2,1)}, bf16[1,12,128,128]{3,2,1,0:T(8,128)(2,1)S(1)}, u32[]{:S(2)}, u32[]{:S(2)}) collective-permute-start(bf16[1,12,128,128]{3,2,1,0:T(8,128)(2,1)} %get-tuple-element.18), channel_id=1, source_target_pairs={{0,15},{1,14},{2,13},{3,12},{4,7},{5,6},{6,5},{7,4},{8,11},{9,10},... | collective-permute-start | bytes 1179656 | tf_op jit(solution)/shard_map/ppermute | solution.py:193
  79.2 4.9 %collective-permute-start.6 = (bf16[1,12,128,128]{3,2,1,0:T(8,128)(2,1)}, bf16[1,12,128,128]{3,2,1,0:T(8,128)(2,1)}, u32[]{:S(2)}, u32[]{:S(2)}) collective-permute-start(bf16[1,12,128,128]{3,2,1,0:T(8,128)(2,1)} %get-tuple-element.19), channel_id=1, source_target_pairs={{0,8},{1,9},{2,10},{3,11},{4,0},{5,1},{6,2},{7,3},{8,12},{9,13},{1... | collective-permute-start | bytes 1179656 | tf_op jit(solution)/shard_map/ppermute | solution.py:194
  84.2 2.7 %collective-permute-start.8 = (bf16[1,12,128,128]{3,2,1,0:T(8,128)(2,1)}, bf16[1,12,128,128]{3,2,1,0:T(8,128)(2,1)}, u32[]{:S(2)}, u32[]{:S(2)}) collective-permute-start(bf16[1,12,128,128]{3,2,1,0:T(8,128)(2,1)} %get-tuple-element.21), channel_id=1, source_target_pairs={{0,10},{1,11},{2,8},{3,9},{4,2},{5,3},{6,0},{7,1},{8,14},{9,15},{1... | collective-permute-start | bytes 1179656 | tf_op jit(solution)/shard_map/ppermute | solution.py:194
  86.9 7.9 %collective-permute-done.4.refs_4_ = bf16[1,12,128,128]{3,2,1,0:T(8,128)(2,1)S(1)} collective-permute-done((bf16[1,12,128,128]{3,2,1,0:T(8,128)(2,1)}, bf16[1,12,128,128]{3,2,1,0:T(8,128)(2,1)S(1)}, u32[]{:S(2)}, u32[]{:S(2)}) %collective-permute-start.4) | collective-permute-done | bytes 393248 | tf_op jit(solution)/shard_map/ppermute | solution.py:193
  95.0 1.7 %copy-done = bf16[6,12,128,128]{3,2,1,0:T(8,128)(2,1)S(1)} copy-done((bf16[6,12,128,128]{3,2,1,0:T(8,128)(2,1)S(1)}, bf16[6,12,128,128]{3,2,1,0:T(8,128)(2,1)}, u32[]{:S(2)}) %copy-start) | copy-done | bytes 2359320
  96.6 11.2 %blocks.3.refs_0_ = bf16[6,12,128,128]{3,2,1,0:T(8,128)(2,1)} custom-call(s32[72]{0:T(128)S(1)} %sub.40.place_ref, s32[864]{0:T(1024)S(1)} %sub.36.slot_ref, s32[8]{0:T(128)S(1)} %copy-done.1, s32[8]{0:T(128)S(1)} %pad_add_fusion.3.row_ref, bf16[6,12,128,128]{3,2,1,0:T(8,128)(2,1)S(1)} %copy-done, f32[6,1,128]{2,1,0:T(1,128)S(1)} %broadcast_in_dim.256.scale_row_ref, ...), custom_call_target="tpu_custom_call" | custom-call | flops 1811939328 | bytes 5505024 | tf_op jit(solution)/shard_map/blocks/pallas_call | solution.py:129
  107.8 1.9 %collective-permute-done.6.refs_6_ = bf16[1,12,128,128]{3,2,1,0:T(8,128)(2,1)} collective-permute-done((bf16[1,12,128,128]{3,2,1,0:T(8,128)(2,1)}, bf16[1,12,128,128]{3,2,1,0:T(8,128)(2,1)}, u32[]{:S(2)}, u32[]{:S(2)}) %collective-permute-start.6) | collective-permute-done | bytes 393248 | tf_op jit(solution)/shard_map/ppermute | solution.py:194
  109.8 8.4 %collective-permute-done.7.refs_7_ = bf16[1,12,128,128]{3,2,1,0:T(8,128)(2,1)} collective-permute-done((bf16[1,12,128,128]{3,2,1,0:T(8,128)(2,1)}, bf16[1,12,128,128]{3,2,1,0:T(8,128)(2,1)}, u32[]{:S(2)}, u32[]{:S(2)}) %collective-permute-start.7) | collective-permute-done | bytes 393248 | tf_op jit(solution)/shard_map/ppermute | solution.py:194
  118.1 9.1 %blocks.4.refs_0_ = bf16[6,12,128,128]{3,2,1,0:T(8,128)(2,1)} custom-call(s32[72]{0:T(128)S(1)} %sub.38.place_ref, s32[864]{0:T(1024)S(1)} %sub.36.slot_ref, s32[6]{0:T(128)S(1)} %pad_add_fusion.1.source_ref, s32[6]{0:T(128)S(1)} %concatenate.23.row_ref, bf16[6,12,128,128]{3,2,1,0:T(8,128)(2,1)S(1)} %copy-done, ...), custom_call_target="tpu_custom_call", output_to_operand_aliasing={{}: (7, {})} | custom-call | flops 1358954496 | bytes 4718592 | tf_op jit(solution)/shard_map/blocks/pallas_call | solution.py:129
  127.3 1.0 collective-permute-done.8.refs_1_
  128.2 8.4 %collective-permute-done.9.refs_2_ = bf16[1,12,128,128]{3,2,1,0:T(8,128)(2,1)} collective-permute-done((bf16[1,12,128,128]{3,2,1,0:T(8,128)(2,1)}, bf16[1,12,128,128]{3,2,1,0:T(8,128)(2,1)}, u32[]{:S(2)}, u32[]{:S(2)}) %collective-permute-start.9) | collective-permute-done | bytes 393248 | tf_op jit(solution)/shard_map/ppermute | solution.py:194
  136.6 5.0 %blocks.5 = bf16[6,12,128,128]{3,2,1,0:T(8,128)(2,1)} custom-call(s32[72]{0:T(128)S(1)} %sub.34.place_ref, s32[864]{0:T(1024)S(1)} %sub.36.slot_ref, s32[2]{0:T(128)S(1)} %get-tuple-element.29.source_ref, s32[2]{0:T(128)S(1)} %broadcast_16_row_ref.2.row_ref, bf16[6,12,128,128]{3,2,1,0:T(8,128)(2,1)S(1)} %copy-done, ...), custom_call_target="tpu_custom_call", output_to_operand_aliasing={{}: (7, {})} | custom-call | flops 452984832 | bytes 3145728 | tf_op jit(solution)/shard_map/blocks/pallas_call | solution.py:129
  (72 shorter events, 2.2 us)
Async XLA Ops:
  1.9 14.3 %all-to-all-start = ((s32[16,7,128]{2,1,0:T(8,128)}), s32[16,7,128]{2,1,0:T(8,128)S(1)}, u32[]{:S(2)}, u32[]{:S(2)}) async-start(s32[16,7,128]{2,1,0:T(8,128)} %write_note.1), calls=%async_computation | async-start | bytes 131072 | tf_op jit(solution)/shard_map/all_to_all | solution.py:254
  9.3 57.1 %collective-permute-start.1 = (bf16[6,12,128,128]{3,2,1,0:T(8,128)(2,1)}, bf16[6,12,128,128]{3,2,1,0:T(8,128)(2,1)}, u32[]{:S(2)}, u32[]{:S(2)}) collective-permute-start(bf16[6,12,128,128]{3,2,1,0:T(8,128)(2,1)} %tiles_ref.5), channel_id=1, source_target_pairs={{4,8},{5,9},{6,10},{7,11},{8,4},{9,5},{10,6},{11,7},{20,24},{21,25... | collective-permute-start | bytes 7077896 | tf_op jit(solution)/shard_map/ppermute | solution.py:257
  16.2 0.6 copy-start.2
  18.2 5.6 %copy-start.6 = (s32[9]{0:T(128)S(1)}, s32[9]{0:T(128)}, u32[]{:S(2)}) copy-start(s32[9]{0:T(128)} %select_reduce_fusion.10) | copy-start | bytes 112
  21.6 36.7 %collective-permute-start = (bf16[4,12,128,128]{3,2,1,0:T(8,128)(2,1)}, bf16[4,12,128,128]{3,2,1,0:T(8,128)(2,1)}, u32[]{:S(2)}, u32[]{:S(2)}) collective-permute-start(bf16[4,12,128,128]{3,2,1,0:T(8,128)(2,1)} %move_rows.4), channel_id=1, source_target_pairs={{0,4},{1,5},{2,6},{3,7},{4,0},{5,1},{6,2},{7,3},{8,12},{9,13},{10,... | collective-permute-start | bytes 4718600 | tf_op jit(solution)/shard_map/ppermute | solution.py:181
  24.9 7.6 %copy-start.4 = (s32[6,12]{1,0:T(8,128)S(1)}, s32[6,12]{1,0:T(8,128)}, u32[]{:S(2)}) copy-start(s32[6,12]{1,0:T(8,128)} %cols_ref.1) | copy-start | bytes 868
  24.9 7.7 %copy-start.5 = (s32[6]{0:T(128)S(1)}, s32[6]{0:T(128)}, u32[]{:S(2)}) copy-start(s32[6]{0:T(128)} %count_ref.1) | copy-start | bytes 76
  28.5 7.7 %copy-start.3 = (s32[16,7,128]{2,1,0:T(8,128)S(1)}, s32[16,7,128]{2,1,0:T(8,128)}, u32[]{:S(2)}) copy-start(s32[16,7,128]{2,1,0:T(8,128)} %copy-done.2) | copy-start | bytes 172036
  28.5 23.8 %all-to-all-start.1 = ((bf16[4,12,128,128]{3,2,1,0:T(8,128)(2,1)}), bf16[4,12,128,128]{3,2,1,0:T(8,128)(2,1)S(1)}, u32[]{:S(2)}, u32[]{:S(2)}) async-start(bf16[4,12,128,128]{3,2,1,0:T(8,128)(2,1)} %get-tuple-element.14), calls=%async_computation.1 | async-start | bytes 3145728 | tf_op jit(solution)/shard_map/all_to_all | solution.py:183
  32.2 30.4 %copy-start.8 = (s32[16]{0:T(128)S(1)}, s32[16]{0:T(128)}, u32[]{:S(2)}) copy-start(s32[16]{0:T(128)} %get-tuple-element.23) | copy-start | bytes 196
  32.2 30.4 %copy-start.9 = (s32[7]{0:T(128)S(1)}, s32[7]{0:T(128)}, u32[]{:S(2)}) copy-start(s32[7]{0:T(128)} %pad_add_fusion.5) | copy-start | bytes 88
  32.2 33.5 %copy-start.7 = (s32[16]{0:T(128)S(1)}, s32[16]{0:T(128)}, u32[]{:S(2)}) copy-start(s32[16]{0:T(128)} %get-tuple-element.25) | copy-start | bytes 196
  32.9 51.2 %collective-permute-start.2 = (bf16[1,12,128,128]{3,2,1,0:T(8,128)(2,1)}, bf16[1,12,128,128]{3,2,1,0:T(8,128)(2,1)S(1)}, u32[]{:S(2)}, u32[]{:S(2)}) collective-permute-start(bf16[1,12,128,128]{3,2,1,0:T(8,128)(2,1)} %get-tuple-element.15), channel_id=1, source_target_pairs={{0,12},{1,13},{2,14},{3,15},{12,0},{13,1},{14,2},{15,3},{16,28},{1... | collective-permute-start | bytes 1179656 | tf_op jit(solution)/shard_map/ppermute | solution.py:185
  58.3 36.7 %all-to-all-start.2 = ((bf16[4,12,128,128]{3,2,1,0:T(8,128)(2,1)}), bf16[4,12,128,128]{3,2,1,0:T(8,128)(2,1)}, u32[]{:S(2)}, u32[]{:S(2)}) async-start(bf16[4,12,128,128]{3,2,1,0:T(8,128)(2,1)} %collective-permute-done), calls=%async_computation.2 | async-start | bytes 3145728 | tf_op jit(solution)/shard_map/all_to_all | solution.py:184
  66.9 28.1 %copy-start.1 = (s32[8]{0:T(128)S(1)}, s32[8]{0:T(128)}, u32[]{:S(2)}) copy-start(s32[8]{0:T(128)} %constant.75.clone.1.source_ref) | copy-start | bytes 100
  70.9 13.3 %collective-permute-start.3 = (bf16[1,12,128,128]{3,2,1,0:T(8,128)(2,1)}, bf16[1,12,128,128]{3,2,1,0:T(8,128)(2,1)S(1)}, u32[]{:S(2)}, u32[]{:S(2)}) collective-permute-start(bf16[1,12,128,128]{3,2,1,0:T(8,128)(2,1)} %get-tuple-element.16), channel_id=1, source_target_pairs={{0,13},{1,12},{2,15},{3,14},{4,5},{5,4},{6,7},{7,6},{8,9},{9,8},{1... | collective-permute-start | bytes 1179656 | tf_op jit(solution)/shard_map/ppermute | solution.py:193
  73.5 21.4 %collective-permute-start.4 = (bf16[1,12,128,128]{3,2,1,0:T(8,128)(2,1)}, bf16[1,12,128,128]{3,2,1,0:T(8,128)(2,1)S(1)}, u32[]{:S(2)}, u32[]{:S(2)}) collective-permute-start(bf16[1,12,128,128]{3,2,1,0:T(8,128)(2,1)} %get-tuple-element.17), channel_id=1, source_target_pairs={{0,14},{1,15},{2,12},{3,13},{4,6},{5,7},{6,4},{7,5},{8,10},{9,11},... | collective-permute-start | bytes 1179656 | tf_op jit(solution)/shard_map/ppermute | solution.py:193
  77.7 30.1 %collective-permute-start.5 = (bf16[1,12,128,128]{3,2,1,0:T(8,128)(2,1)}, bf16[1,12,128,128]{3,2,1,0:T(8,128)(2,1)S(1)}, u32[]{:S(2)}, u32[]{:S(2)}) collective-permute-start(bf16[1,12,128,128]{3,2,1,0:T(8,128)(2,1)} %get-tuple-element.18), channel_id=1, source_target_pairs={{0,15},{1,14},{2,13},{3,12},{4,7},{5,6},{6,5},{7,4},{8,11},{9,10},... | collective-permute-start | bytes 1179656 | tf_op jit(solution)/shard_map/ppermute | solution.py:193
  79.2 30.6 %collective-permute-start.6 = (bf16[1,12,128,128]{3,2,1,0:T(8,128)(2,1)}, bf16[1,12,128,128]{3,2,1,0:T(8,128)(2,1)}, u32[]{:S(2)}, u32[]{:S(2)}) collective-permute-start(bf16[1,12,128,128]{3,2,1,0:T(8,128)(2,1)} %get-tuple-element.19), channel_id=1, source_target_pairs={{0,8},{1,9},{2,10},{3,11},{4,0},{5,1},{6,2},{7,3},{8,12},{9,13},{1... | collective-permute-start | bytes 1179656 | tf_op jit(solution)/shard_map/ppermute | solution.py:194
  84.1 34.0 %collective-permute-start.7 = (bf16[1,12,128,128]{3,2,1,0:T(8,128)(2,1)}, bf16[1,12,128,128]{3,2,1,0:T(8,128)(2,1)}, u32[]{:S(2)}, u32[]{:S(2)}) collective-permute-start(bf16[1,12,128,128]{3,2,1,0:T(8,128)(2,1)} %get-tuple-element.20), channel_id=1, source_target_pairs={{0,9},{1,8},{2,11},{3,10},{4,1},{5,0},{6,3},{7,2},{8,13},{9,12},{1... | collective-permute-start | bytes 1179656 | tf_op jit(solution)/shard_map/ppermute | solution.py:194
  84.2 44.0 %collective-permute-start.8 = (bf16[1,12,128,128]{3,2,1,0:T(8,128)(2,1)}, bf16[1,12,128,128]{3,2,1,0:T(8,128)(2,1)}, u32[]{:S(2)}, u32[]{:S(2)}) collective-permute-start(bf16[1,12,128,128]{3,2,1,0:T(8,128)(2,1)} %get-tuple-element.21), channel_id=1, source_target_pairs={{0,10},{1,11},{2,8},{3,9},{4,2},{5,3},{6,0},{7,1},{8,14},{9,15},{1... | collective-permute-start | bytes 1179656 | tf_op jit(solution)/shard_map/ppermute | solution.py:194
  94.8 41.8 %collective-permute-start.9 = (bf16[1,12,128,128]{3,2,1,0:T(8,128)(2,1)}, bf16[1,12,128,128]{3,2,1,0:T(8,128)(2,1)}, u32[]{:S(2)}, u32[]{:S(2)}) collective-permute-start(bf16[1,12,128,128]{3,2,1,0:T(8,128)(2,1)} %get-tuple-element.22), channel_id=1, source_target_pairs={{0,11},{1,10},{2,9},{3,8},{4,3},{5,2},{6,1},{7,0},{8,15},{9,14},{1... | collective-permute-start | bytes 1179656 | tf_op jit(solution)/shard_map/ppermute | solution.py:194
  94.9 1.7 %copy-start = (bf16[6,12,128,128]{3,2,1,0:T(8,128)(2,1)S(1)}, bf16[6,12,128,128]{3,2,1,0:T(8,128)(2,1)}, u32[]{:S(2)}) copy-start(bf16[6,12,128,128]{3,2,1,0:T(8,128)(2,1)} %tiles_ref.5) | copy-start | bytes 7077892

commit v8 on v7

--- a/solution.py
+++ b/solution.py
@@ -8,6 +8,7 @@
 from jax.sharding import PartitionSpec as P
 
 VMEM_LIMIT = 48 * 1024 * 1024
+TOGETHER = 4
 SMEM = pl.BlockSpec(memory_space=pltpu.SMEM)
 VMEM = pl.BlockSpec(memory_space=pltpu.VMEM)
 HBM = pl.BlockSpec(memory_space=pl.ANY)
@@ -85,9 +86,9 @@
         scale_ref[i] = jnp.broadcast_to(scale_row_ref[i], (side, side)).T
     wait_rows(total, sources, fetched_ref, sems)
 
-    def two_blocks(step, carry):
-        for k in (0, 1):
-            at = 2 * step + k
+    def some_blocks(step, carry):
+        for k in range(TOGETHER):
+            at = TOGETHER * step + k
             block = list_ref[jnp.minimum(at, count - 1)]
             i, place = block // cands, place_ref[block]
             left, right = [], []
@@ -101,8 +102,8 @@
                 preferred_element_type=jnp.float32,
             )
             stage_ref[at] = (shared * (scale_ref[i] * scale_got_ref[place])).astype(stage_ref.dtype)
-        for k in (0, 1):
-            at = 2 * step + k
+        for k in range(TOGETHER):
+            at = TOGETHER * step + k
 
             @pl.when(at < count)
             def _():
@@ -112,7 +113,7 @@
 
         return carry
 
-    lax.fori_loop(0, (count + 1) // 2, two_blocks, 0)
+    lax.fori_loop(0, (count + TOGETHER - 1) // TOGETHER, some_blocks, 0)
 
     def wait_block(at, carry):
         pltpu.make_async_copy(stage_ref.at[at], out_ref.at[0, 0], out_sems.at[at]).wait()
@@ -135,7 +136,7 @@
         scratch_shapes=[
             pltpu.VMEM((total,) + tiles.shape[1:], tiles.dtype),
             pltpu.VMEM((local_rows, side, side), jnp.float32),
-            pltpu.VMEM((every + every % 2, side, side), jnp.bfloat16),
+            pltpu.VMEM((every + -every % TOGETHER, side, side), jnp.bfloat16),
             pltpu.SMEM((every,), jnp.int32),
             pltpu.SemaphoreType.DMA((total,)),
             pltpu.SemaphoreType.DMA((every,)),

time: 142 us -> 142 us (level)
  Pallas kernels: 37.6 us -> 34.8 us
  waiting for transfers between devices: 51.5 us -> 54.1 us
    pallas_call x3, Pallas kernels: 25.3 us -> 22.8 us  [blocks(): pl.pallas_call(functools.partial(blocks_kernel, total, prior is not None)...]
    ppermute x4, waiting for transfers between devices: 19.6 us -> 21.8 us  [relay(): lax.ppermute(sends[m + 3], 'col', moves([2, 0, 3, 1], m))]
  transfers between devices with their start and end apart: 13 -> 13, of which waited for: 8 -> 8; matrix products, arithmetic and copies ran while one was open for 9% -> 9% of each run, Pallas kernels for 22% -> 20%
where the time goes in v8:
time: 142 us; the launch traced here: 141 us
  waiting for transfers between devices  54.1 us (38%)
  starting transfers between devices  36.6 us (26%)
  Pallas kernels  34.8 us (25%)
  other arithmetic  10.5 us (7%)
  local copies, waits for them, and re-layouts  4.97 us (4%)
    pallas_call x3, Pallas kernels, blocks(): pl.pallas_call(functools.partial(blocks_kernel, total, prior is not None)...  22.8 us
    ppermute x4, waiting for transfers between devices, relay(): lax.ppermute(sends[m + 3], 'col', moves([2, 0, 3, 1], m))  21.8 us
    all_to_all x1, waiting for transfers between devices, relay(): lax.all_to_all(own_send, 'col', split_axis=0, concat_axis=0, axis_index_g...  15.4 us
    pallas_call x3, Pallas kernels, move_rows(): pl.pallas_call(functools.partial(move_rows_kernel, sizes), out_shape=[jax...  10.1 us
    ppermute x4, starting transfers between devices, relay(): lax.ppermute(sends[m + 3], 'col', moves([2, 0, 3, 1], m))  8.17 us
    ppermute x3, waiting for transfers between devices, relay(): lax.ppermute(sends[m - 1], 'col', moves([3, 1, 2, 0], m))  7.97 us
    all_to_all x1, starting transfers between devices, local(): notes = lax.all_to_all(note, 'col', split_axis=0, concat_axis=0, tiled=True)  7.39 us
    ppermute x1, waiting for transfers between devices, relay(): beside = lax.ppermute(beside_send, 'col', moves([1, 0, 3, 2]))  6.84 us
  transfers between devices with their start and end apart: 13, of which 8 were waited for; matrix products, arithmetic and copies ran while one was open for 9% of the time, Pallas kernels for 20%

profile of v8, /device:TPU:0, one launch (start us, length us, event | category | flops | bytes accessed | tf_op | source)
XLA Modules:
  0.0 141.3 jit_solution(4743623335722700638)
XLA Ops:
  0.0 1.9 %write_note.1 = s32[16,7,128]{2,1,0:T(8,128)} custom-call(s32[6,12]{1,0:T(8,128)} %candidates_ref.1, s32[6]{0:T(128)} %count_ref.1, s32[6,12]{1,0:T(8,128)} %cols_ref.1, s32[6,128]{1,0:T(8,128)} %degree_ref.1), custom_call_target="tpu_custom_call" | custom-call | tf_op jit(solution)/shard_map/write_note/pallas_call | solution.py:236
  1.9 7.4 %all-to-all-start = ((s32[16,7,128]{2,1,0:T(8,128)}), s32[16,7,128]{2,1,0:T(8,128)S(1)}, u32[]{:S(2)}, u32[]{:S(2)}) async-start(s32[16,7,128]{2,1,0:T(8,128)} %write_note.1), calls=%async_computation | async-start | bytes 131072 | tf_op jit(solution)/shard_map/all_to_all | solution.py:255
  9.3 2.1 %collective-permute-start.1 = (bf16[6,12,128,128]{3,2,1,0:T(8,128)(2,1)}, bf16[6,12,128,128]{3,2,1,0:T(8,128)(2,1)}, u32[]{:S(2)}, u32[]{:S(2)}) collective-permute-start(bf16[6,12,128,128]{3,2,1,0:T(8,128)(2,1)} %tiles_ref.5), channel_id=1, source_target_pairs={{4,8},{5,9},{6,10},{7,11},{8,4},{9,5},{10,6},{11,7},{20,24},{21,25... | collective-permute-start | bytes 7077896 | tf_op jit(solution)/shard_map/ppermute | solution.py:258
  11.4 0.7 convert_rsqrt_fusion.1
  12.1 0.7 add_select_fusion
  12.9 0.1 pad_add_fusion.4
  13.4 0.1 select_reduce_fusion.5
  14.1 2.1 %all-to-all-done = s32[16,7,128]{2,1,0:T(8,128)S(1)} async-done(((s32[16,7,128]{2,1,0:T(8,128)}), s32[16,7,128]{2,1,0:T(8,128)S(1)}, u32[]{:S(2)}, u32[]{:S(2)}) %all-to-all-start) | async-done | bytes 57376 | tf_op jit(solution)/shard_map/all_to_all | solution.py:255
  16.2 0.6 copy-done.2
  16.8 0.7 select_reduce_fusion.9
  17.5 0.7 select_reduce_fusion.10
  18.2 0.5 broadcast_20_source_ref.2.source_ref
  18.7 2.9 %move_rows.4 = bf16[4,12,128,128]{3,2,1,0:T(8,128)(2,1)} custom-call(s32[4]{0:T(128)} %broadcast_20_source_ref.2.source_ref, s32[4]{0:T(128)} %bitcast.13, bf16[6,12,128,128]{3,2,1,0:T(8,128)(2,1)} %tiles_ref.5), custom_call_target="tpu_custom_call" | custom-call | tf_op jit(solution)/shard_map/move_rows/pallas_call | solution.py:48
  21.6 1.5 %collective-permute-start = (bf16[4,12,128,128]{3,2,1,0:T(8,128)(2,1)}, bf16[4,12,128,128]{3,2,1,0:T(8,128)(2,1)}, u32[]{:S(2)}, u32[]{:S(2)}) collective-permute-start(bf16[4,12,128,128]{3,2,1,0:T(8,128)(2,1)} %move_rows.4), channel_id=1, source_target_pairs={{0,4},{1,5},{2,6},{3,7},{4,0},{5,1},{6,2},{7,3},{8,12},{9,13},{10,... | collective-permute-start | bytes 4718600 | tf_op jit(solution)/shard_map/ppermute | solution.py:182
  23.1 0.6 pad_add_fusion.5
  23.7 0.6 slice.48.row_ref
  24.3 0.5 broadcast_19_source_ref.2.source_ref
  24.8 3.2 %move_rows.3 = (bf16[4,12,128,128]{3,2,1,0:T(8,128)(2,1)}, bf16[1,12,128,128]{3,2,1,0:T(8,128)(2,1)}) custom-call(s32[5]{0:T(128)} %broadcast_19_source_ref.2.source_ref, s32[5]{0:T(128)} %slice.48.row_ref, bf16[6,12,128,128]{3,2,1,0:T(8,128)(2,1)} %tiles_ref.5), custom_call_target="tpu_custom_call" | custom-call | tf_op jit(solution)/shard_map/move_rows/pallas_call | solution.py:48
  28.0 3.7 %all-to-all-start.1 = ((bf16[4,12,128,128]{3,2,1,0:T(8,128)(2,1)}), bf16[4,12,128,128]{3,2,1,0:T(8,128)(2,1)S(1)}, u32[]{:S(2)}, u32[]{:S(2)}) async-start(bf16[4,12,128,128]{3,2,1,0:T(8,128)(2,1)} %get-tuple-element.14), calls=%async_computation.1 | async-start | bytes 3145728 | tf_op jit(solution)/shard_map/all_to_all | solution.py:184
  32.4 3.5 %collective-permute-start.2 = (bf16[1,12,128,128]{3,2,1,0:T(8,128)(2,1)}, bf16[1,12,128,128]{3,2,1,0:T(8,128)(2,1)S(1)}, u32[]{:S(2)}, u32[]{:S(2)}) collective-permute-start(bf16[1,12,128,128]{3,2,1,0:T(8,128)(2,1)} %get-tuple-element.15), channel_id=1, source_target_pairs={{0,12},{1,13},{2,14},{3,15},{12,0},{13,1},{14,2},{15,3},{16,28},{1... | collective-permute-start | bytes 1179656 | tf_op jit(solution)/shard_map/ppermute | solution.py:186
  35.9 0.2 fusion.1
  36.0 0.1 fusion
  36.3 0.1 select_reduce_fusion.3
  36.4 15.4 %all-to-all-done.1.refs_0_ = bf16[4,12,128,128]{3,2,1,0:T(8,128)(2,1)S(1)} async-done(((bf16[4,12,128,128]{3,2,1,0:T(8,128)(2,1)}), bf16[4,12,128,128]{3,2,1,0:T(8,128)(2,1)S(1)}, u32[]{:S(2)}, u32[]{:S(2)}) %all-to-all-start.1) | async-done | bytes 1572896 | tf_op jit(solution)/shard_map/all_to_all | solution.py:184
  51.8 6.8 %collective-permute-done = bf16[4,12,128,128]{3,2,1,0:T(8,128)(2,1)} collective-permute-done((bf16[4,12,128,128]{3,2,1,0:T(8,128)(2,1)}, bf16[4,12,128,128]{3,2,1,0:T(8,128)(2,1)}, u32[]{:S(2)}, u32[]{:S(2)}) %collective-permute-start) | collective-permute-done | bytes 1572896 | tf_op jit(solution)/shard_map/ppermute | solution.py:182
  58.6 4.3 %all-to-all-start.2 = ((bf16[4,12,128,128]{3,2,1,0:T(8,128)(2,1)}), bf16[4,12,128,128]{3,2,1,0:T(8,128)(2,1)}, u32[]{:S(2)}, u32[]{:S(2)}) async-start(bf16[4,12,128,128]{3,2,1,0:T(8,128)(2,1)} %collective-permute-done), calls=%async_computation.2 | async-start | bytes 3145728 | tf_op jit(solution)/shard_map/all_to_all | solution.py:185
  63.0 0.7 select_reduce_fusion.13.row_ref
  63.8 0.3 select_reduce_fusion.1
  64.0 2.0 %select_reduce_fusion = s32[6,12,12]{2,1,0:T(8,128)} fusion(s32[12]{0:T(128)S(1)} %iota_add_fusion.4, s32[6,12,12]{2,1,0:T(8,128)S(1)} %select_reduce_fusion.1, s32[6,12]{1,0:T(8,128)S(1)} %fusion.5), kind=kLoop, calls=%fused_computation | loop fusion | flops 30240 | bytes 7248 | tf_op jit(solution)/shard_map/reduce_sum | solution.py:277
  66.0 0.6 fusion.6
  66.6 0.5 add.106.source_ref
  67.2 4.1 %move_rows.5 = (bf16[1,12,128,128]{3,2,1,0:T(8,128)(2,1)}, bf16[1,12,128,128]{3,2,1,0:T(8,128)(2,1)}, bf16[1,12,128,128]{3,2,1,0:T(8,128)(2,1)}, bf16[1,12,128,1...) custom-call(s32[7]{0:T(128)} %add.106.source_ref, ...), custom_call_target="tpu_custom_call" | custom-call | tf_op jit(solution)/shard_map/move_rows/pallas_call | solution.py:48
  71.3 1.7 %collective-permute-start.3 = (bf16[1,12,128,128]{3,2,1,0:T(8,128)(2,1)}, bf16[1,12,128,128]{3,2,1,0:T(8,128)(2,1)S(1)}, u32[]{:S(2)}, u32[]{:S(2)}) collective-permute-start(bf16[1,12,128,128]{3,2,1,0:T(8,128)(2,1)} %get-tuple-element.16), channel_id=1, source_target_pairs={{0,13},{1,12},{2,15},{3,14},{4,5},{5,4},{6,7},{7,6},{8,9},{9,8},{1... | collective-permute-start | bytes 1179656 | tf_op jit(solution)/shard_map/ppermute | solution.py:194
  73.0 3.3 %collective-permute-start.4 = (bf16[1,12,128,128]{3,2,1,0:T(8,128)(2,1)}, bf16[1,12,128,128]{3,2,1,0:T(8,128)(2,1)S(1)}, u32[]{:S(2)}, u32[]{:S(2)}) collective-permute-start(bf16[1,12,128,128]{3,2,1,0:T(8,128)(2,1)} %get-tuple-element.17), channel_id=1, source_target_pairs={{0,14},{1,15},{2,12},{3,13},{4,6},{5,7},{6,4},{7,5},{8,10},{9,11},... | collective-permute-start | bytes 1179656 | tf_op jit(solution)/shard_map/ppermute | solution.py:194
  76.3 0.6 broadcast_select_fusion
  76.9 0.8 broadcast_add_fusion
  77.8 0.9 collective-permute-start.5
  78.7 5.6 %collective-permute-start.6 = (bf16[1,12,128,128]{3,2,1,0:T(8,128)(2,1)}, bf16[1,12,128,128]{3,2,1,0:T(8,128)(2,1)}, u32[]{:S(2)}, u32[]{:S(2)}) collective-permute-start(bf16[1,12,128,128]{3,2,1,0:T(8,128)(2,1)} %get-tuple-element.19), channel_id=1, source_target_pairs={{0,8},{1,9},{2,10},{3,11},{4,0},{5,1},{6,2},{7,3},{8,12},{9,13},{1... | collective-permute-start | bytes 1179656 | tf_op jit(solution)/shard_map/ppermute | solution.py:195
  84.4 2.6 %collective-permute-start.8 = (bf16[1,12,128,128]{3,2,1,0:T(8,128)(2,1)}, bf16[1,12,128,128]{3,2,1,0:T(8,128)(2,1)}, u32[]{:S(2)}, u32[]{:S(2)}) collective-permute-start(bf16[1,12,128,128]{3,2,1,0:T(8,128)(2,1)} %get-tuple-element.21), channel_id=1, source_target_pairs={{0,10},{1,11},{2,8},{3,9},{4,2},{5,3},{6,0},{7,1},{8,14},{9,15},{1... | collective-permute-start | bytes 1179656 | tf_op jit(solution)/shard_map/ppermute | solution.py:195
  87.0 8.0 %collective-permute-done.4.refs_4_ = bf16[1,12,128,128]{3,2,1,0:T(8,128)(2,1)S(1)} collective-permute-done((bf16[1,12,128,128]{3,2,1,0:T(8,128)(2,1)}, bf16[1,12,128,128]{3,2,1,0:T(8,128)(2,1)S(1)}, u32[]{:S(2)}, u32[]{:S(2)}) %collective-permute-start.4) | collective-permute-done | bytes 393248 | tf_op jit(solution)/shard_map/ppermute | solution.py:194
  95.0 1.7 %copy-done = bf16[6,12,128,128]{3,2,1,0:T(8,128)(2,1)S(1)} copy-done((bf16[6,12,128,128]{3,2,1,0:T(8,128)(2,1)S(1)}, bf16[6,12,128,128]{3,2,1,0:T(8,128)(2,1)}, u32[]{:S(2)}) %copy-start) | copy-done | bytes 2359320
  96.7 10.2 %blocks.3.refs_0_ = bf16[6,12,128,128]{3,2,1,0:T(8,128)(2,1)} custom-call(s32[72]{0:T(128)S(1)} %sub.40.place_ref, s32[864]{0:T(1024)S(1)} %sub.36.slot_ref, s32[8]{0:T(128)S(1)} %copy-done.1, s32[8]{0:T(128)S(1)} %pad_add_fusion.3.row_ref, bf16[6,12,128,128]{3,2,1,0:T(8,128)(2,1)S(1)} %copy-done, f32[6,1,128]{2,1,0:T(1,128)S(1)} %broadcast_in_dim.256.scale_row_ref, ...), custom_call_target="tpu_custom_call" | custom-call | flops 1811939328 | bytes 5505024 | tf_op jit(solution)/shard_map/blocks/pallas_call | solution.py:130
  106.9 3.2 %collective-permute-done.6.refs_6_ = bf16[1,12,128,128]{3,2,1,0:T(8,128)(2,1)} collective-permute-done((bf16[1,12,128,128]{3,2,1,0:T(8,128)(2,1)}, bf16[1,12,128,128]{3,2,1,0:T(8,128)(2,1)}, u32[]{:S(2)}, u32[]{:S(2)}) %collective-permute-start.6) | collective-permute-done | bytes 393248 | tf_op jit(solution)/shard_map/ppermute | solution.py:195
  110.2 8.4 %collective-permute-done.7.refs_7_ = bf16[1,12,128,128]{3,2,1,0:T(8,128)(2,1)} collective-permute-done((bf16[1,12,128,128]{3,2,1,0:T(8,128)(2,1)}, bf16[1,12,128,128]{3,2,1,0:T(8,128)(2,1)}, u32[]{:S(2)}, u32[]{:S(2)}) %collective-permute-start.7) | collective-permute-done | bytes 393248 | tf_op jit(solution)/shard_map/ppermute | solution.py:195
  118.5 8.3 %blocks.4.refs_0_ = bf16[6,12,128,128]{3,2,1,0:T(8,128)(2,1)} custom-call(s32[72]{0:T(128)S(1)} %sub.38.place_ref, s32[864]{0:T(1024)S(1)} %sub.36.slot_ref, s32[6]{0:T(128)S(1)} %pad_add_fusion.1.source_ref, s32[6]{0:T(128)S(1)} %concatenate.23.row_ref, bf16[6,12,128,128]{3,2,1,0:T(8,128)(2,1)S(1)} %copy-done, ...), custom_call_target="tpu_custom_call", output_to_operand_aliasing={{}: (7, {})} | custom-call | flops 1358954496 | bytes 4718592 | tf_op jit(solution)/shard_map/blocks/pallas_call | solution.py:130
  126.8 1.9 %collective-permute-done.8.refs_1_ = bf16[1,12,128,128]{3,2,1,0:T(8,128)(2,1)} collective-permute-done((bf16[1,12,128,128]{3,2,1,0:T(8,128)(2,1)}, bf16[1,12,128,128]{3,2,1,0:T(8,128)(2,1)}, u32[]{:S(2)}, u32[]{:S(2)}) %collective-permute-start.8) | collective-permute-done | bytes 393248 | tf_op jit(solution)/shard_map/ppermute | solution.py:195
  128.7 8.4 %collective-permute-done.9.refs_2_ = bf16[1,12,128,128]{3,2,1,0:T(8,128)(2,1)} collective-permute-done((bf16[1,12,128,128]{3,2,1,0:T(8,128)(2,1)}, bf16[1,12,128,128]{3,2,1,0:T(8,128)(2,1)}, u32[]{:S(2)}, u32[]{:S(2)}) %collective-permute-start.9) | collective-permute-done | bytes 393248 | tf_op jit(solution)/shard_map/ppermute | solution.py:195
  137.1 4.3 %blocks.5 = bf16[6,12,128,128]{3,2,1,0:T(8,128)(2,1)} custom-call(s32[72]{0:T(128)S(1)} %sub.34.place_ref, s32[864]{0:T(1024)S(1)} %sub.36.slot_ref, s32[2]{0:T(128)S(1)} %get-tuple-element.29.source_ref, s32[2]{0:T(128)S(1)} %broadcast_16_row_ref.2.row_ref, bf16[6,12,128,128]{3,2,1,0:T(8,128)(2,1)S(1)} %copy-done, ...), custom_call_target="tpu_custom_call", output_to_operand_aliasing={{}: (7, {})} | custom-call | flops 452984832 | bytes 3145728 | tf_op jit(solution)/shard_map/blocks/pallas_call | solution.py:130
  (72 shorter events, 2.2 us)
Async XLA Ops:
  1.9 14.3 %all-to-all-start = ((s32[16,7,128]{2,1,0:T(8,128)}), s32[16,7,128]{2,1,0:T(8,128)S(1)}, u32[]{:S(2)}, u32[]{:S(2)}) async-start(s32[16,7,128]{2,1,0:T(8,128)} %write_note.1), calls=%async_computation | async-start | bytes 131072 | tf_op jit(solution)/shard_map/all_to_all | solution.py:255
  9.3 57.4 %collective-permute-start.1 = (bf16[6,12,128,128]{3,2,1,0:T(8,128)(2,1)}, bf16[6,12,128,128]{3,2,1,0:T(8,128)(2,1)}, u32[]{:S(2)}, u32[]{:S(2)}) collective-permute-start(bf16[6,12,128,128]{3,2,1,0:T(8,128)(2,1)} %tiles_ref.5), channel_id=1, source_target_pairs={{4,8},{5,9},{6,10},{7,11},{8,4},{9,5},{10,6},{11,7},{20,24},{21,25... | collective-permute-start | bytes 7077896 | tf_op jit(solution)/shard_map/ppermute | solution.py:258
  16.2 0.6 copy-start.2
  18.2 5.5 %copy-start.6 = (s32[9]{0:T(128)S(1)}, s32[9]{0:T(128)}, u32[]{:S(2)}) copy-start(s32[9]{0:T(128)} %select_reduce_fusion.10) | copy-start | bytes 112
  21.6 37.0 %collective-permute-start = (bf16[4,12,128,128]{3,2,1,0:T(8,128)(2,1)}, bf16[4,12,128,128]{3,2,1,0:T(8,128)(2,1)}, u32[]{:S(2)}, u32[]{:S(2)}) collective-permute-start(bf16[4,12,128,128]{3,2,1,0:T(8,128)(2,1)} %move_rows.4), channel_id=1, source_target_pairs={{0,4},{1,5},{2,6},{3,7},{4,0},{5,1},{6,2},{7,3},{8,12},{9,13},{10,... | collective-permute-start | bytes 4718600 | tf_op jit(solution)/shard_map/ppermute | solution.py:182
  24.8 7.3 %copy-start.4 = (s32[6,12]{1,0:T(8,128)S(1)}, s32[6,12]{1,0:T(8,128)}, u32[]{:S(2)}) copy-start(s32[6,12]{1,0:T(8,128)} %cols_ref.1) | copy-start | bytes 868
  24.8 7.3 %copy-start.5 = (s32[6]{0:T(128)S(1)}, s32[6]{0:T(128)}, u32[]{:S(2)}) copy-start(s32[6]{0:T(128)} %count_ref.1) | copy-start | bytes 76
  28.0 8.0 %copy-start.3 = (s32[16,7,128]{2,1,0:T(8,128)S(1)}, s32[16,7,128]{2,1,0:T(8,128)}, u32[]{:S(2)}) copy-start(s32[16,7,128]{2,1,0:T(8,128)} %copy-done.2) | copy-start | bytes 172036
  28.0 23.8 %all-to-all-start.1 = ((bf16[4,12,128,128]{3,2,1,0:T(8,128)(2,1)}), bf16[4,12,128,128]{3,2,1,0:T(8,128)(2,1)S(1)}, u32[]{:S(2)}, u32[]{:S(2)}) async-start(bf16[4,12,128,128]{3,2,1,0:T(8,128)(2,1)} %get-tuple-element.14), calls=%async_computation.1 | async-start | bytes 3145728 | tf_op jit(solution)/shard_map/all_to_all | solution.py:184
  31.7 31.2 %copy-start.8 = (s32[16]{0:T(128)S(1)}, s32[16]{0:T(128)}, u32[]{:S(2)}) copy-start(s32[16]{0:T(128)} %get-tuple-element.23) | copy-start | bytes 196
  31.7 31.2 %copy-start.9 = (s32[7]{0:T(128)S(1)}, s32[7]{0:T(128)}, u32[]{:S(2)}) copy-start(s32[7]{0:T(128)} %pad_add_fusion.5) | copy-start | bytes 88
  31.7 34.3 %copy-start.7 = (s32[16]{0:T(128)S(1)}, s32[16]{0:T(128)}, u32[]{:S(2)}) copy-start(s32[16]{0:T(128)} %get-tuple-element.25) | copy-start | bytes 196
  32.4 51.9 %collective-permute-start.2 = (bf16[1,12,128,128]{3,2,1,0:T(8,128)(2,1)}, bf16[1,12,128,128]{3,2,1,0:T(8,128)(2,1)S(1)}, u32[]{:S(2)}, u32[]{:S(2)}) collective-permute-start(bf16[1,12,128,128]{3,2,1,0:T(8,128)(2,1)} %get-tuple-element.15), channel_id=1, source_target_pairs={{0,12},{1,13},{2,14},{3,15},{12,0},{13,1},{14,2},{15,3},{16,28},{1... | collective-permute-start | bytes 1179656 | tf_op jit(solution)/shard_map/ppermute | solution.py:186
  58.6 36.4 %all-to-all-start.2 = ((bf16[4,12,128,128]{3,2,1,0:T(8,128)(2,1)}), bf16[4,12,128,128]{3,2,1,0:T(8,128)(2,1)}, u32[]{:S(2)}, u32[]{:S(2)}) async-start(bf16[4,12,128,128]{3,2,1,0:T(8,128)(2,1)} %collective-permute-done), calls=%async_computation.2 | async-start | bytes 3145728 | tf_op jit(solution)/shard_map/all_to_all | solution.py:185
  67.2 27.8 %copy-start.1 = (s32[8]{0:T(128)S(1)}, s32[8]{0:T(128)}, u32[]{:S(2)}) copy-start(s32[8]{0:T(128)} %constant.75.clone.1.source_ref) | copy-start | bytes 100
  71.3 13.1 %collective-permute-start.3 = (bf16[1,12,128,128]{3,2,1,0:T(8,128)(2,1)}, bf16[1,12,128,128]{3,2,1,0:T(8,128)(2,1)S(1)}, u32[]{:S(2)}, u32[]{:S(2)}) collective-permute-start(bf16[1,12,128,128]{3,2,1,0:T(8,128)(2,1)} %get-tuple-element.16), channel_id=1, source_target_pairs={{0,13},{1,12},{2,15},{3,14},{4,5},{5,4},{6,7},{7,6},{8,9},{9,8},{1... | collective-permute-start | bytes 1179656 | tf_op jit(solution)/shard_map/ppermute | solution.py:194
  73.0 21.9 %collective-permute-start.4 = (bf16[1,12,128,128]{3,2,1,0:T(8,128)(2,1)}, bf16[1,12,128,128]{3,2,1,0:T(8,128)(2,1)S(1)}, u32[]{:S(2)}, u32[]{:S(2)}) collective-permute-start(bf16[1,12,128,128]{3,2,1,0:T(8,128)(2,1)} %get-tuple-element.17), channel_id=1, source_target_pairs={{0,14},{1,15},{2,12},{3,13},{4,6},{5,7},{6,4},{7,5},{8,10},{9,11},... | collective-permute-start | bytes 1179656 | tf_op jit(solution)/shard_map/ppermute | solution.py:194
  77.8 29.2 %collective-permute-start.5 = (bf16[1,12,128,128]{3,2,1,0:T(8,128)(2,1)}, bf16[1,12,128,128]{3,2,1,0:T(8,128)(2,1)S(1)}, u32[]{:S(2)}, u32[]{:S(2)}) collective-permute-start(bf16[1,12,128,128]{3,2,1,0:T(8,128)(2,1)} %get-tuple-element.18), channel_id=1, source_target_pairs={{0,15},{1,14},{2,13},{3,12},{4,7},{5,6},{6,5},{7,4},{8,11},{9,10},... | collective-permute-start | bytes 1179656 | tf_op jit(solution)/shard_map/ppermute | solution.py:194
  78.7 31.5 %collective-permute-start.6 = (bf16[1,12,128,128]{3,2,1,0:T(8,128)(2,1)}, bf16[1,12,128,128]{3,2,1,0:T(8,128)(2,1)}, u32[]{:S(2)}, u32[]{:S(2)}) collective-permute-start(bf16[1,12,128,128]{3,2,1,0:T(8,128)(2,1)} %get-tuple-element.19), channel_id=1, source_target_pairs={{0,8},{1,9},{2,10},{3,11},{4,0},{5,1},{6,2},{7,3},{8,12},{9,13},{1... | collective-permute-start | bytes 1179656 | tf_op jit(solution)/shard_map/ppermute | solution.py:195
  84.3 34.2 %collective-permute-start.7 = (bf16[1,12,128,128]{3,2,1,0:T(8,128)(2,1)}, bf16[1,12,128,128]{3,2,1,0:T(8,128)(2,1)}, u32[]{:S(2)}, u32[]{:S(2)}) collective-permute-start(bf16[1,12,128,128]{3,2,1,0:T(8,128)(2,1)} %get-tuple-element.20), channel_id=1, source_target_pairs={{0,9},{1,8},{2,11},{3,10},{4,1},{5,0},{6,3},{7,2},{8,13},{9,12},{1... | collective-permute-start | bytes 1179656 | tf_op jit(solution)/shard_map/ppermute | solution.py:195
  84.4 44.3 %collective-permute-start.8 = (bf16[1,12,128,128]{3,2,1,0:T(8,128)(2,1)}, bf16[1,12,128,128]{3,2,1,0:T(8,128)(2,1)}, u32[]{:S(2)}, u32[]{:S(2)}) collective-permute-start(bf16[1,12,128,128]{3,2,1,0:T(8,128)(2,1)} %get-tuple-element.21), channel_id=1, source_target_pairs={{0,10},{1,11},{2,8},{3,9},{4,2},{5,3},{6,0},{7,1},{8,14},{9,15},{1... | collective-permute-start | bytes 1179656 | tf_op jit(solution)/shard_map/ppermute | solution.py:195
  94.9 42.1 %collective-permute-start.9 = (bf16[1,12,128,128]{3,2,1,0:T(8,128)(2,1)}, bf16[1,12,128,128]{3,2,1,0:T(8,128)(2,1)}, u32[]{:S(2)}, u32[]{:S(2)}) collective-permute-start(bf16[1,12,128,128]{3,2,1,0:T(8,128)(2,1)} %get-tuple-element.22), channel_id=1, source_target_pairs={{0,11},{1,10},{2,9},{3,8},{4,3},{5,2},{6,1},{7,0},{8,15},{9,14},{1... | collective-permute-start | bytes 1179656 | tf_op jit(solution)/shard_map/ppermute | solution.py:195
  95.0 1.7 %copy-start = (bf16[6,12,128,128]{3,2,1,0:T(8,128)(2,1)S(1)}, bf16[6,12,128,128]{3,2,1,0:T(8,128)(2,1)}, u32[]{:S(2)}) copy-start(bf16[6,12,128,128]{3,2,1,0:T(8,128)(2,1)} %tiles_ref.5) | copy-start | bytes 7077892

commit v9 on v7

--- a/solution.py
+++ b/solution.py
@@ -57,6 +57,25 @@
         compiler_params=WHOLE_VMEM,
         name="move_rows",
     )(source_ids, row_ids, *sources)
+
+
+def stack_kernel(row_ref, tiles_ref, out_ref, sems):
+    for k in range(out_ref.shape[0]):
+        pltpu.make_async_copy(tiles_ref.at[row_ref[k]], out_ref.at[k], sems.at[k]).start()
+    for k in range(out_ref.shape[0]):
+        pltpu.make_async_copy(tiles_ref.at[0], out_ref.at[k], sems.at[k]).wait()
+
+
+def stack_rows(rows, tiles):
+    return pl.pallas_call(
+        stack_kernel,
+        out_shape=jax.ShapeDtypeStruct(rows.shape + tiles.shape[1:], tiles.dtype),
+        in_specs=[SMEM, HBM],
+        out_specs=VMEM,
+        scratch_shapes=[pltpu.SemaphoreType.DMA(rows.shape)],
+        compiler_params=PARAMS,
+        name="stack_rows",
+    )(rows, tiles)
 
 
 def pick_rows(rows, tiles, sizes):
@@ -177,7 +196,7 @@
 
     beyond = 4 * (plane ^ 3) + (mate ^ flips)
     mine = lookup(jnp.concatenate([4 * (plane ^ 1) + flips, 4 * plane + flips, beyond[:1]]), me)
-    (beside_send,) = pick_rows(mine[:4], tiles, (4,))
+    beside_send = stack_rows(mine[:4], tiles)
     beside = lax.ppermute(beside_send, "col", moves([1, 0, 3, 2]))
     own_send, first_send = pick_rows(mine[4:], tiles, (4, 1))
     own = lax.all_to_all(own_send, "col", split_axis=0, concat_axis=0, axis_index_groups=PLANES, tiled=True)

time: 142 us -> 142 us (level)
    pallas_call x3 -> x2, Pallas kernels: 10.5 us -> 7.04 us  [move_rows(): pl.pallas_call(functools.partial(move_rows_kernel, sizes), out_shape=[jax...]
    pallas_call x0 -> x1, Pallas kernels: none -> 2.5 us  [stack_rows(): pl.pallas_call(stack_kernel, out_shape=jax.ShapeDtypeStruct(rows.shape +...]
  transfers between devices with their start and end apart: 13 -> 13, of which waited for: 8 -> 8; matrix products, arithmetic and copies ran while one was open for 9% -> 9% of each run, Pallas kernels for 22% -> 21%
where the time goes in v9:
time: 142 us; the launch traced here: 141 us
  waiting for transfers between devices  50.5 us (36%)
  starting transfers between devices  37.6 us (26%)
  Pallas kernels  36.7 us (26%)
  other arithmetic  10 us (7%)
  local copies, waits for them, and re-layouts  5.54 us (4%)
    pallas_call x3, Pallas kernels, blocks(): pl.pallas_call(functools.partial(blocks_kernel, total, prior is not None)...  25.3 us
    ppermute x4, waiting for transfers between devices, relay(): lax.ppermute(sends[m + 3], 'col', moves([2, 0, 3, 1], m))  19.6 us
    all_to_all x1, waiting for transfers between devices, relay(): lax.all_to_all(own_send, 'col', split_axis=0, concat_axis=0, axis_index_g...  15.6 us
    ppermute x4, starting transfers between devices, relay(): lax.ppermute(sends[m + 3], 'col', moves([2, 0, 3, 1], m))  8.39 us
    all_to_all x1, starting transfers between devices, local(): notes = lax.all_to_all(note, 'col', split_axis=0, concat_axis=0, tiled=True)  7.39 us
    ppermute x3, starting transfers between devices, relay(): lax.ppermute(sends[m - 1], 'col', moves([3, 1, 2, 0], m))  7.18 us
    ppermute x3, waiting for transfers between devices, relay(): lax.ppermute(sends[m - 1], 'col', moves([3, 1, 2, 0], m))  7.17 us
    pallas_call x2, Pallas kernels, move_rows(): pl.pallas_call(functools.partial(move_rows_kernel, sizes), out_shape=[jax...  7.04 us
  transfers between devices with their start and end apart: 13, of which 8 were waited for; matrix products, arithmetic and copies ran while one was open for 9% of the time, Pallas kernels for 21%

profile of v9, /device:TPU:0, one launch (start us, length us, event | category | flops | bytes accessed | tf_op | source)
XLA Modules:
  0.0 140.8 jit_solution(10088795620463559742)
XLA Ops:
  0.0 1.9 %write_note.1 = s32[16,7,128]{2,1,0:T(8,128)} custom-call(s32[6,12]{1,0:T(8,128)} %candidates_ref.1, s32[6]{0:T(128)} %count_ref.1, s32[6,12]{1,0:T(8,128)} %cols_ref.1, s32[6,128]{1,0:T(8,128)} %degree_ref.1), custom_call_target="tpu_custom_call" | custom-call | tf_op jit(solution)/shard_map/write_note/pallas_call | solution.py:254
  1.9 7.4 %all-to-all-start = ((s32[16,7,128]{2,1,0:T(8,128)}), s32[16,7,128]{2,1,0:T(8,128)S(1)}, u32[]{:S(2)}, u32[]{:S(2)}) async-start(s32[16,7,128]{2,1,0:T(8,128)} %write_note.1), calls=%async_computation | async-start | bytes 131072 | tf_op jit(solution)/shard_map/all_to_all | solution.py:273
  9.3 2.1 %collective-permute-start.1 = (bf16[6,12,128,128]{3,2,1,0:T(8,128)(2,1)}, bf16[6,12,128,128]{3,2,1,0:T(8,128)(2,1)}, u32[]{:S(2)}, u32[]{:S(2)}) collective-permute-start(bf16[6,12,128,128]{3,2,1,0:T(8,128)(2,1)} %tiles_ref.7), channel_id=1, source_target_pairs={{4,8},{5,9},{6,10},{7,11},{8,4},{9,5},{10,6},{11,7},{20,24},{21,25... | collective-permute-start | bytes 7077896 | tf_op jit(solution)/shard_map/ppermute | solution.py:276
  11.4 0.7 convert_rsqrt_fusion.1
  12.1 0.7 add_select_fusion
  12.9 0.1 pad_add_fusion.4
  13.4 0.1 select_reduce_fusion.5
  14.1 2.1 %all-to-all-done = s32[16,7,128]{2,1,0:T(8,128)S(1)} async-done(((s32[16,7,128]{2,1,0:T(8,128)}), s32[16,7,128]{2,1,0:T(8,128)S(1)}, u32[]{:S(2)}, u32[]{:S(2)}) %all-to-all-start) | async-done | bytes 57376 | tf_op jit(solution)/shard_map/all_to_all | solution.py:273
  16.2 0.7 select_reduce_fusion.9
  16.9 0.2 select_reduce_fusion.10
  17.1 1.7 %copy-done = bf16[6,12,128,128]{3,2,1,0:T(8,128)(2,1)S(1)} copy-done((bf16[6,12,128,128]{3,2,1,0:T(8,128)(2,1)S(1)}, bf16[6,12,128,128]{3,2,1,0:T(8,128)(2,1)}, u32[]{:S(2)}) %copy-start) | copy-done | bytes 2359320
  18.7 2.5 %stack_rows.1 = bf16[4,12,128,128]{3,2,1,0:T(8,128)(2,1)} custom-call(s32[4]{0:T(128)S(1)} %bitcast.8, bf16[6,12,128,128]{3,2,1,0:T(8,128)(2,1)S(1)} %copy-done), custom_call_target="tpu_custom_call" | custom-call | tf_op jit(solution)/shard_map/stack_rows/pallas_call | solution.py:70
  21.2 1.3 collective-permute-start
  22.5 0.6 pad_add_fusion.5
  23.1 0.6 slice.48.row_ref
  23.7 0.5 broadcast_20_source_ref.2.source_ref
  24.3 3.6 %move_rows.2 = (bf16[4,12,128,128]{3,2,1,0:T(8,128)(2,1)}, bf16[1,12,128,128]{3,2,1,0:T(8,128)(2,1)}) custom-call(s32[5]{0:T(128)} %broadcast_20_source_ref.2.source_ref, s32[5]{0:T(128)} %slice.48.row_ref, bf16[6,12,128,128]{3,2,1,0:T(8,128)(2,1)} %tiles_ref.7), custom_call_target="tpu_custom_call" | custom-call | tf_op jit(solution)/shard_map/move_rows/pallas_call | solution.py:47
  27.8 3.7 %all-to-all-start.1 = ((bf16[4,12,128,128]{3,2,1,0:T(8,128)(2,1)}), bf16[4,12,128,128]{3,2,1,0:T(8,128)(2,1)S(1)}, u32[]{:S(2)}, u32[]{:S(2)}) async-start(bf16[4,12,128,128]{3,2,1,0:T(8,128)(2,1)} %get-tuple-element.14), calls=%async_computation.1 | async-start | bytes 3145728 | tf_op jit(solution)/shard_map/all_to_all | solution.py:202
  32.2 3.3 %collective-permute-start.2 = (bf16[1,12,128,128]{3,2,1,0:T(8,128)(2,1)}, bf16[1,12,128,128]{3,2,1,0:T(8,128)(2,1)S(1)}, u32[]{:S(2)}, u32[]{:S(2)}) collective-permute-start(bf16[1,12,128,128]{3,2,1,0:T(8,128)(2,1)} %get-tuple-element.15), channel_id=1, source_target_pairs={{0,12},{1,13},{2,14},{3,15},{12,0},{13,1},{14,2},{15,3},{16,28},{1... | collective-permute-start | bytes 1179656 | tf_op jit(solution)/shard_map/ppermute | solution.py:204
  35.5 0.2 fusion.1
  35.7 0.1 fusion
  35.9 0.1 select_reduce_fusion.3
  36.0 15.6 %all-to-all-done.1.refs_0_ = bf16[4,12,128,128]{3,2,1,0:T(8,128)(2,1)S(1)} async-done(((bf16[4,12,128,128]{3,2,1,0:T(8,128)(2,1)}), bf16[4,12,128,128]{3,2,1,0:T(8,128)(2,1)S(1)}, u32[]{:S(2)}, u32[]{:S(2)}) %all-to-all-start.1) | async-done | bytes 1572896 | tf_op jit(solution)/shard_map/all_to_all | solution.py:202
  51.6 6.0 %collective-permute-done = bf16[4,12,128,128]{3,2,1,0:T(8,128)(2,1)} collective-permute-done((bf16[4,12,128,128]{3,2,1,0:T(8,128)(2,1)}, bf16[4,12,128,128]{3,2,1,0:T(8,128)(2,1)}, u32[]{:S(2)}, u32[]{:S(2)}) %collective-permute-start) | collective-permute-done | bytes 1572896 | tf_op jit(solution)/shard_map/ppermute | solution.py:200
  57.6 4.3 %all-to-all-start.2 = ((bf16[4,12,128,128]{3,2,1,0:T(8,128)(2,1)}), bf16[4,12,128,128]{3,2,1,0:T(8,128)(2,1)}, u32[]{:S(2)}, u32[]{:S(2)}) async-start(bf16[4,12,128,128]{3,2,1,0:T(8,128)(2,1)} %collective-permute-done), calls=%async_computation.2 | async-start | bytes 3145728 | tf_op jit(solution)/shard_map/all_to_all | solution.py:203
  62.0 0.7 select_reduce_fusion.13.row_ref
  62.8 0.3 select_reduce_fusion.1
  63.0 2.0 %select_reduce_fusion = s32[6,12,12]{2,1,0:T(8,128)} fusion(s32[12]{0:T(128)S(1)} %iota_add_fusion.4, s32[6,12,12]{2,1,0:T(8,128)S(1)} %select_reduce_fusion.1, s32[6,12]{1,0:T(8,128)S(1)} %fusion.5), kind=kLoop, calls=%fused_computation | loop fusion | flops 30240 | bytes 7248 | tf_op jit(solution)/shard_map/reduce_sum | solution.py:295
  65.0 0.6 fusion.6
  65.7 0.5 add.106.source_ref
  66.2 3.5 %move_rows.3 = (bf16[1,12,128,128]{3,2,1,0:T(8,128)(2,1)}, bf16[1,12,128,128]{3,2,1,0:T(8,128)(2,1)}, bf16[1,12,128,128]{3,2,1,0:T(8,128)(2,1)}, bf16[1,12,128,1...) custom-call(s32[7]{0:T(128)} %add.106.source_ref, ...), custom_call_target="tpu_custom_call" | custom-call | tf_op jit(solution)/shard_map/move_rows/pallas_call | solution.py:47
  69.7 3.0 %collective-permute-start.3 = (bf16[1,12,128,128]{3,2,1,0:T(8,128)(2,1)}, bf16[1,12,128,128]{3,2,1,0:T(8,128)(2,1)S(1)}, u32[]{:S(2)}, u32[]{:S(2)}) collective-permute-start(bf16[1,12,128,128]{3,2,1,0:T(8,128)(2,1)} %get-tuple-element.16), channel_id=1, source_target_pairs={{0,13},{1,12},{2,15},{3,14},{4,5},{5,4},{6,7},{7,6},{8,9},{9,8},{1... | collective-permute-start | bytes 1179656 | tf_op jit(solution)/shard_map/ppermute | solution.py:212
  72.7 2.7 %collective-permute-start.4 = (bf16[1,12,128,128]{3,2,1,0:T(8,128)(2,1)}, bf16[1,12,128,128]{3,2,1,0:T(8,128)(2,1)S(1)}, u32[]{:S(2)}, u32[]{:S(2)}) collective-permute-start(bf16[1,12,128,128]{3,2,1,0:T(8,128)(2,1)} %get-tuple-element.17), channel_id=1, source_target_pairs={{0,14},{1,15},{2,12},{3,13},{4,6},{5,7},{6,4},{7,5},{8,10},{9,11},... | collective-permute-start | bytes 1179656 | tf_op jit(solution)/shard_map/ppermute | solution.py:212
  75.4 0.6 broadcast_select_fusion
  76.0 0.8 broadcast_add_fusion
  76.8 0.1 sub.36.slot_ref
  76.9 1.4 %collective-permute-start.5 = (bf16[1,12,128,128]{3,2,1,0:T(8,128)(2,1)}, bf16[1,12,128,128]{3,2,1,0:T(8,128)(2,1)S(1)}, u32[]{:S(2)}, u32[]{:S(2)}) collective-permute-start(bf16[1,12,128,128]{3,2,1,0:T(8,128)(2,1)} %get-tuple-element.18), channel_id=1, source_target_pairs={{0,15},{1,14},{2,13},{3,12},{4,7},{5,6},{6,5},{7,4},{8,11},{9,10},... | collective-permute-start | bytes 1179656 | tf_op jit(solution)/shard_map/ppermute | solution.py:212
  78.4 5.8 %collective-permute-start.6 = (bf16[1,12,128,128]{3,2,1,0:T(8,128)(2,1)}, bf16[1,12,128,128]{3,2,1,0:T(8,128)(2,1)}, u32[]{:S(2)}, u32[]{:S(2)}) collective-permute-start(bf16[1,12,128,128]{3,2,1,0:T(8,128)(2,1)} %get-tuple-element.19), channel_id=1, source_target_pairs={{0,8},{1,9},{2,10},{3,11},{4,0},{5,1},{6,2},{7,3},{8,12},{9,13},{1... | collective-permute-start | bytes 1179656 | tf_op jit(solution)/shard_map/ppermute | solution.py:213
  84.3 2.6 %collective-permute-start.8 = (bf16[1,12,128,128]{3,2,1,0:T(8,128)(2,1)}, bf16[1,12,128,128]{3,2,1,0:T(8,128)(2,1)}, u32[]{:S(2)}, u32[]{:S(2)}) collective-permute-start(bf16[1,12,128,128]{3,2,1,0:T(8,128)(2,1)} %get-tuple-element.21), channel_id=1, source_target_pairs={{0,10},{1,11},{2,8},{3,9},{4,2},{5,3},{6,0},{7,1},{8,14},{9,15},{1... | collective-permute-start | bytes 1179656 | tf_op jit(solution)/shard_map/ppermute | solution.py:213
  86.9 7.2 %collective-permute-done.4.refs_4_ = bf16[1,12,128,128]{3,2,1,0:T(8,128)(2,1)S(1)} collective-permute-done((bf16[1,12,128,128]{3,2,1,0:T(8,128)(2,1)}, bf16[1,12,128,128]{3,2,1,0:T(8,128)(2,1)S(1)}, u32[]{:S(2)}, u32[]{:S(2)}) %collective-permute-start.4) | collective-permute-done | bytes 393248 | tf_op jit(solution)/shard_map/ppermute | solution.py:212
  94.2 1.7 %copy-done.1 = bf16[6,12,128,128]{3,2,1,0:T(8,128)(2,1)S(1)} copy-done((bf16[6,12,128,128]{3,2,1,0:T(8,128)(2,1)S(1)}, bf16[6,12,128,128]{3,2,1,0:T(8,128)(2,1)}, u32[]{:S(2)}) %copy-start.1) | copy-done | bytes 2359320
  95.8 11.2 %blocks.3.refs_0_ = bf16[6,12,128,128]{3,2,1,0:T(8,128)(2,1)} custom-call(s32[72]{0:T(128)S(1)} %sub.40.place_ref, s32[864]{0:T(1024)S(1)} %sub.36.slot_ref, s32[8]{0:T(128)S(1)} %copy-done.2, s32[8]{0:T(128)S(1)} %pad_add_fusion.3.row_ref, bf16[6,12,128,128]{3,2,1,0:T(8,128)(2,1)S(1)} %copy-done.1, f32[6,1,128]{2,1,0:T(1,128)S(1)} %broadcast_in_dim.256.scale_row_ref, ...), custom_call_target="tpu_custom_call" | custom-call | flops 1811939328 | bytes 5505024 | tf_op jit(solution)/shard_map/blocks/pallas_call | solution.py:148
  107.0 1.5 %collective-permute-done.6.refs_6_ = bf16[1,12,128,128]{3,2,1,0:T(8,128)(2,1)} collective-permute-done((bf16[1,12,128,128]{3,2,1,0:T(8,128)(2,1)}, bf16[1,12,128,128]{3,2,1,0:T(8,128)(2,1)}, u32[]{:S(2)}, u32[]{:S(2)}) %collective-permute-start.6) | collective-permute-done | bytes 393248 | tf_op jit(solution)/shard_map/ppermute | solution.py:213
  108.6 8.4 %collective-permute-done.7.refs_7_ = bf16[1,12,128,128]{3,2,1,0:T(8,128)(2,1)} collective-permute-done((bf16[1,12,128,128]{3,2,1,0:T(8,128)(2,1)}, bf16[1,12,128,128]{3,2,1,0:T(8,128)(2,1)}, u32[]{:S(2)}, u32[]{:S(2)}) %collective-permute-start.7) | collective-permute-done | bytes 393248 | tf_op jit(solution)/shard_map/ppermute | solution.py:213
  117.0 9.1 %blocks.4.refs_0_ = bf16[6,12,128,128]{3,2,1,0:T(8,128)(2,1)} custom-call(s32[72]{0:T(128)S(1)} %sub.38.place_ref, s32[864]{0:T(1024)S(1)} %sub.36.slot_ref, s32[6]{0:T(128)S(1)} %pad_add_fusion.1.source_ref, s32[6]{0:T(128)S(1)} %concatenate.23.row_ref, bf16[6,12,128,128]{3,2,1,0:T(8,128)(2,1)S(1)} %copy-done.1, ...), custom_call_target="tpu_custom_call", output_to_operand_aliasing={{}: (7, {})} | custom-call | flops 1358954496 | bytes 4718592 | tf_op jit(solution)/shard_map/blocks/pallas_call | solution.py:148
  126.1 1.3 collective-permute-done.8.refs_1_
  127.4 8.4 %collective-permute-done.9.refs_2_ = bf16[1,12,128,128]{3,2,1,0:T(8,128)(2,1)} collective-permute-done((bf16[1,12,128,128]{3,2,1,0:T(8,128)(2,1)}, bf16[1,12,128,128]{3,2,1,0:T(8,128)(2,1)}, u32[]{:S(2)}, u32[]{:S(2)}) %collective-permute-start.9) | collective-permute-done | bytes 393248 | tf_op jit(solution)/shard_map/ppermute | solution.py:213
  135.8 5.0 %blocks.5 = bf16[6,12,128,128]{3,2,1,0:T(8,128)(2,1)} custom-call(s32[72]{0:T(128)S(1)} %sub.34.place_ref, s32[864]{0:T(1024)S(1)} %sub.36.slot_ref, s32[2]{0:T(128)S(1)} %get-tuple-element.29.source_ref, s32[2]{0:T(128)S(1)} %broadcast_16_row_ref.2.row_ref, bf16[6,12,128,128]{3,2,1,0:T(8,128)(2,1)S(1)} %copy-done.1, ...), custom_call_target="tpu_custom_call", output_to_operand_aliasing={{}: (7, {})} | custom-call | flops 452984832 | bytes 3145728 | tf_op jit(solution)/shard_map/blocks/pallas_call | solution.py:148
  (71 shorter events, 2.1 us)
Async XLA Ops:
  1.9 14.3 %all-to-all-start = ((s32[16,7,128]{2,1,0:T(8,128)}), s32[16,7,128]{2,1,0:T(8,128)S(1)}, u32[]{:S(2)}, u32[]{:S(2)}) async-start(s32[16,7,128]{2,1,0:T(8,128)} %write_note.1), calls=%async_computation | async-start | bytes 131072 | tf_op jit(solution)/shard_map/all_to_all | solution.py:273
  9.3 56.4 %collective-permute-start.1 = (bf16[6,12,128,128]{3,2,1,0:T(8,128)(2,1)}, bf16[6,12,128,128]{3,2,1,0:T(8,128)(2,1)}, u32[]{:S(2)}, u32[]{:S(2)}) collective-permute-start(bf16[6,12,128,128]{3,2,1,0:T(8,128)(2,1)} %tiles_ref.7), channel_id=1, source_target_pairs={{4,8},{5,9},{6,10},{7,11},{8,4},{9,5},{10,6},{11,7},{20,24},{21,25... | collective-permute-start | bytes 7077896 | tf_op jit(solution)/shard_map/ppermute | solution.py:276
  16.2 7.6 %copy-start.3 = (s32[16,7,128]{2,1,0:T(8,128)}, s32[16,7,128]{2,1,0:T(8,128)S(1)}, u32[]{:S(2)}) copy-start(s32[16,7,128]{2,1,0:T(8,128)S(1)} %all-to-all-done) | copy-start | bytes 172036
  17.1 1.7 %copy-start = (bf16[6,12,128,128]{3,2,1,0:T(8,128)(2,1)S(1)}, bf16[6,12,128,128]{3,2,1,0:T(8,128)(2,1)}, u32[]{:S(2)}) copy-start(bf16[6,12,128,128]{3,2,1,0:T(8,128)(2,1)} %tiles_ref.7) | copy-start | bytes 7077892
  21.2 36.4 %collective-permute-start = (bf16[4,12,128,128]{3,2,1,0:T(8,128)(2,1)}, bf16[4,12,128,128]{3,2,1,0:T(8,128)(2,1)}, u32[]{:S(2)}, u32[]{:S(2)}) collective-permute-start(bf16[4,12,128,128]{3,2,1,0:T(8,128)(2,1)} %stack_rows.1), channel_id=1, source_target_pairs={{0,4},{1,5},{2,6},{3,7},{4,0},{5,1},{6,2},{7,3},{8,12},{9,13},{10,... | collective-permute-start | bytes 4718600 | tf_op jit(solution)/shard_map/ppermute | solution.py:200
  24.3 7.7 %copy-start.5 = (s32[6,12]{1,0:T(8,128)S(1)}, s32[6,12]{1,0:T(8,128)}, u32[]{:S(2)}) copy-start(s32[6,12]{1,0:T(8,128)} %cols_ref.1) | copy-start | bytes 868
  24.3 7.7 %copy-start.6 = (s32[6]{0:T(128)S(1)}, s32[6]{0:T(128)}, u32[]{:S(2)}) copy-start(s32[6]{0:T(128)} %count_ref.1) | copy-start | bytes 76
  27.8 7.9 %copy-start.4 = (s32[16,7,128]{2,1,0:T(8,128)S(1)}, s32[16,7,128]{2,1,0:T(8,128)}, u32[]{:S(2)}) copy-start(s32[16,7,128]{2,1,0:T(8,128)} %copy-done.3) | copy-start | bytes 172036
  27.8 23.8 %all-to-all-start.1 = ((bf16[4,12,128,128]{3,2,1,0:T(8,128)(2,1)}), bf16[4,12,128,128]{3,2,1,0:T(8,128)(2,1)S(1)}, u32[]{:S(2)}, u32[]{:S(2)}) async-start(bf16[4,12,128,128]{3,2,1,0:T(8,128)(2,1)} %get-tuple-element.14), calls=%async_computation.1 | async-start | bytes 3145728 | tf_op jit(solution)/shard_map/all_to_all | solution.py:202
  31.6 30.4 %copy-start.8 = (s32[16]{0:T(128)S(1)}, s32[16]{0:T(128)}, u32[]{:S(2)}) copy-start(s32[16]{0:T(128)} %get-tuple-element.23) | copy-start | bytes 196
  31.6 30.4 %copy-start.9 = (s32[7]{0:T(128)S(1)}, s32[7]{0:T(128)}, u32[]{:S(2)}) copy-start(s32[7]{0:T(128)} %pad_add_fusion.5) | copy-start | bytes 88
  31.6 33.5 %copy-start.7 = (s32[16]{0:T(128)S(1)}, s32[16]{0:T(128)}, u32[]{:S(2)}) copy-start(s32[16]{0:T(128)} %get-tuple-element.25) | copy-start | bytes 196
  32.2 52.0 %collective-permute-start.2 = (bf16[1,12,128,128]{3,2,1,0:T(8,128)(2,1)}, bf16[1,12,128,128]{3,2,1,0:T(8,128)(2,1)S(1)}, u32[]{:S(2)}, u32[]{:S(2)}) collective-permute-start(bf16[1,12,128,128]{3,2,1,0:T(8,128)(2,1)} %get-tuple-element.15), channel_id=1, source_target_pairs={{0,12},{1,13},{2,14},{3,15},{12,0},{13,1},{14,2},{15,3},{16,28},{1... | collective-permute-start | bytes 1179656 | tf_op jit(solution)/shard_map/ppermute | solution.py:204
  57.6 36.5 %all-to-all-start.2 = ((bf16[4,12,128,128]{3,2,1,0:T(8,128)(2,1)}), bf16[4,12,128,128]{3,2,1,0:T(8,128)(2,1)}, u32[]{:S(2)}, u32[]{:S(2)}) async-start(bf16[4,12,128,128]{3,2,1,0:T(8,128)(2,1)} %collective-permute-done), calls=%async_computation.2 | async-start | bytes 3145728 | tf_op jit(solution)/shard_map/all_to_all | solution.py:203
  66.2 27.9 %copy-start.2 = (s32[8]{0:T(128)S(1)}, s32[8]{0:T(128)}, u32[]{:S(2)}) copy-start(s32[8]{0:T(128)} %constant.75.clone.1.source_ref) | copy-start | bytes 100
  69.7 14.6 %collective-permute-start.3 = (bf16[1,12,128,128]{3,2,1,0:T(8,128)(2,1)}, bf16[1,12,128,128]{3,2,1,0:T(8,128)(2,1)S(1)}, u32[]{:S(2)}, u32[]{:S(2)}) collective-permute-start(bf16[1,12,128,128]{3,2,1,0:T(8,128)(2,1)} %get-tuple-element.16), channel_id=1, source_target_pairs={{0,13},{1,12},{2,15},{3,14},{4,5},{5,4},{6,7},{7,6},{8,9},{9,8},{1... | collective-permute-start | bytes 1179656 | tf_op jit(solution)/shard_map/ppermute | solution.py:212
  72.7 21.4 %collective-permute-start.4 = (bf16[1,12,128,128]{3,2,1,0:T(8,128)(2,1)}, bf16[1,12,128,128]{3,2,1,0:T(8,128)(2,1)S(1)}, u32[]{:S(2)}, u32[]{:S(2)}) collective-permute-start(bf16[1,12,128,128]{3,2,1,0:T(8,128)(2,1)} %get-tuple-element.17), channel_id=1, source_target_pairs={{0,14},{1,15},{2,12},{3,13},{4,6},{5,7},{6,4},{7,5},{8,10},{9,11},... | collective-permute-start | bytes 1179656 | tf_op jit(solution)/shard_map/ppermute | solution.py:212
  76.9 30.1 %collective-permute-start.5 = (bf16[1,12,128,128]{3,2,1,0:T(8,128)(2,1)}, bf16[1,12,128,128]{3,2,1,0:T(8,128)(2,1)S(1)}, u32[]{:S(2)}, u32[]{:S(2)}) collective-permute-start(bf16[1,12,128,128]{3,2,1,0:T(8,128)(2,1)} %get-tuple-element.18), channel_id=1, source_target_pairs={{0,15},{1,14},{2,13},{3,12},{4,7},{5,6},{6,5},{7,4},{8,11},{9,10},... | collective-permute-start | bytes 1179656 | tf_op jit(solution)/shard_map/ppermute | solution.py:212
  78.4 30.2 %collective-permute-start.6 = (bf16[1,12,128,128]{3,2,1,0:T(8,128)(2,1)}, bf16[1,12,128,128]{3,2,1,0:T(8,128)(2,1)}, u32[]{:S(2)}, u32[]{:S(2)}) collective-permute-start(bf16[1,12,128,128]{3,2,1,0:T(8,128)(2,1)} %get-tuple-element.19), channel_id=1, source_target_pairs={{0,8},{1,9},{2,10},{3,11},{4,0},{5,1},{6,2},{7,3},{8,12},{9,13},{1... | collective-permute-start | bytes 1179656 | tf_op jit(solution)/shard_map/ppermute | solution.py:213
  84.2 32.8 %collective-permute-start.7 = (bf16[1,12,128,128]{3,2,1,0:T(8,128)(2,1)}, bf16[1,12,128,128]{3,2,1,0:T(8,128)(2,1)}, u32[]{:S(2)}, u32[]{:S(2)}) collective-permute-start(bf16[1,12,128,128]{3,2,1,0:T(8,128)(2,1)} %get-tuple-element.20), channel_id=1, source_target_pairs={{0,9},{1,8},{2,11},{3,10},{4,1},{5,0},{6,3},{7,2},{8,13},{9,12},{1... | collective-permute-start | bytes 1179656 | tf_op jit(solution)/shard_map/ppermute | solution.py:213
  84.3 43.1 %collective-permute-start.8 = (bf16[1,12,128,128]{3,2,1,0:T(8,128)(2,1)}, bf16[1,12,128,128]{3,2,1,0:T(8,128)(2,1)}, u32[]{:S(2)}, u32[]{:S(2)}) collective-permute-start(bf16[1,12,128,128]{3,2,1,0:T(8,128)(2,1)} %get-tuple-element.21), channel_id=1, source_target_pairs={{0,10},{1,11},{2,8},{3,9},{4,2},{5,3},{6,0},{7,1},{8,14},{9,15},{1... | collective-permute-start | bytes 1179656 | tf_op jit(solution)/shard_map/ppermute | solution.py:213
  94.1 41.7 %collective-permute-start.9 = (bf16[1,12,128,128]{3,2,1,0:T(8,128)(2,1)}, bf16[1,12,128,128]{3,2,1,0:T(8,128)(2,1)}, u32[]{:S(2)}, u32[]{:S(2)}) collective-permute-start(bf16[1,12,128,128]{3,2,1,0:T(8,128)(2,1)} %get-tuple-element.22), channel_id=1, source_target_pairs={{0,11},{1,10},{2,9},{3,8},{4,3},{5,2},{6,1},{7,0},{8,15},{9,14},{1... | collective-permute-start | bytes 1179656 | tf_op jit(solution)/shard_map/ppermute | solution.py:213
  94.2 1.7 %copy-start.1 = (bf16[6,12,128,128]{3,2,1,0:T(8,128)(2,1)S(1)}, bf16[6,12,128,128]{3,2,1,0:T(8,128)(2,1)}, u32[]{:S(2)}) copy-start(bf16[6,12,128,128]{3,2,1,0:T(8,128)(2,1)} %tiles_ref.7) | copy-start | bytes 7077892
